TPU v7x, 256 devices: a whole 4x4x8 slice. The times are simulated.
256 devices in a mesh: section: 16 (over y_hi, z), head: 4 (over y_lo, core), page: 4 (over x).
Axes of the slice: x: 4, y: 4 (y_hi: 2, y_lo: 2; y = y_hi * 2 + y_lo), z: 8, core: 2. Of those that a mesh axis runs over, the one named last changes fastest.
Arguments:
- grad_in: float32 [16, 64, 3072], P('section', None, 'page'), may hold values from -6 to 6
- grad_fresh: float32 [64, 3072], P(None, 'page'), may hold values from -6 to 6
- queries: float32 [16, 2, 64, 3072], P('section', None, None, 'head'), may hold values from -320 to 320
- key_cache: float32 [16, 2048, 1024], P('section', 'page', 'head'), may hold values from -6 to 6
- value_cache: float32 [16, 2048, 1024], P('section', 'page', 'head'), may hold values from -6 to 6
- key_fresh: float32 [2048, 1024], P('page', 'head'), may hold values from -6 to 6
- value_fresh: float32 [2048, 1024], P('page', 'head'), may hold values from -6 to 6
- key_grad_in: float32 [16, 2048, 1024], P('section', 'page', 'head'), may hold values from -4 to 4
- value_grad_in: float32 [16, 2048, 1024], P('section', 'page', 'head'), may hold values from -4 to 4
- page_table: int32 [16, 16], P('section'), may hold values from 0 to 15, as said below
- offsets: int32 [16], P('section'), may hold values from 0 to 1984
- page_fresh: int32 [16], replicated, may hold values from 0 to 15, as said below
- offset_fresh: int32 [1], replicated, may hold values from 0 to 1984
- w_query: float32 [16, 3072, 3072], P('section', 'page', 'head'), may hold values from -0.109375 to 0.109375
- w_out: float32 [16, 3072, 3072], P('section', 'head', 'page'), may hold values from -0.109375 to 0.109375
Outputs:
- grad_next: float32 [16, 64, 3072], P('section', None, 'page')
- key_grad_next: float32 [16, 2048, 1024], P('section', 'page', 'head')
- value_grad_next: float32 [16, 2048, 1024], P('section', 'page', 'head')
Inputs may be any that keep to these rules, and one draw needn't show every extreme that they name: `page_table`: each row is a permutation of 0 to 15: entry b is the logical block held in physical rows b * 128 to (b + 1) * 128 - 1. `page_fresh`: A permutation of 0 to 15, read as page_table's rows.
All inputs are finite; a program needn't handle non-finite values.
Results may differ from a plain program's by a relative error of at most 0.0003.
Values sent between devices are 32-bit elements; how exact they have to be, the bound alone decides.
No kernel may reach another device: no remote copies, remote signals or barrier semaphores. Data moves between devices by JAX's collectives and lax.ppermute only.
A program may use at most 64 MiB of HBM per device.

v0:
```python
import jax
import jax.numpy as jnp
from jax import lax
from jax.sharding import PartitionSpec as P

HD = 128
BLOCK = 128


precise = lax.Precision.HIGHEST


def merged(value, axis, join):
    pieces = jax.tree.map(lambda part: lax.all_gather(part, axis), value)
    head = jax.tree.map(lambda part: part[0], pieces)
    tail = jax.tree.map(lambda part: part[1:], pieces)
    so_far, _ = lax.scan(lambda so_far, piece: (join(so_far, piece), None), head, tail)
    return so_far


def shifted(value, axis, steps):
    count = lax.axis_size(axis)
    first, last = (max(0, -steps), min(count, count - steps))
    return lax.ppermute(value, axis, [(source, source + steps) for source in range(first, last)])


def combine_parts(left_part, right_part):
    left_top, left_total, left_weighted, left_dout = left_part
    right_top, right_total, right_weighted, right_dout = right_part
    joint_top = jnp.maximum(left_top, right_top)
    left_scale = jnp.exp(left_top - joint_top)
    right_scale = jnp.exp(right_top - joint_top)
    joint_total = left_total * left_scale + right_total * right_scale
    query_count, heads_here = joint_top.shape
    joint_weighted = (
        left_weighted.reshape(query_count, heads_here, -1) * left_scale[..., None]
        + right_weighted.reshape(query_count, heads_here, -1) * right_scale[..., None]
    ).reshape(left_weighted.shape)
    return (joint_top, joint_total, joint_weighted, left_dout + right_dout)


def layer_backward(
    incoming,
    saved_query,
    key_block,
    value_block,
    table_row,
    offset_now,
    w_query_layer,
    w_out_layer,
    key_sum,
    value_sum,
):
    query_count = saved_query.shape[0]
    key_count = key_block.shape[0]
    shared = key_block.shape[1] // HD
    heads_here = saved_query.shape[1] // HD
    group_size = heads_here // shared
    score_scale = HD ** (-0.5)
    dout_part = jnp.einsum("qc,hc->qh", incoming, w_out_layer, precision=precise)
    block_count = key_count // BLOCK
    local_table = lax.dynamic_slice_in_dim(
        table_row, lax.axis_index("page") * block_count, block_count
    )
    positions = jnp.repeat(local_table, BLOCK) * BLOCK + jnp.tile(
        jnp.arange(BLOCK, dtype=jnp.int32), block_count
    )
    visible = positions[None, :] <= offset_now + jnp.arange(query_count, dtype=jnp.int32)[:, None]
    query_heads = saved_query.reshape(query_count, shared, group_size, HD)
    key_heads = key_block.reshape(key_count, shared, HD)
    value_heads = value_block.reshape(key_count, shared, HD)
    scores = jnp.einsum("qgrd,kgd->grqk", query_heads, key_heads, precision=precise) * score_scale
    masked = jnp.where(visible, scores, -1e30)
    local_top = jnp.max(masked, axis=-1)
    stat_top = local_top.transpose(2, 0, 1).reshape(query_count, heads_here)
    weights_raw = jnp.where(visible, jnp.exp(masked - local_top[..., None]), 0.0)
    local_total = jnp.sum(weights_raw, axis=-1)
    local_weighted = jnp.einsum(
        "grqk,kgd->qgrd", weights_raw, value_heads, precision=precise
    ).reshape(query_count, heads_here * HD)
    stat_total = local_total.transpose(2, 0, 1).reshape(query_count, heads_here)
    row_top, row_total, weighted, d_out = merged(
        (stat_top, stat_total, local_weighted, dout_part), "page", combine_parts
    )
    top_back = row_top.reshape(query_count, shared, group_size).transpose(1, 2, 0)[..., None]
    total_back = row_total.reshape(query_count, shared, group_size).transpose(1, 2, 0)[..., None]
    probs = jnp.where(visible, jnp.exp(masked - top_back), 0.0) / total_back
    attended = (weighted.reshape(query_count, heads_here, HD) / row_total[..., None]).reshape(
        query_count, shared, group_size, HD
    )
    dout_heads = d_out.reshape(query_count, shared, group_size, HD)
    delta = jnp.sum(dout_heads * attended, axis=-1).transpose(1, 2, 0)[..., None]
    d_prob = jnp.einsum("qgrd,kgd->grqk", dout_heads, value_heads, precision=precise)
    d_score = probs * (d_prob - delta)
    query_part = (
        jnp.einsum("grqk,kgd->qgrd", d_score, key_heads, precision=precise).reshape(
            query_count, heads_here * HD
        )
        * score_scale
    )
    key_step = (
        jnp.einsum("grqk,qgrd->kgd", d_score, query_heads, precision=precise).reshape(
            key_count, shared * HD
        )
        * score_scale
    )
    value_step = jnp.einsum("grqk,qgrd->kgd", probs, dout_heads, precision=precise).reshape(
        key_count, shared * HD
    )
    d_query = lax.psum(query_part, "page")
    input_part = jnp.einsum("qh,ch->qc", d_query, w_query_layer, precision=precise)
    return (input_part, key_sum + key_step, value_sum + value_step)


def full_input(incoming, input_part):
    return incoming + lax.psum(input_part, "head")


def per_device(
    grad_in,
    grad_fresh,
    queries,
    key_cache,
    value_cache,
    key_fresh,
    value_fresh,
    key_grad_in,
    value_grad_in,
    page_table,
    offsets,
    page_fresh,
    offset_fresh,
    w_query,
    w_out,
):
    is_final = lax.axis_index("section") == lax.axis_size("section") - 1
    w_query_layer = w_query[0]
    w_out_layer = w_out[0]
    input_part, key_sum, value_sum = layer_backward(
        grad_in[0],
        queries[0, 0],
        key_cache[0],
        value_cache[0],
        page_table[0],
        offsets[0],
        w_query_layer,
        w_out_layer,
        key_grad_in[0],
        value_grad_in[0],
    )
    outgoing = full_input(grad_in[0], input_part)
    received, key_start, value_start, next_keys, next_values, next_table, next_offsets = shifted(
        (outgoing, key_sum, value_sum, key_cache[0], value_cache[0], page_table[0], offsets),
        "section",
        -1,
    )
    incoming = jnp.where(is_final, grad_fresh, received)
    key_start = jnp.where(is_final, jnp.zeros_like(key_start), key_start)
    value_start = jnp.where(is_final, jnp.zeros_like(value_start), value_start)
    next_keys = jnp.where(is_final, key_fresh, next_keys)
    next_values = jnp.where(is_final, value_fresh, next_values)
    next_table = jnp.where(is_final, page_fresh, next_table)
    offset_next = jnp.where(is_final, offset_fresh[0], next_offsets[0])
    final_part, key_final, value_final = layer_backward(
        incoming,
        queries[0, 1],
        next_keys,
        next_values,
        next_table,
        offset_next,
        w_query_layer,
        w_out_layer,
        key_start,
        value_start,
    )
    grad_done = full_input(incoming, final_part)
    return (grad_done[None], key_final[None], value_final[None])


def solution(mesh):
    placed = (
        P("section", None, "page"),
        P(None, "page"),
        P("section", None, None, "head"),
        P("section", "page", "head"),
        P("section", "page", "head"),
        P("page", "head"),
        P("page", "head"),
        P("section", "page", "head"),
        P("section", "page", "head"),
        P("section", None),
        P("section"),
        P(),
        P(),
        P("section", "page", "head"),
        P("section", "head", "page"),
    )
    return jax.shard_map(
        per_device,
        mesh=mesh,
        in_specs=placed,
        out_specs=(
            P("section", None, "page"),
            P("section", "page", "head"),
            P("section", "page", "head"),
        ),
        check_vma=False,
    )
```

profile of v0, /device:TPU:24, one launch (start us, length us, event | category | flops | bytes accessed | tf_op | source)
XLA Modules:
  0.0 421.6 jit_solution(8215147296763703528)
XLA Ops:
  7.2 8.7 %collective-permute-start.3 = (s32[1]{0:T(128)}, s32[1]{0:T(128)}, u32[]{:S(2)}, u32[]{:S(2)}) collective-permute-start(s32[1]{0:T(128)} %param.29), channel_id=1, source_target_pairs={{16,0},{32,16},{48,32},{64,48},{80,64},{96,80},{112,96},{128,112},... | collective-permute-start | bytes 20 | tf_op jit(solution)/shard_map/ppermute | solution.py:24
  19.3 2.2 reshape_squeeze.12
  28.6 13.7 %all_gather.32 = f32[4,64,768]{2,1,0:T(8,128)S(1)} all-gather(f32[1,64,768]{2,1,0:T(8,128)S(1)} %all_gather_reshape.20), channel_id=1, replica_groups=mesh['section'=16,'head'=4,'page'=4] {'page'}, dimensions={0}, use_global_device_ids=true | all-gather | bytes 983040 | tf_op jit(solution)/shard_map/all_gather | solution.py:14
  43.5 12.1 %all_gather.31 = f32[4,64,6]{1,2,0:T(8,128)S(1)} all-gather(f32[1,64,6]{1,2,0:T(8,128)S(1)} %all_gather_reshape.19), channel_id=1, replica_groups=mesh['section'=16,'head'=4,'page'=4] {'page'}, dimensions={0}, use_global_device_ids=true | all-gather | bytes 7680 | tf_op jit(solution)/shard_map/all_gather | solution.py:14
  56.8 12.1 %all_gather.30 = f32[4,64,6]{1,2,0:T(8,128)S(1)} all-gather(f32[1,64,6]{1,2,0:T(8,128)} %all_gather_reshape.18), channel_id=1, replica_groups=mesh['section'=16,'head'=4,'page'=4] {'page'}, dimensions={0}, use_global_device_ids=true | all-gather | bytes 7680 | tf_op jit(solution)/shard_map/all_gather | solution.py:14
  70.1 2.4 fusion.12
  72.5 13.3 %all-gather = f32[256,768]{1,0:T(8,128)S(1)} all-gather(f32[64,768]{1,0:T(8,128)S(1)} %fusion.12), channel_id=2, replica_groups=mesh['section'=16,'head'=4,'page'=4] {'page'}, dimensions={0}, use_global_device_ids=true | all-gather | bytes 983040 | tf_op jit(solution)/shard_map/all_gather | solution.py:14
  88.8 15.2 %while.32 = (s32[]{:T(128)}, f32[64,6]{1,0:T(8,128)}, f32[64,6]{1,0:T(8,128)}, f32[64,768]{1,0:T(8,128)S(1)}, f32[64,768]{1,0:T(8,128)S(1)}, /*index=5*/f32[3,64...) while((s32[]{:T(128)}, f32[64,6]{1,0:T(8,128)}, ...), condition=%wide.region_3.4_spmd, body=%wide.region_2.3_spmd.sunk | while | flops 198914 | bytes 1993841 | solution.py:17
  106.4 2.7 fusion.45
  109.2 2.1 copy.115
  111.2 2.1 bitcast_add_fusion.2
  113.3 2.9 collective-permute-start.6
  118.7 2.1 fusion.18
  122.7 2.9 collective-permute-start.2
  125.6 2.9 collective-permute-start.1
  136.1 2.2 collective-permute-start.5
  139.1 27.2 %all-reduce.5.cloned.1.call-done = f32[64,768]{1,0:T(8,128)} async-done(((f32[64,768]{1,0:T(8,128)}), f32[64,768]{1,0:T(8,128)}) %all-reduce.5.cloned.1.call-update) | async-done | bytes 196624 | tf_op jit(solution)/shard_map/psum | solution.py:110
  166.2 4.8 %fusion.8 = f32[64,768]{1,0:T(8,128)} fusion(f32[64,768]{1,0:T(8,128)} %all-reduce.5.cloned.1.call-done, f32[1,768,768]{2,1,0:T(8,128)} %param.32), kind=kOutput, calls=%fused_computation.26 | convolution fusion | flops 452984832 | bytes 2752512 | tf_op jit(solution)/shard_map/qh,ch->qc/dot_general | solution.py:111
  171.2 40.9 %all-reduce.7.cloned.1.call-done = f32[64,768]{1,0:T(8,128)} async-done(((f32[64,768]{1,0:T(8,128)}), f32[64,768]{1,0:T(8,128)}) %all-reduce.7.cloned.1.call-update) | async-done | bytes 196624 | tf_op jit(solution)/shard_map/psum | solution.py:116
  213.8 5.8 %collective-permute-start = (f32[64,768]{1,0:T(8,128)}, f32[64,768]{1,0:T(8,128)}, u32[]{:S(2)}, u32[]{:S(2)}) collective-permute-start(f32[64,768]{1,0:T(8,128)} %bitcast_add_fusion.4), channel_id=1, source_target_pairs={{16,0},{32,16},{48,32},{64,48},{80,64},{96,80},{112,96},{128,112},... | collective-permute-start | bytes 589832 | tf_op jit(solution)/shard_map/ppermute | solution.py:24
  219.6 2.1 broadcast_select_fusion
  225.1 12.2 %all_gather.36 = f32[4,64,6]{1,2,0:T(8,128)S(1)} all-gather(f32[1,64,6]{1,2,0:T(8,128)S(1)} %all_gather_reshape.22), channel_id=1, replica_groups=mesh['section'=16,'head'=4,'page'=4] {'page'}, dimensions={0}, use_global_device_ids=true | all-gather | bytes 7680 | tf_op jit(solution)/shard_map/all_gather | solution.py:14
  237.3 11.9 %all_gather.35 = f32[4,64,6]{1,2,0:T(8,128)S(1)} all-gather(f32[1,64,6]{1,2,0:T(8,128)S(1)} %all_gather_reshape.21), channel_id=1, replica_groups=mesh['section'=16,'head'=4,'page'=4] {'page'}, dimensions={0}, use_global_device_ids=true | all-gather | bytes 7680 | tf_op jit(solution)/shard_map/all_gather | solution.py:14
  249.9 2.1 reshape.140
  254.9 13.6 %all_gather.37 = f32[4,64,768]{2,1,0:T(8,128)S(1)} all-gather(f32[1,64,768]{2,1,0:T(8,128)} %all_gather_reshape.23), channel_id=1, replica_groups=mesh['section'=16,'head'=4,'page'=4] {'page'}, dimensions={0}, use_global_device_ids=true | all-gather | bytes 983040 | tf_op jit(solution)/shard_map/all_gather | solution.py:14
  272.7 3.3 fusion.10
  276.0 13.5 %all-gather.1 = f32[256,768]{1,0:T(8,128)S(1)} all-gather(f32[64,768]{1,0:T(8,128)S(1)} %fusion.10), channel_id=3, replica_groups=mesh['section'=16,'head'=4,'page'=4] {'page'}, dimensions={0}, use_global_device_ids=true | all-gather | bytes 983040 | tf_op jit(solution)/shard_map/all_gather | solution.py:14
  290.4 15.2 %while.33 = (s32[]{:T(128)}, f32[64,6]{1,0:T(8,128)}, f32[64,6]{1,0:T(8,128)}, f32[64,768]{1,0:T(8,128)S(1)}, f32[64,768]{1,0:T(8,128)S(1)}, /*index=5*/f32[3,64...) while((s32[]{:T(128)}, f32[64,6]{1,0:T(8,128)}, ...), condition=%wide.region_10.11_spmd, body=%wide.region_9.10_spmd.sunk | while | flops 198914 | bytes 1993841 | solution.py:17
  308.3 2.7 fusion.46
  325.1 42.3 %all-reduce.9.cloned.1.call-done = f32[64,768]{1,0:T(8,128)} async-done(((f32[64,768]{1,0:T(8,128)}), f32[64,768]{1,0:T(8,128)}) %all-reduce.9.cloned.1.call-update) | async-done | bytes 196624 | tf_op jit(solution)/shard_map/psum | solution.py:110
  367.4 4.8 %fusion.6 = f32[64,768]{1,0:T(8,128)} fusion(f32[64,768]{1,0:T(8,128)} %all-reduce.9.cloned.1.call-done, f32[1,768,768]{2,1,0:T(8,128)} %param.32), kind=kOutput, calls=%fused_computation.24 | convolution fusion | flops 452984832 | bytes 2752512 | tf_op jit(solution)/shard_map/qh,ch->qc/dot_general | solution.py:111
  374.2 39.2 %all-reduce.11.cloned.1.call-done = f32[64,768]{1,0:T(8,128)} async-done(((f32[64,768]{1,0:T(8,128)}), f32[64,768]{1,0:T(8,128)}) %all-reduce.11.cloned.1.call-update) | async-done | bytes 196624 | tf_op jit(solution)/shard_map/psum | solution.py:116
  (202 shorter events, 94.2 us)
Async XLA Ops:
  7.2 62.9 %copy-start = (f32[1,768,768]{2,1,0:T(8,128)S(1)}, f32[1,768,768]{2,1,0:T(8,128)}, u32[]{:S(2)}) copy-start(f32[1,768,768]{2,1,0:T(8,128)} %param.33) | copy-start | bytes 7077892
  7.2 14.3 %copy-start.22 = (f32[1,512,256]{2,1,0:T(8,128)S(1)}, f32[1,512,256]{2,1,0:T(8,128)}, u32[]{:S(2)}) copy-start(f32[1,512,256]{2,1,0:T(8,128)} %param.23) | copy-start | bytes 1572868
  7.2 159.0 %all-reduce.5.cloned.1.call-start = ((), (), s32[]{:S(2)}) async-start(), calls=%async_computation | async-start | bytes 393216 | tf_op jit(solution)/shard_map/psum | solution.py:110
  7.2 128.8 %collective-permute-start.3 = (s32[1]{0:T(128)}, s32[1]{0:T(128)}, u32[]{:S(2)}, u32[]{:S(2)}) collective-permute-start(s32[1]{0:T(128)} %param.29), channel_id=1, source_target_pairs={{16,0},{32,16},{48,32},{64,48},{80,64},{96,80},{112,96},{128,112},... | collective-permute-start | bytes 20 | tf_op jit(solution)/shard_map/ppermute | solution.py:24
  19.3 7.4 %copy-start.10 = (f32[64,2,3,128]{3,2,1,0:T(4,128)}, f32[64,2,3,128]{3,2,1,0:T(4,128)S(1)}, u32[]{:S(2)}) copy-start(f32[64,2,3,128]{3,2,1,0:T(4,128)S(1)} %reshape_squeeze.13) | copy-start | bytes 589828
  22.6 4.0 copy-start.19
  27.5 42.6 %copy-start.15 = (f32[1,64,768]{2,1,0:T(8,128)S(1)}, f32[1,64,768]{2,1,0:T(8,128)}, u32[]{:S(2)}) copy-start(f32[1,64,768]{2,1,0:T(8,128)} %param.19) | copy-start | bytes 589828
  28.6 14.6 %copy-start.20 = (pred[64,512]{1,0:T(8,128)(4,1)S(1)}, pred[64,512]{1,0:T(8,128)(4,1)}, u32[]{:S(2)}) copy-start(pred[64,512]{1,0:T(8,128)(4,1)} %copy-done.19) | copy-start | bytes 98308
  70.1 16.6 %copy-start.24 = (f32[64,6]{0,1:T(8,128)S(1)}, f32[64,6]{0,1:T(8,128)}, u32[]{:S(2)}) copy-start(f32[64,6]{0,1:T(8,128)} %slice_bitcast_fusion.4) | copy-start | bytes 4612
  109.2 9.5 %copy-start.21 = (pred[64,512]{1,0:T(8,128)(4,1)S(1)}, pred[64,512]{1,0:T(8,128)(4,1)}, u32[]{:S(2)}) copy-start(pred[64,512]{1,0:T(8,128)(4,1)} %copy-done.19) | copy-start | bytes 98308
  113.3 209.8 %collective-permute-start.6 = (f32[512,256]{1,0:T(8,128)}, f32[512,256]{1,0:T(8,128)}, u32[]{:S(2)}, u32[]{:S(2)}) collective-permute-start(f32[512,256]{1,0:T(8,128)} %bitcast_add_fusion.2), channel_id=1, source_target_pairs={{16,0},{32,16},{48,32},{64,48},{80,64},{96,80},{112,96},{128,112},... | collective-permute-start | bytes 1572872 | tf_op jit(solution)/shard_map/ppermute | solution.py:24
  118.7 4.0 copy-start.26
  118.7 11.8 %copy-start.11 = (f32[64,2,3,128]{3,2,1,0:T(4,128)S(1)}, f32[64,2,3,128]{3,2,1,0:T(4,128)}, u32[]{:S(2)}) copy-start(f32[64,2,3,128]{3,2,1,0:T(4,128)} %copy-done.10) | copy-start | bytes 589828
  120.8 12.3 %copy-start.14 = (f32[1,1,64,768]{3,2,1,0:T(8,128)S(1)}, f32[1,1,64,768]{3,2,1,0:T(8,128)}, u32[]{:S(2)}) copy-start(f32[1,1,64,768]{3,2,1,0:T(8,128)} %get-tuple-element.196) | copy-start | bytes 589828
  122.6 16.3 %copy-start.25 = (s32[16]{0:T(128)S(1)}, s32[16]{0:T(128)}, u32[]{:S(2)}) copy-start(s32[16]{0:T(128)} %param.30) | copy-start | bytes 196
  122.6 89.5 %all-reduce.7.cloned.1.call-start = ((), (), s32[]{:S(2)}) async-start(), calls=%async_computation.1 | async-start | bytes 393216 | tf_op jit(solution)/shard_map/psum | solution.py:116
  122.7 16.2 %collective-permute-start.2 = (s32[16]{0:T(128)S(1)}, s32[16]{0:T(128)S(1)}, u32[]{:S(2)}, u32[]{:S(2)}) collective-permute-start(s32[16]{0:T(128)S(1)} %bitcast.260), channel_id=1, source_target_pairs={{16,0},{32,16},{48,32},{64,48},{80,64},{96,80},{112,96},{128,112},... | collective-permute-start | bytes 200 | tf_op jit(solution)/shard_map/ppermute | solution.py:24
  125.6 94.0 %collective-permute-start.1 = (f32[512,256]{1,0:T(8,128)}, f32[512,256]{1,0:T(8,128)}, u32[]{:S(2)}, u32[]{:S(2)}) collective-permute-start(f32[512,256]{1,0:T(8,128)} %bitcast.242), channel_id=1, source_target_pairs={{16,0},{32,16},{48,32},{64,48},{80,64},{96,80},{112,96},{128,112},... | collective-permute-start | bytes 1572872 | tf_op jit(solution)/shard_map/ppermute | solution.py:24
  128.5 91.1 %collective-permute-start.4 = (f32[512,256]{1,0:T(8,128)}, f32[512,256]{1,0:T(8,128)}, u32[]{:S(2)}, u32[]{:S(2)}) collective-permute-start(f32[512,256]{1,0:T(8,128)} %bitcast.243), channel_id=1, source_target_pairs={{16,0},{32,16},{48,32},{64,48},{80,64},{96,80},{112,96},{128,112},... | collective-permute-start | bytes 1572872 | tf_op jit(solution)/shard_map/ppermute | solution.py:24
  134.1 78.0 %copy-start.16 = (f32[1,64,768]{2,1,0:T(8,128)S(1)}, f32[1,64,768]{2,1,0:T(8,128)}, u32[]{:S(2)}) copy-start(f32[1,64,768]{2,1,0:T(8,128)} %param.19) | copy-start | bytes 589828
  136.1 236.2 %collective-permute-start.5 = (f32[512,256]{1,0:T(8,128)}, f32[512,256]{1,0:T(8,128)}, u32[]{:S(2)}, u32[]{:S(2)}) collective-permute-start(f32[512,256]{1,0:T(8,128)} %bitcast_add_fusion.3), channel_id=1, source_target_pairs={{16,0},{32,16},{48,32},{64,48},{80,64},{96,80},{112,96},{128,112},... | collective-permute-start | bytes 1572872 | tf_op jit(solution)/shard_map/ppermute | solution.py:24
  171.0 196.4 %all-reduce.9.cloned.1.call-start = ((), (), s32[]{:S(2)}) async-start(), calls=%async_computation.2 | async-start | bytes 393216 | tf_op jit(solution)/shard_map/psum | solution.py:110
  171.2 80.8 %copy-start.17 = (pred[64,512]{1,0:T(8,128)(4,1)}, pred[64,512]{1,0:T(8,128)(4,1)S(1)}, u32[]{:S(2)}) copy-start(pred[64,512]{1,0:T(8,128)(4,1)S(1)} %broadcast_compare_fusion) | copy-start | bytes 98308
  171.2 51.7 %copy-start.8 = (f32[64,2,3,128]{3,2,1,0:T(4,128)S(1)}, f32[64,2,3,128]{3,2,1,0:T(4,128)}, u32[]{:S(2)}) copy-start(f32[64,2,3,128]{3,2,1,0:T(4,128)} %reshape_squeeze.15) | copy-start | bytes 589828
  213.8 58.9 %collective-permute-start = (f32[64,768]{1,0:T(8,128)}, f32[64,768]{1,0:T(8,128)}, u32[]{:S(2)}, u32[]{:S(2)}) collective-permute-start(f32[64,768]{1,0:T(8,128)} %bitcast_add_fusion.4), channel_id=1, source_target_pairs={{16,0},{32,16},{48,32},{64,48},{80,64},{96,80},{112,96},{128,112},... | collective-permute-start | bytes 589832 | tf_op jit(solution)/shard_map/ppermute | solution.py:24
  237.3 14.6 %copy-start.23 = (f32[4,64,6]{1,2,0:T(8,128)}, f32[4,64,6]{1,2,0:T(8,128)S(1)}, u32[]{:S(2)}) copy-start(f32[4,64,6]{1,2,0:T(8,128)S(1)} %all_gather.36) | copy-start | bytes 18436
  254.9 17.8 %copy-start.12 = (f32[64,768]{1,0:T(8,128)S(1)}, f32[64,768]{1,0:T(8,128)}, u32[]{:S(2)}) copy-start(f32[64,768]{1,0:T(8,128)} %param.20) | copy-start | bytes 589828
  272.7 17.8 %slice-start = ((f32[4,64,6]{1,2,0:T(8,128)}), f32[3,64,6]{1,2,0:T(8,128)S(1)}, s32[]{:S(2)}) async-start(f32[4,64,6]{1,2,0:T(8,128)} %copy-done.23), calls=%async_computation.4 | async-start | bytes 24576 | tf_op jit(solution)/shard_map/slice | solution.py:16
  308.3 7.1 %copy-start.18 = (pred[64,512]{1,0:T(8,128)(4,1)S(1)}, pred[64,512]{1,0:T(8,128)(4,1)}, u32[]{:S(2)}) copy-start(pred[64,512]{1,0:T(8,128)(4,1)} %copy-done.17) | copy-start | bytes 98308
  323.0 49.2 %copy-start.6 = (f32[512,256]{1,0:T(8,128)S(1)}, f32[512,256]{1,0:T(8,128)}, u32[]{:S(2)}) copy-start(f32[512,256]{1,0:T(8,128)} %copy.113) | copy-start | bytes 1572868
  323.1 90.3 %all-reduce.11.cloned.1.call-start = ((), (), s32[]{:S(2)}) async-start(), calls=%async_computation.3 | async-start | bytes 393216 | tf_op jit(solution)/shard_map/psum | solution.py:116
  325.1 88.3 %copy-start.13 = (f32[64,768]{1,0:T(8,128)S(1)}, f32[64,768]{1,0:T(8,128)}, u32[]{:S(2)}) copy-start(f32[64,768]{1,0:T(8,128)} %param.20) | copy-start | bytes 589828
  (7 other events, 12.6 us)
Sparse Core Ops, SparseCore 0:
  122.8 43.3 all-reduce.4
  171.1 40.9 all-reduce.6
  323.2 44.2 all-reduce.8
  372.4 40.9 all-reduce.10
where the time goes:
time: 426 us; the launch traced here: 422 us
  waiting for transfers between devices  150 us (35%)
  blocking collectives  103 us (24%)
  local copies, waits for them, and re-layouts  53.1 us (12%)
  matrix products  38.3 us (9%)
  other arithmetic  34 us (8%)
  starting transfers between devices  27.6 us (6%)
  between operations  16.2 us (4%)
    all_gather x8, blocking collectives, merged(): pieces = jax.tree.map(lambda part: lax.all_gather(part, axis), value)  103 us
    psum x2, waiting for transfers between devices, full_input(): return incoming + lax.psum(input_part, 'head')  80.1 us
    psum x2, waiting for transfers between devices, layer_backward(): d_query = lax.psum(query_part, 'page')  69.5 us
    ppermute x7, starting transfers between devices, shifted(): lax.ppermute(value, axis, [(source, source + steps) for source in range(f...  27.4 us
    dynamic_slice x24, local copies, waits for them, and re-layouts, merged(): lax.scan(lambda so_far, piece: (join(so_far, piece), None), head, tail)  12.7 us
    dot_general x2, matrix products, layer_backward(): jnp.einsum('qh,ch->qc', d_query, w_query_layer, precision=precise)  9.59 us
    add x6, other arithmetic, combine_parts(): joint_total = left_total * left_scale + right_total * right_scale  8.65 us
  transfers between devices with their start and end apart: 11, of which 4 were waited for; matrix products, arithmetic and copies ran while one was open for 29% of the time, Pallas kernels for 0%

commit v1 on v0

v1 whole, which is shorter than its diff:
```python
import functools

import jax
import jax.numpy as jnp
from jax import lax
from jax.experimental import pallas as pl
from jax.experimental.pallas import tpu as pltpu
from jax.sharding import PartitionSpec as P

HD = 128
BLOCK = 128
Q = 64
HALF = Q // 2
KEYS = 512
KV = 2
GROUP = 3
ROWS = GROUP * Q
WIDE = KV * GROUP * HD
SCALE = HD ** (-0.5)
F32 = jnp.float32
BF16 = jnp.bfloat16
NN = (((1,), (0,)), ((), ()))
NT = (((1,), (1,)), ((), ()))


def split(x):
    high = x.astype(BF16)
    return high, (x - high.astype(F32)).astype(BF16)


def dot(a, b, dims):
    return lax.dot_general(a, b, dims, preferred_element_type=F32)


def dot3(a, b, dims):
    (a_high, a_low), (b_high, b_low) = a, b
    return dot(a_high, b_high, dims) + (dot(a_low, b_high, dims) + dot(a_high, b_low, dims))


def stacked(x, g):
    return jnp.concatenate([x[:, (g * GROUP + r) * HD : (g * GROUP + r + 1) * HD] for r in range(GROUP)], 0)


def spread(groups):
    return jnp.concatenate([groups[g][r * Q : (r + 1) * Q] for g in range(KV) for r in range(GROUP)], 1)


def as_columns(row):
    return jnp.transpose(jnp.broadcast_to(row, (HD, ROWS)))


def call(body, outs, *args, scratch=(), mb=24, smem=()):
    in_specs = [
        pl.BlockSpec(memory_space=pltpu.SMEM if i in smem else pltpu.VMEM) for i in range(len(args))
    ]
    return pl.pallas_call(
        body,
        out_shape=[jax.ShapeDtypeStruct(s, d) for s, d in outs],
        in_specs=in_specs,
        out_specs=[pl.BlockSpec(memory_space=pltpu.VMEM)] * len(outs),
        scratch_shapes=scratch,
        compiler_params=pltpu.CompilerParams(vmem_limit_bytes=mb << 20),
    )(*args)


def dout_first_body(g_ref, w_ref, top_ref, bottom_ref, high_ref, low_ref):
    g = split(g_ref[...])
    w = split(w_ref[...])
    high_ref[...], low_ref[...] = w
    part = dot3(g, w, NT)
    top_ref[...] = part[:HALF]
    bottom_ref[...] = part[HALF:]


def dout_first(g, w):
    tile = 256
    count = w.shape[0] // tile
    half = pl.BlockSpec((HALF, tile), lambda i: (0, i))
    rows = pl.BlockSpec((tile, WIDE), lambda i: (i, 0))
    return pl.pallas_call(
        dout_first_body,
        grid=(count,),
        out_shape=[jax.ShapeDtypeStruct((HALF, WIDE), F32)] * 2 + [jax.ShapeDtypeStruct(w.shape, BF16)] * 2,
        in_specs=[pl.BlockSpec((Q, WIDE), lambda i: (0, 0)), rows],
        out_specs=[half, half, rows, rows],
        compiler_params=pltpu.CompilerParams(vmem_limit_bytes=24 << 20),
    )(g, w)


def dout_second_body(mine_ref, other_ref, fresh_ref, high_ref, low_ref, top_ref, bottom_ref, g_ref):
    core = lax.axis_index("head") % 2
    final = lax.axis_index("section") == lax.axis_size("section") - 1
    mine, other = mine_ref[...], other_ref[...]
    top = jnp.where(core == 0, mine, other)
    bottom = jnp.where(core == 0, other, mine)
    g = jnp.where(final, fresh_ref[...], jnp.concatenate([top, bottom], 0))
    g_ref[...] = g
    part = dot3(split(g), (high_ref[...], low_ref[...]), NT)
    top_ref[...] = part[:HALF]
    bottom_ref[...] = part[HALF:]


def dout_second(mine, other, fresh, high, low):
    half = ((HALF, WIDE), F32)
    return call(dout_second_body, [half, half, ((Q, WIDE), F32)], mine, other, fresh, high, low)


def split_body(w_ref, high_ref, low_ref):
    high_ref[...], low_ref[...] = split(w_ref[...])


def split_weights(w):
    tile = 256
    rows = pl.BlockSpec((tile, w.shape[1]), lambda i: (i, 0))
    return pl.pallas_call(
        split_body,
        grid=(w.shape[0] // tile,),
        out_shape=[jax.ShapeDtypeStruct(w.shape, BF16)] * 2,
        in_specs=[rows],
        out_specs=[rows, rows],
        compiler_params=pltpu.CompilerParams(vmem_limit_bytes=24 << 20),
    )(w)


def scores_body(q_ref, k_ref, table_ref, s_ref, top_ref):
    page = lax.axis_index("page")
    offset = table_ref[16]
    query = lax.broadcasted_iota(jnp.int32, (BLOCK, ROWS), 1) % Q
    key = lax.broadcasted_iota(jnp.int32, (BLOCK, ROWS), 0)
    top_ref[...] = jnp.zeros_like(top_ref)
    for g in range(KV):
        s = lax.dot_general(
            k_ref[:, g * HD : (g + 1) * HD],
            stacked(q_ref[...], g),
            NT,
            precision=lax.Precision.HIGHEST,
            preferred_element_type=F32,
        ) * SCALE
        best = None
        for b in range(KEYS // BLOCK):
            start = table_ref[page * (KEYS // BLOCK) + b] * BLOCK
            seen = start + key <= offset + query
            block = jnp.where(seen, s[b * BLOCK : (b + 1) * BLOCK], -1e30)
            s_ref[g, b * BLOCK : (b + 1) * BLOCK] = block
            most = jnp.max(block, axis=0, keepdims=True)
            best = most if best is None else jnp.maximum(best, most)
        top_ref[g : g + 1, :ROWS] = best


def scores(q, k, table):
    return call(scores_body, [((KV, KEYS, ROWS), F32), ((8, 256), F32)], q, k, table, smem=(2,))


def weights_body(s_ref, t0, t1, t2, t3, k_ref, v_ref, e_ref, top_ref, bottom_ref, kt_high, kt_low, v_high, v_low):
    best = jnp.maximum(jnp.maximum(t0[...], t1[...]), jnp.maximum(t2[...], t3[...]))
    v_high[...], v_low[...] = split(v_ref[...])
    groups, totals = [], []
    for g in range(KV):
        e = jnp.exp(s_ref[g] - best[g : g + 1, :ROWS])
        e_ref[g] = e
        totals.append(jnp.sum(e, axis=0, keepdims=True))
        kt = split(jnp.transpose(k_ref[:, g * HD : (g + 1) * HD]))
        kt_high[g], kt_low[g] = kt
        groups.append(jnp.transpose(dot3(kt, split(e), NN)))
    b = spread(groups)
    top_ref[:HALF] = b[:HALF]
    top_ref[HALF:] = jnp.zeros((8, WIDE), F32)
    for g in range(KV):
        top_ref[HALF + g : HALF + g + 1, :ROWS] = totals[g]
    bottom_ref[...] = b[HALF:]


def weights(s, tops, k, v):
    return call(
        weights_body,
        [
            ((KV, KEYS, ROWS), F32),
            ((HALF + 8, WIDE), F32),
            ((HALF, WIDE), F32),
            ((KV, HD, KEYS), BF16),
            ((KV, HD, KEYS), BF16),
            ((KEYS, KV * HD), BF16),
            ((KEYS, KV * HD), BF16),
        ],
        s, *tops, k, v,
    )


def products_body(d0, d1, d2, d3, e_ref, kt_high, kt_low, v_high, v_low, dp_ref, top_ref, bottom_ref, dout_ref):
    dout = jnp.concatenate([d0[...] + d1[...], d2[...] + d3[...]], 0)
    dout_ref[...] = dout
    groups, deltas = [], []
    for g in range(KV):
        cols = slice(g * HD, (g + 1) * HD)
        dp = dot3((v_high[:, cols], v_low[:, cols]), split(stacked(dout, g)), NT)
        dp_ref[g] = dp
        x = e_ref[g] * dp
        deltas.append(jnp.sum(x, axis=0, keepdims=True))
        groups.append(jnp.transpose(dot3((kt_high[g], kt_low[g]), split(x), NN)))
    a = spread(groups)
    top_ref[:HALF] = a[:HALF]
    top_ref[HALF:] = jnp.zeros((8, WIDE), F32)
    for g in range(KV):
        top_ref[HALF + g : HALF + g + 1, :ROWS] = deltas[g]
    bottom_ref[...] = a[HALF:]


def products(dout, e, kt_high, kt_low, v_high, v_low):
    return call(
        products_body,
        [((KV, KEYS, ROWS), F32), ((HALF + 8, WIDE), F32), ((HALF, WIDE), F32), ((Q, WIDE), F32)],
        *dout, e, kt_high, kt_low, v_high, v_low,
    )


def input_body(a0, a1, a2, a3, b0, b1, b2, b3, g_ref, high_ref, low_ref, keep_ref, send_ref):
    head = lax.axis_index("head")
    a_top, b_top = a0[...] + a1[...], b0[...] + b1[...]
    a = jnp.concatenate([a_top[:HALF], a2[...] + a3[...]], 0)
    b = jnp.concatenate([b_top[:HALF], b2[...] + b3[...]], 0)
    groups = []
    for g in range(KV):
        total = b_top[HALF + g : HALF + g + 1, :ROWS]
        delta = a_top[HALF + g : HALF + g + 1, :ROWS] / total
        groups.append((stacked(a, g) - as_columns(delta) * stacked(b, g)) * as_columns(SCALE / total))
    part = dot3(split(spread(groups)), (high_ref[...], low_ref[...]), NT)
    part = part + jnp.where(head == 0, g_ref[...], 0.0)
    first = head % 2 == 0
    keep_ref[...] = jnp.where(first, part[:HALF], part[HALF:])
    send_ref[...] = jnp.where(first, part[HALF:], part[:HALF])


def input_gradient(a, b, g, high, low):
    half = ((HALF, WIDE), F32)
    return call(input_body, [half, half], *a, *b, g, high, low)


def sums_body(a0, a1, b0, b1, e_ref, dp_ref, dout_ref, q_ref, key_ref, value_ref, key_out, value_out):
    a_top, b_top = a0[HALF:] + a1[HALF:], b0[HALF:] + b1[HALF:]
    for g in range(KV):
        total = b_top[g : g + 1, :ROWS]
        delta = a_top[g : g + 1, :ROWS] / total
        probs = e_ref[g] * (1.0 / total)
        d_score = probs * (dp_ref[g] - delta)
        cols = slice(g * HD, (g + 1) * HD)
        value_out[:, cols] = value_ref[:, cols] + dot3(split(probs), split(stacked(dout_ref[...], g)), NN)
        key_out[:, cols] = key_ref[:, cols] + SCALE * dot3(split(d_score), split(stacked(q_ref[...], g)), NN)


def gradient_sums(a, b, e, dp, dout, q, key_sum, value_sum):
    cache = ((KEYS, KV * HD), F32)
    return call(sums_body, [cache, cache], a[0], a[1], b[0], b[1], e, dp, dout, q, key_sum, value_sum)


def swap(bits, n=4):
    return [(i, i ^ bits) for i in range(n)]


def page_sum(top, bottom):
    top = top + lax.ppermute(top, "page", swap(1))
    bottom = bottom + lax.ppermute(bottom, "page", swap(3))
    return (top, lax.ppermute(top, "page", swap(3)), bottom, lax.ppermute(bottom, "page", swap(1)))


def page_all(x):
    return [x] + [lax.ppermute(x, "page", [(i, (i + d) % 4) for i in range(4)]) for d in (1, 2, 3)]


def back(flip=0):
    heads = 4
    return [
        (s * heads + h, (s - 1) * heads + (h ^ flip)) for s in range(1, 16) for h in range(heads)
    ]


def tied(value, after):
    return lax.optimization_barrier((value, after))[0]


def per_device(
    grad_in, grad_fresh, queries, key_cache, value_cache, key_fresh, value_fresh, key_grad_in, value_grad_in,
    page_table, offsets, page_fresh, offset_fresh, w_query, w_out,
):
    is_final = lax.axis_index("section") == lax.axis_size("section") - 1
    both = ("section", "head")
    g1, q1, q2 = grad_in[0], queries[0, 0], queries[0, 1]
    k1, v1 = key_cache[0], value_cache[0]
    pad = jnp.zeros((111,), jnp.int32)
    table1 = jnp.concatenate([page_table[0], offsets, pad])
    table_fresh = jnp.concatenate([page_fresh, offset_fresh, pad])

    top, bottom, wo_high, wo_low = dout_first(g1, w_out[0])
    dout1 = page_sum(top, bottom)
    s1, m1 = scores(q1, k1, table1)
    tops1 = page_all(m1)
    e1, b_top, b_bottom, *splits1 = weights(s1, tops1, k1, v1)
    b1 = page_sum(b_top, b_bottom)
    wq_high, wq_low = split_weights(w_query[0])

    back_section = [(i, i - 1) for i in range(1, 16)]
    table2 = jnp.where(is_final, table_fresh, lax.ppermute(table1, "section", back_section))
    k2 = jnp.where(is_final, key_fresh, lax.ppermute(k1, "section", back_section))
    v2 = jnp.where(is_final, value_fresh, lax.ppermute(v1, "section", back_section))

    dp1, a_top, a_bottom, dout1 = products(dout1, e1, *splits1)
    a1 = page_sum(a_top, a_bottom)
    keep, send = input_gradient(a1, b1, g1, wq_high, wq_low)
    part = keep + lax.ppermute(send, "head", swap(1))
    mine = lax.ppermute(part, both, back()) + lax.ppermute(part, both, back(2))
    other = lax.ppermute(mine, "head", swap(1))
    key_sum, value_sum = gradient_sums(a1, b1, e1, dp1, dout1, q1, key_grad_in[0], value_grad_in[0])
    key_sum, value_sum = tied((key_sum, value_sum), mine)
    key_sum = lax.ppermute(key_sum, "section", back_section)
    value_sum = lax.ppermute(value_sum, "section", back_section)

    s2, m2 = scores(q2, k2, table2)
    tops2 = page_all(m2)
    e2, b_top, b_bottom, *splits2 = weights(s2, tops2, k2, v2)
    b2 = page_sum(b_top, b_bottom)

    top, bottom, g2 = dout_second(mine, other, grad_fresh, wo_high, wo_low)
    dout2 = page_sum(top, bottom)
    dp2, a_top, a_bottom, dout2 = products(dout2, e2, *splits2)
    a2 = page_sum(a_top, a_bottom)
    keep, send = input_gradient(a2, b2, g2, wq_high, wq_low)
    part = keep + lax.ppermute(send, "head", swap(1))
    mine = part + lax.ppermute(part, "head", swap(2))
    other = lax.ppermute(mine, "head", swap(1))
    first = lax.axis_index("head") % 2 == 0
    grad_done = jnp.concatenate([jnp.where(first, mine, other), jnp.where(first, other, mine)], 0)
    key_final, value_final = gradient_sums(a2, b2, e2, dp2, dout2, q2, key_sum, value_sum)
    return (grad_done[None], key_final[None], value_final[None])


def solution(mesh):
    placed = (
        P("section", None, "page"),
        P(None, "page"),
        P("section", None, None, "head"),
        P("section", "page", "head"),
        P("section", "page", "head"),
        P("page", "head"),
        P("page", "head"),
        P("section", "page", "head"),
        P("section", "page", "head"),
        P("section", None),
        P("section"),
        P(),
        P(),
        P("section", "page", "head"),
        P("section", "head", "page"),
    )
    return jax.shard_map(
        per_device,
        mesh=mesh,
        in_specs=placed,
        out_specs=(
            P("section", None, "page"),
            P("section", "page", "head"),
            P("section", "page", "head"),
        ),
        check_vma=False,
    )
```

time: 426 us -> 144 us (0.34)
  waiting for transfers between devices: 150 us -> 31.4 us
  blocking collectives: 103 us -> 0 us
  starting transfers between devices: 27.6 us -> 67.8 us
  matrix products: 38.3 us -> 0 us
  local copies, waits for them, and re-layouts: 53.1 us -> 15.3 us
  other arithmetic: 34 us -> 4.91 us
  Pallas kernels: 0 us -> 20.7 us
  between operations: 16.2 us -> 2.56 us
    psum x4 -> x0, waiting for transfers between devices: 150 us -> none  [the longest x2 80.1 us: full_input(): return incoming + lax.psum(input_part, 'head')]
    all_gather x8 -> x0, blocking collectives: 103 us -> none  [merged(): pieces = jax.tree.map(lambda part: lax.all_gather(part, axis), value)]
    ppermute x7 -> x42, starting transfers between devices: 27.4 us -> 67.8 us  [the longest x6 11.3 us: page_sum(): bottom = bottom + lax.ppermute(bottom, 'page', swap(3))]
    dot_general x16 -> x0, matrix products: 38.3 us -> none  [the longest x2 9.59 us: layer_backward(): jnp.einsum('qh,ch->qc', d_query, w_query_layer, precision=precise)]
    ppermute x7 -> x42, waiting for transfers between devices: 0.02 us -> 31.4 us  [the longest x1 8.33 us: per_device(): lax.ppermute(table1, 'section', back_section)]
    pallas_call x0 -> x13, Pallas kernels: none -> 20.7 us  [the longest x11 18.6 us: call(): pl.pallas_call(body, out_shape=[jax.ShapeDtypeStruct(s, d) for s, d in ou...]
    add x19 -> x16, other arithmetic: 21.8 us -> 1.84 us  [the longest x1 0.95 us: per_device(): mine = lax.ppermute(part, both, back()) + lax.ppermute(part, both, back(2))]
    unnamed x54 -> x84, local copies, waits for them, and re-layouts: 1.9 us -> 14.6 us
  transfers between devices with their start and end apart: 11 -> 42, of which waited for: 4 -> 15; matrix products, arithmetic and copies ran while one was open for 29% -> 3% of each run, Pallas kernels for 0% -> 13%
where the time goes in v1:
time: 144 us; the launch traced here: 143 us
  starting transfers between devices  67.8 us (47%)
  waiting for transfers between devices  31.4 us (22%)
  Pallas kernels  20.7 us (14%)
  local copies, waits for them, and re-layouts  15.3 us (11%)
  other arithmetic  4.91 us (3%)
  between operations  2.56 us (2%)
    pallas_call x11, Pallas kernels, call(): pl.pallas_call(body, out_shape=[jax.ShapeDtypeStruct(s, d) for s, d in ou...  18.6 us
    unnamed x84, local copies, waits for them, and re-layouts  14.6 us
    ppermute x6, starting transfers between devices, page_sum(): bottom = bottom + lax.ppermute(bottom, 'page', swap(3))  11.3 us
    ppermute x6, starting transfers between devices, page_sum(): lax.ppermute(top, 'page', swap(3))  9.85 us
    ppermute x6, starting transfers between devices, page_all(): lax.ppermute(x, 'page', [(i, (i + d) % 4) for i in range(4)])  9.15 us
    ppermute x1, starting transfers between devices, per_device(): lax.ppermute(k1, 'section', back_section)  8.42 us
    ppermute x1, waiting for transfers between devices, per_device(): lax.ppermute(table1, 'section', back_section)  8.33 us
    ppermute x6, waiting for transfers between devices, page_sum(): lax.ppermute(bottom, 'page', swap(1))  7.34 us
  transfers between devices with their start and end apart: 42, of which 15 were waited for; matrix products, arithmetic and copies ran while one was open for 3% of the time, Pallas kernels for 13%

profile of v1, /device:TPU:24, one launch (start us, length us, event | category | flops | bytes accessed | tf_op | source)
XLA Modules:
  0.0 142.7 jit_solution(7014177635203634048)
XLA Ops:
  0.6 1.7 %copy-done.2 = f32[1,768,768]{2,1,0:T(8,128)S(1)} copy-done((f32[1,768,768]{2,1,0:T(8,128)S(1)}, f32[1,768,768]{2,1,0:T(8,128)}, u32[]{:S(2)}) %copy-start.2) | copy-done | bytes 2359320
  3.2 1.6 %shard_map.166 = (f32[32,768]{1,0:T(8,128)S(1)}, f32[32,768]{1,0:T(8,128)S(1)}, bf16[768,768]{1,0:T(8,128)(2,1)S(1)}, bf16[768,768]{1,0:T(8,128)(2,1)S(1)}) custom-call(f32[64,768]{1,0:T(8,128)S(1)} %bitcast.18, f32[768,768]{1,0:T(8,128)S(1)} %bitcast.16), custom_call_target="tpu_custom_call" | custom-call | tf_op jit(solution)/shard_map/pallas_call | solution.py:80
  5.9 2.8 %collective-permute-start.2 = (f32[32,768]{1,0:T(8,128)S(1)}, f32[32,768]{1,0:T(8,128)S(1)}, u32[]{:S(2)}, u32[]{:S(2)}) collective-permute-start(f32[32,768]{1,0:T(8,128)S(1)} %get-tuple-element.49), channel_id=1, source_target_pairs={{0,3},{1,2},{2,1},{3,0},{4,7},{5,6},{6,5},{7,4},{8,11},{9,10},{10,... | collective-permute-start | bytes 294920 | tf_op jit(solution)/shard_map/ppermute | solution.py:261
  14.8 2.1 %shard_map.167 = (f32[2,512,192]{2,1,0:T(8,128)S(1)}, f32[8,256]{1,0:T(8,128)S(1)}) custom-call(f32[64,768]{1,0:T(8,128)S(1)} %get-tuple-element.94.q_ref, f32[512,256]{1,0:T(8,128)} %bitcast.3.k_ref, s32[128]{0:T(128)S(1)} %pad_add_fusion.1.table_ref), custom_call_target="tpu_custom_call" | custom-call | tf_op jit(solution)/shard_map/pallas_call | solution.py:56
  18.4 2.1 %collective-permute-start.5 = (f32[8,256]{1,0:T(8,128)S(1)}, f32[8,256]{1,0:T(8,128)S(1)}, u32[]{:S(2)}, u32[]{:S(2)}) collective-permute-start(f32[8,256]{1,0:T(8,128)S(1)} %get-tuple-element.51.t0), channel_id=1, source_target_pairs={{0,2},{1,3},{2,0},{3,1},{4,6},{5,7},{6,4},{7,5},{8,10},{9,11},{10,... | collective-permute-start | bytes 24584 | tf_op jit(solution)/shard_map/ppermute | solution.py:266
  21.8 1.7 %collective-permute-done.5.t2 = f32[8,256]{1,0:T(8,128)S(1)} collective-permute-done((f32[8,256]{1,0:T(8,128)S(1)}, f32[8,256]{1,0:T(8,128)S(1)}, u32[]{:S(2)}, u32[]{:S(2)}) %collective-permute-start.5) | collective-permute-done | bytes 8224 | tf_op jit(solution)/shard_map/ppermute | solution.py:266
  24.2 2.0 %shard_map.168 = (f32[2,512,192]{2,1,0:T(8,128)S(1)}, f32[40,768]{1,0:T(8,128)S(1)}, f32[32,768]{1,0:T(8,128)S(1)}, bf16[2,128,512]{2,1,0:T(8,128)(2,1)S(1)}, bf...) custom-call(f32[2,512,192]{2,1,0:T(8,128)S(1)} %get-tuple-element.50.s_ref, ...), custom_call_target="tpu_custom_call" | custom-call | tf_op jit(solution)/shard_map/pallas_call | solution.py:56
  26.9 1.7 %shard_map.169 = (f32[2,512,192]{2,1,0:T(8,128)S(1)}, f32[40,768]{1,0:T(8,128)S(1)}, f32[32,768]{1,0:T(8,128)S(1)}, f32[64,768]{1,0:T(8,128)S(1)}) custom-call(f32[32,768]{1,0:T(8,128)S(1)} %add.53.d0, f32[32,768]{1,0:T(8,128)S(1)} %collective-permute-done.1.d1, f32[32,768]{1,0:T(8,128)S(1)} %add.54.d2, f32[32,768]{1,0:T(8,128)S(1)} %collective-permute-done.3.d3, ...), custom_call_target="tpu_custom_call" | custom-call | tf_op jit(solution)/shard_map/pallas_call | solution.py:56
  30.7 1.8 %collective-permute-start.13 = (f32[32,768]{1,0:T(8,128)S(1)}, f32[32,768]{1,0:T(8,128)S(1)}, u32[]{:S(2)}, u32[]{:S(2)}) collective-permute-start(f32[32,768]{1,0:T(8,128)S(1)} %get-tuple-element.60), channel_id=1, source_target_pairs={{0,3},{1,2},{2,1},{3,0},{4,7},{5,6},{6,5},{7,4},{8,11},{9,10},{10,... | collective-permute-start | bytes 294920 | tf_op jit(solution)/shard_map/ppermute | solution.py:261
  33.9 1.9 %collective-permute-start.12 = (f32[40,768]{1,0:T(8,128)S(1)}, f32[40,768]{1,0:T(8,128)S(1)}, u32[]{:S(2)}, u32[]{:S(2)}) collective-permute-start(f32[40,768]{1,0:T(8,128)S(1)} %add.57.b0), channel_id=1, source_target_pairs={{0,3},{1,2},{2,1},{3,0},{4,7},{5,6},{6,5},{7,4},{8,11},{9,10},{10,... | collective-permute-start | bytes 368648 | tf_op jit(solution)/shard_map/ppermute | solution.py:262
  37.4 8.4 %collective-permute-start.23 = (f32[512,256]{1,0:T(8,128)}, f32[512,256]{1,0:T(8,128)}, u32[]{:S(2)}, u32[]{:S(2)}) collective-permute-start(f32[512,256]{1,0:T(8,128)} %bitcast.3.k_ref), channel_id=1, source_target_pairs={{16,0},{32,16},{48,32},{64,48},{80,64},{96,80},{112,96},{128,112},... | collective-permute-start | bytes 1572872 | tf_op jit(solution)/shard_map/ppermute | solution.py:302
  46.0 2.3 %collective-permute-start.10 = (f32[32,768]{1,0:T(8,128)S(1)}, f32[32,768]{1,0:T(8,128)S(1)}, u32[]{:S(2)}, u32[]{:S(2)}) collective-permute-start(f32[32,768]{1,0:T(8,128)S(1)} %add.56.a2), channel_id=1, source_target_pairs={{0,1},{1,0},{2,3},{3,2},{4,5},{5,4},{6,7},{7,6},{8,9},{9,8},{10,11... | collective-permute-start | bytes 294920 | tf_op jit(solution)/shard_map/ppermute | solution.py:262
  48.7 1.8 %collective-permute-done.14.b3 = f32[32,768]{1,0:T(8,128)S(1)} collective-permute-done((f32[32,768]{1,0:T(8,128)S(1)}, f32[32,768]{1,0:T(8,128)S(1)}, u32[]{:S(2)}, u32[]{:S(2)}) %collective-permute-start.14) | collective-permute-done | bytes 98336 | tf_op jit(solution)/shard_map/ppermute | solution.py:262
  54.9 2.9 %collective-permute-start.16 = (f32[32,768]{1,0:T(8,128)}, f32[32,768]{1,0:T(8,128)}, u32[]{:S(2)}, u32[]{:S(2)}) collective-permute-start(f32[32,768]{1,0:T(8,128)} %add.59), channel_id=1, source_target_pairs={{16,0},{20,4},{24,8},{28,12},{32,16},{36,20},{40,24},{44,28},{48,3... | collective-permute-start | bytes 294920 | tf_op jit(solution)/shard_map/ppermute | solution.py:309
  57.8 1.9 %collective-permute-start.17 = (f32[32,768]{1,0:T(8,128)}, f32[32,768]{1,0:T(8,128)}, u32[]{:S(2)}, u32[]{:S(2)}) collective-permute-start(f32[32,768]{1,0:T(8,128)} %add.59), channel_id=1, source_target_pairs={{16,8},{20,12},{24,0},{28,4},{32,24},{36,28},{40,16},{44,20},{48,4... | collective-permute-start | bytes 294920 | tf_op jit(solution)/shard_map/ppermute | solution.py:309
  59.7 3.8 %collective-permute-start.28 = (f32[512,256]{1,0:T(8,128)}, f32[512,256]{1,0:T(8,128)}, u32[]{:S(2)}, u32[]{:S(2)}) collective-permute-start(f32[512,256]{1,0:T(8,128)} %bitcast.5.v_ref), channel_id=1, source_target_pairs={{16,0},{32,16},{48,32},{64,48},{80,64},{96,80},{112,96},{128,112},... | collective-permute-start | bytes 1572872 | tf_op jit(solution)/shard_map/ppermute | solution.py:303
  63.6 2.0 %collective-permute-start.24 = (s32[128]{0:T(128)S(1)}, s32[128]{0:T(128)S(1)}, u32[]{:S(2)}, u32[]{:S(2)}) collective-permute-start(s32[128]{0:T(128)S(1)} %pad_add_fusion.1.table_ref), channel_id=1, source_target_pairs={{16,0},{32,16},{48,32},{64,48},{80,64},{96,80},{112,96},{128,112},... | collective-permute-start | bytes 1544 | tf_op jit(solution)/shard_map/ppermute | solution.py:301
  67.3 8.3 %collective-permute-done.24 = s32[128]{0:T(128)S(1)} collective-permute-done((s32[128]{0:T(128)S(1)}, s32[128]{0:T(128)S(1)}, u32[]{:S(2)}, u32[]{:S(2)}) %collective-permute-start.24) | collective-permute-done | bytes 544 | tf_op jit(solution)/shard_map/ppermute | solution.py:301
  80.4 1.9 %collective-permute-start.21 = (f32[32,768]{1,0:T(8,128)S(1)}, f32[32,768]{1,0:T(8,128)S(1)}, u32[]{:S(2)}, u32[]{:S(2)}) collective-permute-start(f32[32,768]{1,0:T(8,128)S(1)} %get-tuple-element.68), channel_id=1, source_target_pairs={{0,3},{1,2},{2,1},{3,0},{4,7},{5,6},{6,5},{7,4},{8,11},{9,10},{10,... | collective-permute-start | bytes 294920 | tf_op jit(solution)/shard_map/ppermute | solution.py:261
  88.7 2.0 %collective-permute-start.27 = (f32[8,256]{1,0:T(8,128)S(1)}, f32[8,256]{1,0:T(8,128)S(1)}, u32[]{:S(2)}, u32[]{:S(2)}) collective-permute-start(f32[8,256]{1,0:T(8,128)S(1)} %get-tuple-element.70.t0), channel_id=1, source_target_pairs={{0,3},{1,0},{2,1},{3,2},{4,7},{5,4},{6,5},{7,6},{8,11},{9,8},{10,9... | collective-permute-start | bytes 24584 | tf_op jit(solution)/shard_map/ppermute | solution.py:266
  90.9 1.9 %collective-permute-start.20 = (f32[32,768]{1,0:T(8,128)S(1)}, f32[32,768]{1,0:T(8,128)S(1)}, u32[]{:S(2)}, u32[]{:S(2)}) collective-permute-start(f32[32,768]{1,0:T(8,128)S(1)} %add.61.d0), channel_id=1, source_target_pairs={{0,3},{1,2},{2,1},{3,0},{4,7},{5,6},{6,5},{7,4},{8,11},{9,10},{10,... | collective-permute-start | bytes 294920 | tf_op jit(solution)/shard_map/ppermute | solution.py:262
  94.9 1.6 %collective-permute-start.35 = (f32[32,768]{1,0:T(8,128)S(1)}, f32[32,768]{1,0:T(8,128)S(1)}, u32[]{:S(2)}, u32[]{:S(2)}) collective-permute-start(f32[32,768]{1,0:T(8,128)S(1)} %get-tuple-element.79), channel_id=1, source_target_pairs={{0,3},{1,2},{2,1},{3,0},{4,7},{5,6},{6,5},{7,4},{8,11},{9,10},{10,... | collective-permute-start | bytes 294920 | tf_op jit(solution)/shard_map/ppermute | solution.py:261
  97.8 1.7 %shard_map.175 = (f32[2,512,192]{2,1,0:T(8,128)S(1)}, f32[40,768]{1,0:T(8,128)S(1)}, f32[32,768]{1,0:T(8,128)S(1)}, f32[64,768]{1,0:T(8,128)S(1)}) custom-call(f32[32,768]{1,0:T(8,128)S(1)} %add.61.d0, f32[32,768]{1,0:T(8,128)S(1)} %collective-permute-done.20.d1, f32[32,768]{1,0:T(8,128)S(1)} %add.62.d2, f32[32,768]{1,0:T(8,128)S(1)} %collective-permute-done.22.d3, ...), custom_call_target="tpu_custom_call" | custom-call | tf_op jit(solution)/shard_map/pallas_call | solution.py:56
  101.3 2.0 %shard_map.177 = (f32[512,256]{1,0:T(8,128)}, f32[512,256]{1,0:T(8,128)}) custom-call(f32[40,768]{1,0:T(8,128)S(1)} %copy-done.13, f32[40,768]{1,0:T(8,128)S(1)} %copy-done.27, f32[40,768]{1,0:T(8,128)S(1)} %add.57.b0, f32[40,768]{1,0:T(8,128)S(1)} %copy-done.25, f32[2,512,192]{2,1,0:T(8,128)S(1)} %get-tuple-element.52.e_ref, f32[2,512,192]{2,1,0:T(8,128)S(1)} %copy-done.17, ...), custom_call_target="tpu_custom_call" | custom-call | tf_op jit(solution)/shard_map/pallas_call | solution.py:56
  103.3 7.1 %collective-permute-start.40 = (f32[512,256]{1,0:T(8,128)}, f32[512,256]{1,0:T(8,128)}, u32[]{:S(2)}, u32[]{:S(2)}) collective-permute-start(f32[512,256]{1,0:T(8,128)} %get-tuple-element.89), channel_id=1, source_target_pairs={{16,0},{32,16},{48,32},{64,48},{80,64},{96,80},{112,96},{128,112},... | collective-permute-start | bytes 1572872 | tf_op jit(solution)/shard_map/ppermute | solution.py:313
  110.4 1.9 %collective-permute-start.41 = (f32[512,256]{1,0:T(8,128)}, f32[512,256]{1,0:T(8,128)}, u32[]{:S(2)}, u32[]{:S(2)}) collective-permute-start(f32[512,256]{1,0:T(8,128)} %get-tuple-element.90), channel_id=1, source_target_pairs={{16,0},{32,16},{48,32},{64,48},{80,64},{96,80},{112,96},{128,112},... | collective-permute-start | bytes 1572872 | tf_op jit(solution)/shard_map/ppermute | solution.py:314
  112.3 1.7 %collective-permute-start.31 = (f32[32,768]{1,0:T(8,128)S(1)}, f32[32,768]{1,0:T(8,128)S(1)}, u32[]{:S(2)}, u32[]{:S(2)}) collective-permute-start(f32[32,768]{1,0:T(8,128)S(1)} %get-tuple-element.77), channel_id=1, source_target_pairs={{0,3},{1,2},{2,1},{3,0},{4,7},{5,6},{6,5},{7,4},{8,11},{9,10},{10,... | collective-permute-start | bytes 294920 | tf_op jit(solution)/shard_map/ppermute | solution.py:261
  114.6 1.7 %collective-permute-start.34 = (f32[40,768]{1,0:T(8,128)S(1)}, f32[40,768]{1,0:T(8,128)S(1)}, u32[]{:S(2)}, u32[]{:S(2)}) collective-permute-start(f32[40,768]{1,0:T(8,128)S(1)} %add.65.b0), channel_id=1, source_target_pairs={{0,3},{1,2},{2,1},{3,0},{4,7},{5,6},{6,5},{7,4},{8,11},{9,10},{10,... | collective-permute-start | bytes 368648 | tf_op jit(solution)/shard_map/ppermute | solution.py:262
  116.3 2.6 %collective-permute-done.31 = f32[32,768]{1,0:T(8,128)S(1)} collective-permute-done((f32[32,768]{1,0:T(8,128)S(1)}, f32[32,768]{1,0:T(8,128)S(1)}, u32[]{:S(2)}, u32[]{:S(2)}) %collective-permute-start.31) | collective-permute-done | bytes 98336 | tf_op jit(solution)/shard_map/ppermute | solution.py:261
  120.8 4.5 %collective-permute-done.32.a3 = f32[32,768]{1,0:T(8,128)S(1)} collective-permute-done((f32[32,768]{1,0:T(8,128)S(1)}, f32[32,768]{1,0:T(8,128)S(1)}, u32[]{:S(2)}, u32[]{:S(2)}) %collective-permute-start.32) | collective-permute-done | bytes 98336 | tf_op jit(solution)/shard_map/ppermute | solution.py:262
  129.0 3.9 %collective-permute-done.38 = f32[32,768]{1,0:T(8,128)S(1)} collective-permute-done((f32[32,768]{1,0:T(8,128)S(1)}, f32[32,768]{1,0:T(8,128)S(1)}, u32[]{:S(2)}, u32[]{:S(2)}) %collective-permute-start.38) | collective-permute-done | bytes 98336 | tf_op jit(solution)/shard_map/ppermute | solution.py:327
  138.8 3.2 %shard_map.178 = (f32[512,256]{1,0:T(8,128)}, f32[512,256]{1,0:T(8,128)}) custom-call(f32[40,768]{1,0:T(8,128)S(1)} %copy-done.15, f32[40,768]{1,0:T(8,128)S(1)} %copy-done.31, f32[40,768]{1,0:T(8,128)S(1)} %add.65.b0, f32[40,768]{1,0:T(8,128)S(1)} %copy-done.29, f32[2,512,192]{2,1,0:T(8,128)S(1)} %copy-done.1, f32[2,512,192]{2,1,0:T(8,128)S(1)} %copy-done.19, ...), custom_call_target="tpu_custom_call" | custom-call | tf_op jit(solution)/shard_map/pallas_call | solution.py:56
  (173 shorter events, 51.5 us)
Async XLA Ops:
  5.9 5.8 %collective-permute-start.2 = (f32[32,768]{1,0:T(8,128)S(1)}, f32[32,768]{1,0:T(8,128)S(1)}, u32[]{:S(2)}, u32[]{:S(2)}) collective-permute-start(f32[32,768]{1,0:T(8,128)S(1)} %get-tuple-element.49), channel_id=1, source_target_pairs={{0,3},{1,2},{2,1},{3,0},{4,7},{5,6},{6,5},{7,4},{8,11},{9,10},{10,... | collective-permute-start | bytes 294920 | tf_op jit(solution)/shard_map/ppermute | solution.py:261
  11.7 15.1 %collective-permute-start.3 = (f32[32,768]{1,0:T(8,128)S(1)}, f32[32,768]{1,0:T(8,128)S(1)}, u32[]{:S(2)}, u32[]{:S(2)}) collective-permute-start(f32[32,768]{1,0:T(8,128)S(1)} %add.54.d2), channel_id=1, source_target_pairs={{0,1},{1,0},{2,3},{3,2},{4,5},{5,4},{6,7},{7,6},{8,9},{9,8},{10,11... | collective-permute-start | bytes 294920 | tf_op jit(solution)/shard_map/ppermute | solution.py:262
  13.4 13.4 %collective-permute-start.1 = (f32[32,768]{1,0:T(8,128)S(1)}, f32[32,768]{1,0:T(8,128)S(1)}, u32[]{:S(2)}, u32[]{:S(2)}) collective-permute-start(f32[32,768]{1,0:T(8,128)S(1)} %add.53.d0), channel_id=1, source_target_pairs={{0,3},{1,2},{2,1},{3,0},{4,7},{5,6},{6,5},{7,4},{8,11},{9,10},{10,... | collective-permute-start | bytes 294920 | tf_op jit(solution)/shard_map/ppermute | solution.py:262
  26.2 7.7 %collective-permute-start.11 = (f32[40,768]{1,0:T(8,128)S(1)}, f32[40,768]{1,0:T(8,128)S(1)}, u32[]{:S(2)}, u32[]{:S(2)}) collective-permute-start(f32[40,768]{1,0:T(8,128)S(1)} %get-tuple-element.59), channel_id=1, source_target_pairs={{0,1},{1,0},{2,3},{3,2},{4,5},{5,4},{6,7},{7,6},{8,9},{9,8},{10,11... | collective-permute-start | bytes 368648 | tf_op jit(solution)/shard_map/ppermute | solution.py:260
  29.2 6.7 %collective-permute-start.7 = (f32[40,768]{1,0:T(8,128)S(1)}, f32[40,768]{1,0:T(8,128)S(1)}, u32[]{:S(2)}, u32[]{:S(2)}) collective-permute-start(f32[40,768]{1,0:T(8,128)S(1)} %get-tuple-element.57), channel_id=1, source_target_pairs={{0,1},{1,0},{2,3},{3,2},{4,5},{5,4},{6,7},{7,6},{8,9},{9,8},{10,11... | collective-permute-start | bytes 368648 | tf_op jit(solution)/shard_map/ppermute | solution.py:260
  30.7 15.1 %collective-permute-start.13 = (f32[32,768]{1,0:T(8,128)S(1)}, f32[32,768]{1,0:T(8,128)S(1)}, u32[]{:S(2)}, u32[]{:S(2)}) collective-permute-start(f32[32,768]{1,0:T(8,128)S(1)} %get-tuple-element.60), channel_id=1, source_target_pairs={{0,3},{1,2},{2,1},{3,0},{4,7},{5,6},{6,5},{7,4},{8,11},{9,10},{10,... | collective-permute-start | bytes 294920 | tf_op jit(solution)/shard_map/ppermute | solution.py:261
  32.5 13.4 %collective-permute-start.9 = (f32[32,768]{1,0:T(8,128)S(1)}, f32[32,768]{1,0:T(8,128)S(1)}, u32[]{:S(2)}, u32[]{:S(2)}) collective-permute-start(f32[32,768]{1,0:T(8,128)S(1)} %get-tuple-element.58), channel_id=1, source_target_pairs={{0,3},{1,2},{2,1},{3,0},{4,7},{5,6},{6,5},{7,4},{8,11},{9,10},{10,... | collective-permute-start | bytes 294920 | tf_op jit(solution)/shard_map/ppermute | solution.py:261
  33.9 16.6 %collective-permute-start.12 = (f32[40,768]{1,0:T(8,128)S(1)}, f32[40,768]{1,0:T(8,128)S(1)}, u32[]{:S(2)}, u32[]{:S(2)}) collective-permute-start(f32[40,768]{1,0:T(8,128)S(1)} %add.57.b0), channel_id=1, source_target_pairs={{0,3},{1,2},{2,1},{3,0},{4,7},{5,6},{6,5},{7,4},{8,11},{9,10},{10,... | collective-permute-start | bytes 368648 | tf_op jit(solution)/shard_map/ppermute | solution.py:262
  35.9 15.7 %collective-permute-start.8 = (f32[40,768]{1,0:T(8,128)S(1)}, f32[40,768]{1,0:T(8,128)S(1)}, u32[]{:S(2)}, u32[]{:S(2)}) collective-permute-start(f32[40,768]{1,0:T(8,128)S(1)} %add.55.a0), channel_id=1, source_target_pairs={{0,3},{1,2},{2,1},{3,0},{4,7},{5,6},{6,5},{7,4},{8,11},{9,10},{10,... | collective-permute-start | bytes 368648 | tf_op jit(solution)/shard_map/ppermute | solution.py:262
  37.4 45.6 %collective-permute-start.23 = (f32[512,256]{1,0:T(8,128)}, f32[512,256]{1,0:T(8,128)}, u32[]{:S(2)}, u32[]{:S(2)}) collective-permute-start(f32[512,256]{1,0:T(8,128)} %bitcast.3.k_ref), channel_id=1, source_target_pairs={{16,0},{32,16},{48,32},{64,48},{80,64},{96,80},{112,96},{128,112},... | collective-permute-start | bytes 1572872 | tf_op jit(solution)/shard_map/ppermute | solution.py:302
  46.0 5.6 %collective-permute-start.10 = (f32[32,768]{1,0:T(8,128)S(1)}, f32[32,768]{1,0:T(8,128)S(1)}, u32[]{:S(2)}, u32[]{:S(2)}) collective-permute-start(f32[32,768]{1,0:T(8,128)S(1)} %add.56.a2), channel_id=1, source_target_pairs={{0,1},{1,0},{2,3},{3,2},{4,5},{5,4},{6,7},{7,6},{8,9},{9,8},{10,11... | collective-permute-start | bytes 294920 | tf_op jit(solution)/shard_map/ppermute | solution.py:262
  54.9 11.3 %collective-permute-start.16 = (f32[32,768]{1,0:T(8,128)}, f32[32,768]{1,0:T(8,128)}, u32[]{:S(2)}, u32[]{:S(2)}) collective-permute-start(f32[32,768]{1,0:T(8,128)} %add.59), channel_id=1, source_target_pairs={{16,0},{20,4},{24,8},{28,12},{32,16},{36,20},{40,24},{44,28},{48,3... | collective-permute-start | bytes 294920 | tf_op jit(solution)/shard_map/ppermute | solution.py:309
  57.8 8.5 %collective-permute-start.17 = (f32[32,768]{1,0:T(8,128)}, f32[32,768]{1,0:T(8,128)}, u32[]{:S(2)}, u32[]{:S(2)}) collective-permute-start(f32[32,768]{1,0:T(8,128)} %add.59), channel_id=1, source_target_pairs={{16,8},{20,12},{24,0},{28,4},{32,24},{36,28},{40,16},{44,20},{48,4... | collective-permute-start | bytes 294920 | tf_op jit(solution)/shard_map/ppermute | solution.py:309
  59.7 31.1 %collective-permute-start.28 = (f32[512,256]{1,0:T(8,128)}, f32[512,256]{1,0:T(8,128)}, u32[]{:S(2)}, u32[]{:S(2)}) collective-permute-start(f32[512,256]{1,0:T(8,128)} %bitcast.5.v_ref), channel_id=1, source_target_pairs={{16,0},{32,16},{48,32},{64,48},{80,64},{96,80},{112,96},{128,112},... | collective-permute-start | bytes 1572872 | tf_op jit(solution)/shard_map/ppermute | solution.py:303
  63.6 12.1 %collective-permute-start.24 = (s32[128]{0:T(128)S(1)}, s32[128]{0:T(128)S(1)}, u32[]{:S(2)}, u32[]{:S(2)}) collective-permute-start(s32[128]{0:T(128)S(1)} %pad_add_fusion.1.table_ref), channel_id=1, source_target_pairs={{16,0},{32,16},{48,32},{64,48},{80,64},{96,80},{112,96},{128,112},... | collective-permute-start | bytes 1544 | tf_op jit(solution)/shard_map/ppermute | solution.py:301
  67.2 8.5 %collective-permute-start.18 = (f32[32,768]{1,0:T(8,128)S(1)}, f32[32,768]{1,0:T(8,128)S(1)}, u32[]{:S(2)}, u32[]{:S(2)}) collective-permute-start(f32[32,768]{1,0:T(8,128)S(1)} %add.60.mine_ref), channel_id=1, source_target_pairs={{0,4},{4,0},{8,12},{12,8},{1,5},{5,1},{9,13},{13,9},{2,6},{6,2},{1... | collective-permute-start | bytes 294920 | tf_op jit(solution)/shard_map/ppermute | solution.py:310
  80.4 8.3 %collective-permute-start.21 = (f32[32,768]{1,0:T(8,128)S(1)}, f32[32,768]{1,0:T(8,128)S(1)}, u32[]{:S(2)}, u32[]{:S(2)}) collective-permute-start(f32[32,768]{1,0:T(8,128)S(1)} %get-tuple-element.68), channel_id=1, source_target_pairs={{0,3},{1,2},{2,1},{3,0},{4,7},{5,6},{6,5},{7,4},{8,11},{9,10},{10,... | collective-permute-start | bytes 294920 | tf_op jit(solution)/shard_map/ppermute | solution.py:261
  82.4 8.3 %collective-permute-start.19 = (f32[32,768]{1,0:T(8,128)S(1)}, f32[32,768]{1,0:T(8,128)S(1)}, u32[]{:S(2)}, u32[]{:S(2)}) collective-permute-start(f32[32,768]{1,0:T(8,128)S(1)} %get-tuple-element.67), channel_id=1, source_target_pairs={{0,1},{1,0},{2,3},{3,2},{4,5},{5,4},{6,7},{7,6},{8,9},{9,8},{10,11... | collective-permute-start | bytes 294920 | tf_op jit(solution)/shard_map/ppermute | solution.py:260
  85.8 8.2 %collective-permute-start.25 = (f32[8,256]{1,0:T(8,128)S(1)}, f32[8,256]{1,0:T(8,128)S(1)}, u32[]{:S(2)}, u32[]{:S(2)}) collective-permute-start(f32[8,256]{1,0:T(8,128)S(1)} %get-tuple-element.70.t0), channel_id=1, source_target_pairs={{0,1},{1,2},{2,3},{3,0},{4,5},{5,6},{6,7},{7,4},{8,9},{9,10},{10,1... | collective-permute-start | bytes 24584 | tf_op jit(solution)/shard_map/ppermute | solution.py:266
  87.2 6.7 %collective-permute-start.26 = (f32[8,256]{1,0:T(8,128)S(1)}, f32[8,256]{1,0:T(8,128)S(1)}, u32[]{:S(2)}, u32[]{:S(2)}) collective-permute-start(f32[8,256]{1,0:T(8,128)S(1)} %get-tuple-element.70.t0), channel_id=1, source_target_pairs={{0,2},{1,3},{2,0},{3,1},{4,6},{5,7},{6,4},{7,5},{8,10},{9,11},{10,... | collective-permute-start | bytes 24584 | tf_op jit(solution)/shard_map/ppermute | solution.py:266
  90.7 6.4 %collective-permute-start.22 = (f32[32,768]{1,0:T(8,128)S(1)}, f32[32,768]{1,0:T(8,128)S(1)}, u32[]{:S(2)}, u32[]{:S(2)}) collective-permute-start(f32[32,768]{1,0:T(8,128)S(1)} %add.62.d2), channel_id=1, source_target_pairs={{0,1},{1,0},{2,3},{3,2},{4,5},{5,4},{6,7},{7,6},{8,9},{9,8},{10,11... | collective-permute-start | bytes 294920 | tf_op jit(solution)/shard_map/ppermute | solution.py:262
  90.9 6.9 %collective-permute-start.20 = (f32[32,768]{1,0:T(8,128)S(1)}, f32[32,768]{1,0:T(8,128)S(1)}, u32[]{:S(2)}, u32[]{:S(2)}) collective-permute-start(f32[32,768]{1,0:T(8,128)S(1)} %add.61.d0), channel_id=1, source_target_pairs={{0,3},{1,2},{2,1},{3,0},{4,7},{5,6},{6,5},{7,4},{8,11},{9,10},{10,... | collective-permute-start | bytes 294920 | tf_op jit(solution)/shard_map/ppermute | solution.py:262
  94.9 17.5 %collective-permute-start.35 = (f32[32,768]{1,0:T(8,128)S(1)}, f32[32,768]{1,0:T(8,128)S(1)}, u32[]{:S(2)}, u32[]{:S(2)}) collective-permute-start(f32[32,768]{1,0:T(8,128)S(1)} %get-tuple-element.79), channel_id=1, source_target_pairs={{0,3},{1,2},{2,1},{3,0},{4,7},{5,6},{6,5},{7,4},{8,11},{9,10},{10,... | collective-permute-start | bytes 294920 | tf_op jit(solution)/shard_map/ppermute | solution.py:261
  96.5 17.6 %collective-permute-start.33 = (f32[40,768]{1,0:T(8,128)S(1)}, f32[40,768]{1,0:T(8,128)S(1)}, u32[]{:S(2)}, u32[]{:S(2)}) collective-permute-start(f32[40,768]{1,0:T(8,128)S(1)} %get-tuple-element.78), channel_id=1, source_target_pairs={{0,1},{1,0},{2,3},{3,2},{4,5},{5,4},{6,7},{7,6},{8,9},{9,8},{10,11... | collective-permute-start | bytes 368648 | tf_op jit(solution)/shard_map/ppermute | solution.py:260
  100.4 14.2 %collective-permute-start.29 = (f32[40,768]{1,0:T(8,128)S(1)}, f32[40,768]{1,0:T(8,128)S(1)}, u32[]{:S(2)}, u32[]{:S(2)}) collective-permute-start(f32[40,768]{1,0:T(8,128)S(1)} %get-tuple-element.76), channel_id=1, source_target_pairs={{0,1},{1,0},{2,3},{3,2},{4,5},{5,4},{6,7},{7,6},{8,9},{9,8},{10,11... | collective-permute-start | bytes 368648 | tf_op jit(solution)/shard_map/ppermute | solution.py:260
  103.3 29.7 %collective-permute-start.40 = (f32[512,256]{1,0:T(8,128)}, f32[512,256]{1,0:T(8,128)}, u32[]{:S(2)}, u32[]{:S(2)}) collective-permute-start(f32[512,256]{1,0:T(8,128)} %get-tuple-element.89), channel_id=1, source_target_pairs={{16,0},{32,16},{48,32},{64,48},{80,64},{96,80},{112,96},{128,112},... | collective-permute-start | bytes 1572872 | tf_op jit(solution)/shard_map/ppermute | solution.py:313
  110.4 22.6 %collective-permute-start.41 = (f32[512,256]{1,0:T(8,128)}, f32[512,256]{1,0:T(8,128)}, u32[]{:S(2)}, u32[]{:S(2)}) collective-permute-start(f32[512,256]{1,0:T(8,128)} %get-tuple-element.90), channel_id=1, source_target_pairs={{16,0},{32,16},{48,32},{64,48},{80,64},{96,80},{112,96},{128,112},... | collective-permute-start | bytes 1572872 | tf_op jit(solution)/shard_map/ppermute | solution.py:314
  112.3 6.6 %collective-permute-start.31 = (f32[32,768]{1,0:T(8,128)S(1)}, f32[32,768]{1,0:T(8,128)S(1)}, u32[]{:S(2)}, u32[]{:S(2)}) collective-permute-start(f32[32,768]{1,0:T(8,128)S(1)} %get-tuple-element.77), channel_id=1, source_target_pairs={{0,3},{1,2},{2,1},{3,0},{4,7},{5,6},{6,5},{7,4},{8,11},{9,10},{10,... | collective-permute-start | bytes 294920 | tf_op jit(solution)/shard_map/ppermute | solution.py:261
  114.1 6.4 %collective-permute-start.36 = (f32[32,768]{1,0:T(8,128)S(1)}, f32[32,768]{1,0:T(8,128)S(1)}, u32[]{:S(2)}, u32[]{:S(2)}) collective-permute-start(f32[32,768]{1,0:T(8,128)S(1)} %add.66.b2), channel_id=1, source_target_pairs={{0,1},{1,0},{2,3},{3,2},{4,5},{5,4},{6,7},{7,6},{8,9},{9,8},{10,11... | collective-permute-start | bytes 294920 | tf_op jit(solution)/shard_map/ppermute | solution.py:262
  114.6 6.2 %collective-permute-start.34 = (f32[40,768]{1,0:T(8,128)S(1)}, f32[40,768]{1,0:T(8,128)S(1)}, u32[]{:S(2)}, u32[]{:S(2)}) collective-permute-start(f32[40,768]{1,0:T(8,128)S(1)} %add.65.b0), channel_id=1, source_target_pairs={{0,3},{1,2},{2,1},{3,0},{4,7},{5,6},{6,5},{7,4},{8,11},{9,10},{10,... | collective-permute-start | bytes 368648 | tf_op jit(solution)/shard_map/ppermute | solution.py:262
  118.9 6.3 %collective-permute-start.30 = (f32[40,768]{1,0:T(8,128)S(1)}, f32[40,768]{1,0:T(8,128)S(1)}, u32[]{:S(2)}, u32[]{:S(2)}) collective-permute-start(f32[40,768]{1,0:T(8,128)S(1)} %add.63.a0), channel_id=1, source_target_pairs={{0,3},{1,2},{2,1},{3,0},{4,7},{5,6},{6,5},{7,4},{8,11},{9,10},{10,... | collective-permute-start | bytes 368648 | tf_op jit(solution)/shard_map/ppermute | solution.py:262
  132.9 9.1 %collective-permute-start.39 = (f32[32,768]{1,0:T(8,128)S(1)}, f32[32,768]{1,0:T(8,128)S(1)}, u32[]{:S(2)}, u32[]{:S(2)}) collective-permute-start(f32[32,768]{1,0:T(8,128)S(1)} %add.68), channel_id=1, source_target_pairs={{0,4},{4,0},{8,12},{12,8},{1,5},{5,1},{9,13},{13,9},{2,6},{6,2},{1... | collective-permute-start | bytes 294920 | tf_op jit(solution)/shard_map/ppermute | solution.py:328
  (52 other events, 279.6 us)

commit v2 on v1

v2 whole, which is shorter than its diff:
```python
import functools

import jax
import jax.numpy as jnp
from jax import lax
from jax.experimental import pallas as pl
from jax.experimental.pallas import tpu as pltpu
from jax.sharding import PartitionSpec as P

HD = 128
BLOCK = 128
Q = 64
HALF = Q // 2
FRONT_MB = 60
TAIL = 8
KEYS = 512
KV = 2
GROUP = 3
ROWS = GROUP * Q
WIDE = KV * GROUP * HD
SCALE = HD ** (-0.5)
F32 = jnp.float32
BF16 = jnp.bfloat16
NN = (((1,), (0,)), ((), ()))
NT = (((1,), (1,)), ((), ()))


def split(x):
    high = x.astype(BF16)
    return high, (x - high.astype(F32)).astype(BF16)


def dot(a, b, dims):
    return lax.dot_general(a, b, dims, preferred_element_type=F32)


def dot3(a, b, dims):
    (a_high, a_low), (b_high, b_low) = a, b
    return dot(a_high, b_high, dims) + (dot(a_low, b_high, dims) + dot(a_high, b_low, dims))


def stacked(x, g):
    return jnp.concatenate([x[:, (g * GROUP + r) * HD : (g * GROUP + r + 1) * HD] for r in range(GROUP)], 0)


def spread(groups):
    return jnp.concatenate([groups[g][r * Q : (r + 1) * Q] for g in range(KV) for r in range(GROUP)], 1)


def as_columns(row):
    return jnp.transpose(jnp.broadcast_to(row, (HD, ROWS)))


def call(body, outs, *args, scratch=(), mb=6, smem=(), free=()):
    spaces = [pltpu.SMEM if i in smem else pl.ANY if i in free else pltpu.VMEM for i in range(len(args))]
    return pl.pallas_call(
        body,
        out_shape=[jax.ShapeDtypeStruct(s, d) for s, d in outs],
        in_specs=[pl.BlockSpec(memory_space=space) for space in spaces],
        out_specs=[pl.BlockSpec(memory_space=pltpu.VMEM)] * len(outs),
        scratch_shapes=scratch,
        cost_estimate=pl.CostEstimate(flops=0, bytes_accessed=0, transcendentals=0),
        compiler_params=pltpu.CompilerParams(vmem_limit_bytes=mb << 20),
    )(*args)


SCORES = ((KV, KEYS, ROWS), F32)
CACHE = ((KEYS, KV * HD), F32)
FULL = ((Q, WIDE), F32)
PIECE = ((HALF, WIDE), F32)
WITH_ROWS = ((Q + TAIL, WIDE), F32)
STATS = ((TAIL, WIDE), F32)
PACK = ((2 * KEYS + TAIL, KV * HD), F32)
WEIGHT = ((WIDE, WIDE), BF16)
KEYS_T = ((KV, HD, KEYS), BF16)
CACHE_BF = ((KEYS, KV * HD), BF16)


def limits(table_ref, offset_ref):
    page = lax.axis_index("page")
    rows = []
    for b in range(8):
        bound = offset_ref[0] - table_ref[page * 4 + b % 4] * BLOCK
        rows.append(jnp.full((1, KV * HD), bound, jnp.int32).astype(F32))
    return jnp.concatenate(rows, 0)


def masked_scores(g, q, k, bounds, s_ref):
    lead = (
        lax.broadcasted_iota(jnp.int32, (BLOCK, ROWS), 0) - lax.broadcasted_iota(jnp.int32, (BLOCK, ROWS), 1) % Q
    ).astype(F32)
    s = lax.dot_general(
        k, stacked(q, g), NT, precision=lax.Precision.HIGHEST, preferred_element_type=F32
    ) * SCALE
    best = None
    for b in range(KEYS // BLOCK):
        block = jnp.where(lead <= bounds[b : b + 1, :ROWS], s[b * BLOCK : (b + 1) * BLOCK], -1e30)
        s_ref[g, b * BLOCK : (b + 1) * BLOCK] = block
        most = jnp.max(block, axis=0, keepdims=True)
        best = most if best is None else jnp.maximum(best, most)
    return best


def front_body(
    q_hbm, k_hbm, v_hbm, g_hbm, w_hbm, table_ref, offset_ref, fresh_table_ref, fresh_offset_ref,
    s_ref, part_ref, pack_hbm, fresh_ref,
    q_ref, pack_ref, g_ref, w_ref, sems,
):
    count = 3
    tile = WIDE // count
    copies = [
        pltpu.make_async_copy(q_hbm.at[0, 0], q_ref, sems.at[0]),
        pltpu.make_async_copy(k_hbm.at[0], pack_ref.at[pl.ds(0, KEYS)], sems.at[1]),
        pltpu.make_async_copy(g_hbm.at[0], g_ref, sems.at[2]),
    ]
    for i in range(count):
        part = pl.ds(i * tile, tile)
        copies.append(pltpu.make_async_copy(w_hbm.at[0, part], w_ref.at[part], sems.at[3 + i]))
    for copy in copies:
        copy.start()
    load = pltpu.make_async_copy(v_hbm.at[0], pack_ref.at[pl.ds(KEYS, KEYS)], sems.at[3 + count])
    load.start()
    bounds = limits(table_ref, offset_ref)
    pack_ref[2 * KEYS :] = bounds
    fresh_ref[...] = limits(fresh_table_ref, fresh_offset_ref)
    copies[0].wait()
    copies[1].wait()
    part_ref[Q:] = jnp.full((TAIL, WIDE), -1e30, F32)
    for g in range(KV):
        best = masked_scores(g, q_ref[...], pack_ref[:KEYS, g * HD : (g + 1) * HD], bounds, s_ref)
        part_ref[Q + g : Q + g + 1, :ROWS] = best
    load.wait()
    store = pltpu.make_async_copy(pack_ref, pack_hbm, sems.at[4 + count])
    store.start()
    copies[2].wait()
    grad = split(g_ref[...])
    for i in range(count):
        copies[3 + i].wait()
        part = slice(i * tile, (i + 1) * tile)
        part_ref[:Q, part] = dot3(grad, split(w_ref[part]), NT)
    store.wait()


def front(queries, keys, values, grad, w_out, table, offset, fresh_table, fresh_offset):
    hbm, smem, vmem = (pl.BlockSpec(memory_space=m) for m in (pltpu.HBM, pltpu.SMEM, pltpu.VMEM))
    outs = [SCORES, WITH_ROWS, PACK, ((TAIL, KV * HD), F32)]
    return pl.pallas_call(
        front_body,
        out_shape=[jax.ShapeDtypeStruct(s, d) for s, d in outs],
        in_specs=[hbm] * 5 + [smem] * 4,
        out_specs=[vmem, vmem, hbm, vmem],
        scratch_shapes=[
            pltpu.VMEM((Q, WIDE), F32),
            pltpu.VMEM(PACK[0], F32),
            pltpu.VMEM((Q, WIDE), F32),
            pltpu.VMEM((WIDE, WIDE), F32),
            pltpu.SemaphoreType.DMA((8,)),
        ],
        cost_estimate=pl.CostEstimate(flops=0, bytes_accessed=0, transcendentals=0),
        compiler_params=pltpu.CompilerParams(vmem_limit_bytes=FRONT_MB << 20),
    )(queries, keys, values, grad, w_out, table, offset, fresh_table, fresh_offset)


def joined(mine, other):
    first = lax.axis_index("head") % 2 == 0
    return jnp.concatenate([jnp.where(first, mine, other), jnp.where(first, other, mine)], 0)


def dout_body(mine_ref, other_ref, fresh_ref, stats_ref, high_ref, low_ref, *refs):
    part_ref, g_ref = refs[-2:]
    final = lax.axis_index("section") == lax.axis_size("section") - 1
    g = jnp.where(final, fresh_ref[...], joined(mine_ref[...], other_ref[...]))
    g_ref[...] = g
    part_ref[:Q] = dot3(split(g), (high_ref[...], low_ref[...]), NT)
    part_ref[Q:] = stats_ref[...]


def dout_second(received, fresh, stats, high, low, *after):
    free = range(6, 6 + len(after))
    return call(dout_body, [WITH_ROWS, FULL], *received, fresh, stats, high, low, *after, free=free)


def split_body(w_ref, *refs):
    high_ref, low_ref = refs[-2:]
    high_ref[...], low_ref[...] = split(w_ref[...])


def split_weights(w, *after):
    return call(split_body, [WEIGHT, WEIGHT], w, *after, free=range(1, 1 + len(after)))


def caches_body(k_ref, v_ref, *refs):
    kt_high, kt_low, v_high, v_low = refs[-4:]
    for g in range(KV):
        kt_high[g], kt_low[g] = split(jnp.transpose(k_ref[:, g * HD : (g + 1) * HD]))
    v_high[...], v_low[...] = split(v_ref[...])


def caches(k, v, *after):
    outs = [KEYS_T, KEYS_T, CACHE_BF, CACHE_BF]
    return call(caches_body, outs, k, v, *after, free=range(2, 2 + len(after)))


def second_body(q_ref, pack_ref, k_ref, v_ref, bounds_ref, grad_ref, *refs):
    s_ref, top_ref, kt_high, kt_low, v_high, v_low, copy_ref = refs[-7:]
    final = lax.axis_index("section") == lax.axis_size("section") - 1
    bounds = jnp.where(final, bounds_ref[...], pack_ref[2 * KEYS :])
    top_ref[...] = jnp.full(top_ref.shape, -1e30, F32)
    for g in range(KV):
        cols = slice(g * HD, (g + 1) * HD)
        k = jnp.where(final, k_ref[:, cols], pack_ref[:KEYS, cols])
        top_ref[g : g + 1, :ROWS] = masked_scores(g, q_ref[0, 1], k, bounds, s_ref)
        kt_high[g], kt_low[g] = split(jnp.transpose(k))
    v_high[...], v_low[...] = split(jnp.where(final, v_ref[...], pack_ref[KEYS : 2 * KEYS]))
    copy_ref[...] = grad_ref[...]


def second(queries, pack, k_fresh, v_fresh, bounds, grad, *after):
    outs = [SCORES, STATS, KEYS_T, KEYS_T, CACHE_BF, CACHE_BF, FULL]
    free = range(6, 6 + len(after))
    return call(second_body, outs, queries, pack, k_fresh, v_fresh, bounds, grad, *after, free=free)


def products_body(d0_ref, d1_ref, s_ref, kt_high, kt_low, v_high, v_low, *refs):
    e_ref, dp_ref, a_ref, b_ref, dout_ref = refs[-5:]
    d0, d1 = d0_ref[...], d1_ref[...]
    best = jnp.maximum(d0[Q:], d1[Q:])
    dout = d0[:Q] + d1[:Q]
    dout_ref[...] = dout
    a_ref[Q:] = jnp.zeros((TAIL, WIDE), F32)
    a_groups, b_groups = [], []
    for g in range(KV):
        cols = slice(g * HD, (g + 1) * HD)
        kt = kt_high[g], kt_low[g]
        e = jnp.exp(s_ref[g] - best[g : g + 1, :ROWS])
        e_ref[g] = e
        dp = dot3((v_high[:, cols], v_low[:, cols]), split(stacked(dout, g)), NT)
        dp_ref[g] = dp
        total = jnp.sum(e, axis=0, keepdims=True)
        delta = jnp.sum(e * dp, axis=0, keepdims=True)
        mean = jnp.where(total > 0, delta / total, 0.0)
        b = jnp.transpose(dot3(kt, split(e), NN))
        centred = jnp.transpose(dot3(kt, split(e * (dp - mean)), NN))
        a_groups.append(centred + as_columns(mean) * b)
        b_groups.append(b)
        a_ref[Q + g : Q + g + 1, :ROWS] = delta
        a_ref[Q + KV + g : Q + KV + g + 1, :ROWS] = total
    a_ref[:Q] = spread(a_groups)
    b_ref[...] = spread(b_groups)


def products(dout, s, kt_high, kt_low, v_high, v_low, *after):
    outs = [SCORES, SCORES, WITH_ROWS, FULL, FULL]
    free = range(7, 7 + len(after))
    return call(products_body, outs, *dout, s, kt_high, kt_low, v_high, v_low, *after, free=free)


def input_body(step, a0, a1, b0, b1, g_ref, high_ref, low_ref, *refs):
    head = lax.axis_index("head")
    a_all, b_all = a0[...] + a1[...], b0[...] + b1[...]
    refs[-1][...] = a_all[Q:]
    groups = []
    for g in range(KV):
        total = a_all[Q + KV + g : Q + KV + g + 1, :ROWS]
        delta = a_all[Q + g : Q + g + 1, :ROWS] / total
        a, b = stacked(a_all[:Q], g), stacked(b_all, g)
        groups.append((a - as_columns(delta) * b) * as_columns(SCALE / total))
    part = dot3(split(spread(groups)), (high_ref[...], low_ref[...]), NT)
    part = part + jnp.where(head == 0, g_ref[...], 0.0)
    if step == 1:
        refs[-2][...] = part
        return
    keep_ref, send_ref = refs[-3:-1]
    first = head % 2 == 0
    keep_ref[...] = jnp.where(first, part[:HALF], part[HALF:])
    send_ref[...] = jnp.where(first, part[HALF:], part[:HALF])


def input_gradient(step, a, b, g, high, low, *after):
    outs = [PIECE, PIECE, STATS] if step == 0 else [FULL, STATS]
    return call(functools.partial(input_body, step), outs, *a, *b, g, high, low, *after, free=range(7, 7 + len(after)))


def sums_body(step, row_ref, e_ref, dp_ref, dout_ref, q_ref, *refs):
    if step == 0:
        key_in, value_in, both_out = refs[0].at[0], refs[1].at[0], refs[-1]
        key_out, value_out = both_out.at[:KEYS], both_out.at[KEYS:]
    else:
        key_in, value_in = refs[0].at[:KEYS], refs[0].at[KEYS:]
        key_out, value_out = refs[-2:]
    for g in range(KV):
        total = row_ref[KV + g : KV + g + 1, :ROWS]
        delta = row_ref[g : g + 1, :ROWS] / total
        probs = e_ref[g] * (1.0 / total)
        d_score = probs * (dp_ref[g] - delta)
        cols = slice(g * HD, (g + 1) * HD)
        value_out[:, cols] = value_in[:, cols] + dot3(split(probs), split(stacked(dout_ref[...], g)), NN)
        q = split(stacked(q_ref[0, step], g))
        key_out[:, cols] = key_in[:, cols] + SCALE * dot3(split(d_score), q, NN)


def gradient_sums(step, rows, e, dp, dout, queries, sums, *after):
    outs = [((2 * KEYS, KV * HD), F32)] if step == 0 else [CACHE, CACHE]
    count = 5 + len(sums)
    free = range(count, count + len(after))
    return call(functools.partial(sums_body, step), outs, rows, e, dp, dout, queries, *sums, *after, free=free)


def swap(bits, n=4):
    return [(i, i ^ bits) for i in range(n)]


def neighbours(turn):
    return [(h * 4 + p, h * 4 + (p ^ (1 if (h + turn) % 2 == 0 else 3))) for h in range(4) for p in range(4)]


def page_sum(x, join=jnp.add):
    x = join(x, lax.ppermute(x, ("head", "page"), neighbours(0)))
    return x, lax.ppermute(x, ("head", "page"), neighbours(1))


def sum_and_top(a, b):
    rows = lax.broadcasted_iota(jnp.int32, a.shape, 0)
    return jnp.where(rows < Q, a + b, jnp.maximum(a, b))


def tied(value, after):
    return lax.optimization_barrier((value, after))[0]


def per_device(
    grad_in, grad_fresh, queries, key_cache, value_cache, key_fresh, value_fresh, key_grad_in, value_grad_in,
    page_table, offsets, page_fresh, offset_fresh, w_query, w_out,
):
    back_section = [(i, i - 1) for i in range(1, 16)]

    s1, part, pack, fresh_bounds = front(
        queries, key_cache, value_cache, grad_in, w_out, page_table[0], offsets, page_fresh, offset_fresh
    )
    dout1 = page_sum(part, sum_and_top)
    pack2 = lax.ppermute(pack, "section", back_section)
    split1 = caches(key_cache[0], value_cache[0], dout1[0])
    wq_high, wq_low = split_weights(w_query[0], dout1[0])
    e1, dp1, a, b, dout1 = products(dout1, s1, *split1, wq_high)
    a1, b1 = page_sum(a), page_sum(b)
    wo_high, wo_low = split_weights(w_out[0], a1[0])
    keep, send, rows1 = input_gradient(0, a1, b1, grad_in[0], wq_high, wq_low, wo_high)
    part = keep + lax.ppermute(send, "head", swap(1))
    (sums,) = gradient_sums(0, rows1, e1, dp1, dout1, queries, (key_grad_in, value_grad_in), part)
    part = part + lax.ppermute(part, "head", swap(2))
    mine = lax.ppermute(tied(part, sums), "section", back_section)
    s2, m2, *split2, fresh = second(queries, pack2, key_fresh, value_fresh, fresh_bounds, grad_fresh, part)
    mine = tied(mine, m2)
    other = lax.ppermute(mine, "head", swap(1))

    part, g2 = dout_second((mine, other), fresh, m2, wo_high, wo_low, sums)
    dout2 = page_sum(part, sum_and_top)
    sums = lax.ppermute(tied(sums, part), "section", back_section)
    e2, dp2, a, b, dout2 = products(dout2, s2, *split2)
    a2, b2 = page_sum(a), page_sum(b)
    part, rows2 = input_gradient(1, a2, b2, g2, wq_high, wq_low)
    part = part + lax.ppermute(part, "head", swap(1))
    key_final, value_final = gradient_sums(1, rows2, e2, dp2, dout2, queries, (sums,), part)
    grad_done = part + tied(lax.ppermute(part, "head", swap(2)), key_final)
    return (grad_done[None], key_final[None], value_final[None])


def solution(mesh):
    placed = (
        P("section", None, "page"),
        P(None, "page"),
        P("section", None, None, "head"),
        P("section", "page", "head"),
        P("section", "page", "head"),
        P("page", "head"),
        P("page", "head"),
        P("section", "page", "head"),
        P("section", "page", "head"),
        P("section", None),
        P("section"),
        P(),
        P(),
        P("section", "page", "head"),
        P("section", "head", "page"),
    )
    return jax.shard_map(
        per_device,
        mesh=mesh,
        in_specs=placed,
        out_specs=(
            P("section", None, "page"),
            P("section", "page", "head"),
            P("section", "page", "head"),
        ),
        check_vma=False,
    )
```

time: 144 us -> 108 us (0.75)
  starting transfers between devices: 67.8 us -> 39.2 us
  local copies, waits for them, and re-layouts: 15.3 us -> 0.9 us
  waiting for transfers between devices: 31.4 us -> 44.8 us
  other arithmetic: 4.91 us -> 2 us
  Pallas kernels: 20.7 us -> 18.8 us
    ppermute x38 -> x18, starting transfers between devices: 67.4 us -> 39.1 us  [the longest x6 12.2 us: page_sum(): return (x, lax.ppermute(x, ('head', 'page'), neighbours(1)))]
    unnamed x84 -> x26, local copies, waits for them, and re-layouts: 14.6 us -> 0.9 us
    ppermute x38 -> x18, waiting for transfers between devices: 28.8 us -> 42.2 us  [the longest x6 17.8 us: page_sum(): x = join(x, lax.ppermute(x, ('head', 'page'), neighbours(0)))]
    pallas_call x11, Pallas kernels: 18.6 us -> 12.2 us  [call(): pl.pallas_call(body, out_shape=[jax.ShapeDtypeStruct(s, d) for s, d in ou...]
    pallas_call x2 -> x1, Pallas kernels: 2.06 us -> 6.65 us  [front(): pl.pallas_call(front_body, out_shape=[jax.ShapeDtypeStruct(s, d) for s, d...]
  transfers between devices with their start and end apart: 42 -> 20, of which waited for: 15 -> 14; matrix products, arithmetic and copies ran while one was open for 3% -> 1% of each run, Pallas kernels for 13% -> 10%
where the time goes in v2:
time: 108 us
  waiting for transfers between devices  44.8 us (41%)
  starting transfers between devices  39.2 us (36%)
  Pallas kernels  18.8 us (17%)
  between operations  2.26 us (2%)
  other arithmetic  2 us (2%)
    ppermute x6, waiting for transfers between devices, page_sum(): x = join(x, lax.ppermute(x, ('head', 'page'), neighbours(0)))  17.8 us
    ppermute x6, waiting for transfers between devices, page_sum(): return (x, lax.ppermute(x, ('head', 'page'), neighbours(1)))  13.7 us
    ppermute x6, starting transfers between devices, page_sum(): return (x, lax.ppermute(x, ('head', 'page'), neighbours(1)))  12.2 us
    pallas_call x11, Pallas kernels, call(): pl.pallas_call(body, out_shape=[jax.ShapeDtypeStruct(s, d) for s, d in ou...  12.2 us
    ppermute x1, starting transfers between devices, per_device(): pack2 = lax.ppermute(pack, 'section', back_section)  8.42 us
    ppermute x1, starting transfers between devices, per_device(): sums = lax.ppermute(tied(sums, part), 'section', back_section)  7.64 us
    pallas_call x1, Pallas kernels, front(): pl.pallas_call(front_body, out_shape=[jax.ShapeDtypeStruct(s, d) for s, d...  6.65 us
    ppermute x6, starting transfers between devices, page_sum(): x = join(x, lax.ppermute(x, ('head', 'page'), neighbours(0)))  5.87 us
  transfers between devices with their start and end apart: 20, of which 14 were waited for; matrix products, arithmetic and copies ran while one was open for 1% of the time, Pallas kernels for 10%

profile of v2, /device:TPU:24, one launch (start us, length us, event | category | flops | bytes accessed | tf_op | source)
XLA Modules:
  0.0 108.0 jit_solution(7736258237125392979)
XLA Ops:
  1.9 6.7 %shard_map.166 = (f32[2,512,192]{2,1,0:T(8,128)}, f32[72,768]{1,0:T(8,128)}, f32[1032,256]{1,0:T(8,128)}, f32[8,256]{1,0:T(8,128)}) custom-call(f32[1,2,64,768]{3,2,1,0:T(8,128)} %q_ref.5, f32[1,512,256]{2,1,0:T(8,128)} %k_hbm.1, f32[1,512,256]{2,1,0:T(8,128)} %v_hbm.1, f32[1,64,768]{2,1,0:T(8,128)} %g_hbm.1, f32[1,768,768]{2,1,0:T(8,128)} %w_hbm.1, ...), custom_call_target="tpu_custom_call" | custom-call | tf_op jit(solution)/shard_map/pallas_call | solution.py:147
  8.6 1.6 %collective-permute-start = (f32[72,768]{1,0:T(8,128)}, f32[72,768]{1,0:T(8,128)S(1)}, u32[]{:S(2)}, u32[]{:S(2)}) collective-permute-start(f32[72,768]{1,0:T(8,128)} %get-tuple-element.45), channel_id=1, source_target_pairs={{0,1},{1,0},{2,3},{3,2},{4,7},{5,6},{6,5},{7,4},{8,9},{9,8},{10,11... | collective-permute-start | bytes 663560 | tf_op jit(solution)/shard_map/ppermute | solution.py:318
  10.2 8.4 %collective-permute-start.9 = (f32[1032,256]{1,0:T(8,128)}, f32[1032,256]{1,0:T(8,128)S(1)}, u32[]{:S(2)}, u32[]{:S(2)}) collective-permute-start(f32[1032,256]{1,0:T(8,128)} %get-tuple-element.63), channel_id=1, source_target_pairs={{16,0},{32,16},{48,32},{64,48},{80,64},{96,80},{112,96},{128,112},... | collective-permute-start | bytes 3170312 | tf_op jit(solution)/shard_map/ppermute | solution.py:341
  18.6 1.0 maximum_select_fusion.1.refs_0_.d0_ref
  19.7 2.2 %collective-permute-start.1 = (f32[72,768]{1,0:T(8,128)S(1)}, f32[72,768]{1,0:T(8,128)S(1)}, u32[]{:S(2)}, u32[]{:S(2)}) collective-permute-start(f32[72,768]{1,0:T(8,128)S(1)} %maximum_select_fusion.1.refs_0_.d0_ref), channel_id=1, source_target_pairs={{0,3},{1,2},{2,1},{3,0},{4,5},{5,4},{6,7},{7,6},{8,11},{9,10},{10,... | collective-permute-start | bytes 663560 | tf_op jit(solution)/shard_map/ppermute | solution.py:319
  23.3 3.5 %collective-permute-done.1.d1_ref = f32[72,768]{1,0:T(8,128)S(1)} collective-permute-done((f32[72,768]{1,0:T(8,128)S(1)}, f32[72,768]{1,0:T(8,128)S(1)}, u32[]{:S(2)}, u32[]{:S(2)}) %collective-permute-start.1) | collective-permute-done | bytes 221216 | tf_op jit(solution)/shard_map/ppermute | solution.py:319
  26.9 1.6 %shard_map.169 = (f32[2,512,192]{2,1,0:T(8,128)S(1)}, f32[2,512,192]{2,1,0:T(8,128)S(1)}, f32[72,768]{1,0:T(8,128)S(1)}, f32[64,768]{1,0:T(8,128)S(1)}, f32[64,768]{1,0:T(8,128)S(1)}) custom-call(f32[72,768]{1,0:T(8,128)S(1)} %maximum_select_fusion.1.refs_0_.d0_ref, f32[72,768]{1,0:T(8,128)S(1)} %collective-permute-done.1.d1_ref, ...), custom_call_target="tpu_custom_call" | custom-call | tf_op jit(solution)/shard_map/pallas_call | solution.py:56
  28.6 2.0 %collective-permute-start.4 = (f32[64,768]{1,0:T(8,128)S(1)}, f32[64,768]{1,0:T(8,128)S(1)}, u32[]{:S(2)}, u32[]{:S(2)}) collective-permute-start(f32[64,768]{1,0:T(8,128)S(1)} %get-tuple-element.53), channel_id=1, source_target_pairs={{0,1},{1,0},{2,3},{3,2},{4,7},{5,6},{6,5},{7,4},{8,9},{9,8},{10,11... | collective-permute-start | bytes 589832 | tf_op jit(solution)/shard_map/ppermute | solution.py:318
  30.7 3.9 %collective-permute-done.2 = f32[72,768]{1,0:T(8,128)S(1)} collective-permute-done((f32[72,768]{1,0:T(8,128)S(1)}, f32[72,768]{1,0:T(8,128)S(1)}, u32[]{:S(2)}, u32[]{:S(2)}) %collective-permute-start.2) | collective-permute-done | bytes 221216 | tf_op jit(solution)/shard_map/ppermute | solution.py:318
  34.6 2.5 %collective-permute-start.3 = (f32[72,768]{1,0:T(8,128)S(1)}, f32[72,768]{1,0:T(8,128)S(1)}, u32[]{:S(2)}, u32[]{:S(2)}) collective-permute-start(f32[72,768]{1,0:T(8,128)S(1)} %add.31.refs_0_.a0), channel_id=1, source_target_pairs={{0,3},{1,2},{2,1},{3,0},{4,5},{5,4},{6,7},{7,6},{8,11},{9,10},{10,... | collective-permute-start | bytes 663560 | tf_op jit(solution)/shard_map/ppermute | solution.py:319
  37.5 3.8 %collective-permute-start.5 = (f32[64,768]{1,0:T(8,128)S(1)}, f32[64,768]{1,0:T(8,128)S(1)}, u32[]{:S(2)}, u32[]{:S(2)}) collective-permute-start(f32[64,768]{1,0:T(8,128)S(1)} %add.32.b0), channel_id=1, source_target_pairs={{0,3},{1,2},{2,1},{3,0},{4,5},{5,4},{6,7},{7,6},{8,11},{9,10},{10,... | collective-permute-start | bytes 589832 | tf_op jit(solution)/shard_map/ppermute | solution.py:319
  41.7 3.2 %collective-permute-done.5.b1 = f32[64,768]{1,0:T(8,128)S(1)} collective-permute-done((f32[64,768]{1,0:T(8,128)S(1)}, f32[64,768]{1,0:T(8,128)S(1)}, u32[]{:S(2)}, u32[]{:S(2)}) %collective-permute-start.5) | collective-permute-done | bytes 196640 | tf_op jit(solution)/shard_map/ppermute | solution.py:319
  45.0 1.2 %shard_map.171 = (f32[32,768]{1,0:T(8,128)S(1)}, f32[32,768]{1,0:T(8,128)S(1)}, f32[8,768]{1,0:T(8,128)S(1)}) custom-call(f32[72,768]{1,0:T(8,128)S(1)} %add.31.refs_0_.a0, f32[72,768]{1,0:T(8,128)S(1)} %collective-permute-done.3.a1, f32[64,768]{1,0:T(8,128)S(1)} %add.32.b0, f32[64,768]{1,0:T(8,128)S(1)} %collective-permute-done.5.b1, ...), custom_call_target="tpu_custom_call" | custom-call | tf_op jit(solution)/shard_map/pallas_call | solution.py:56
  46.2 1.3 %collective-permute-done.6 = f32[32,768]{1,0:T(8,128)S(1)} collective-permute-done((f32[32,768]{1,0:T(8,128)S(1)}, f32[32,768]{1,0:T(8,128)S(1)}, u32[]{:S(2)}, u32[]{:S(2)}) %collective-permute-start.6) | collective-permute-done | bytes 98336 | tf_op jit(solution)/shard_map/ppermute | solution.py:348
  47.7 1.0 shard_map.172.refs_0_
  48.7 3.7 %collective-permute-done.7 = f32[32,768]{1,0:T(8,128)S(1)} collective-permute-done((f32[32,768]{1,0:T(8,128)S(1)}, f32[32,768]{1,0:T(8,128)S(1)}, u32[]{:S(2)}, u32[]{:S(2)}) %collective-permute-start.7) | collective-permute-done | bytes 98336 | tf_op jit(solution)/shard_map/ppermute | solution.py:350
  52.5 4.7 %collective-permute-start.8 = (f32[32,768]{1,0:T(8,128)S(1)}, f32[32,768]{1,0:T(8,128)S(1)}, u32[]{:S(2)}, u32[]{:S(2)}) collective-permute-start(f32[32,768]{1,0:T(8,128)S(1)} %add.34.refs_0_), channel_id=1, source_target_pairs={{16,0},{32,16},{48,32},{64,48},{80,64},{96,80},{112,96},{128,112},... | collective-permute-start | bytes 294920 | tf_op jit(solution)/shard_map/ppermute | solution.py:351
  57.2 1.2 %shard_map.173 = (f32[2,512,192]{2,1,0:T(8,128)S(1)}, f32[8,768]{1,0:T(8,128)S(1)}, bf16[2,128,512]{2,1,0:T(8,128)(2,1)S(1)}, bf16[2,128,512]{2,1,0:T(8,128)(2,1...) custom-call(f32[1,2,64,768]{3,2,1,0:T(8,128)S(1)} %copy-done.1, ...), custom_call_target="tpu_custom_call" | custom-call | tf_op jit(solution)/shard_map/pallas_call | solution.py:56
  59.2 1.3 %collective-permute-done.10.other_ref = f32[32,768]{1,0:T(8,128)S(1)} collective-permute-done((f32[32,768]{1,0:T(8,128)S(1)}, f32[32,768]{1,0:T(8,128)S(1)}, u32[]{:S(2)}, u32[]{:S(2)}) %collective-permute-start.10) | collective-permute-done | bytes 98336 | tf_op jit(solution)/shard_map/ppermute | solution.py:354
  60.5 1.2 %shard_map.174 = (f32[72,768]{1,0:T(8,128)S(1)}, f32[64,768]{1,0:T(8,128)S(1)}) custom-call(f32[32,768]{1,0:T(8,128)S(1)} %collective-permute-done.8.mine_ref, f32[32,768]{1,0:T(8,128)S(1)} %collective-permute-done.10.other_ref, f32[64,768]{1,0:T(8,128)S(1)} %get-tuple-element.67.fresh_ref, f32[8,768]{1,0:T(8,128)S(1)} %get-tuple-element.65.stats_ref, ...), custom_call_target="tpu_custom_call" | custom-call | tf_op jit(solution)/shard_map/pallas_call | solution.py:56
  61.8 5.9 %collective-permute-done.11 = f32[72,768]{1,0:T(8,128)S(1)} collective-permute-done((f32[72,768]{1,0:T(8,128)S(1)}, f32[72,768]{1,0:T(8,128)S(1)}, u32[]{:S(2)}, u32[]{:S(2)}) %collective-permute-start.11) | collective-permute-done | bytes 221216 | tf_op jit(solution)/shard_map/ppermute | solution.py:318
  67.8 3.1 %collective-permute-start.12 = (f32[72,768]{1,0:T(8,128)S(1)}, f32[72,768]{1,0:T(8,128)S(1)}, u32[]{:S(2)}, u32[]{:S(2)}) collective-permute-start(f32[72,768]{1,0:T(8,128)S(1)} %maximum_select_fusion.d0_ref), channel_id=1, source_target_pairs={{0,3},{1,2},{2,1},{3,0},{4,5},{5,4},{6,7},{7,6},{8,11},{9,10},{10,... | collective-permute-start | bytes 663560 | tf_op jit(solution)/shard_map/ppermute | solution.py:319
  70.9 7.6 %collective-permute-start.19 = (f32[1024,256]{1,0:T(8,128)S(1)}, f32[1024,256]{1,0:T(8,128)S(1)}, u32[]{:S(2)}, u32[]{:S(2)}) collective-permute-start(f32[1024,256]{1,0:T(8,128)S(1)} %shard_map.172.refs_0_), channel_id=1, source_target_pairs={{16,0},{32,16},{48,32},{64,48},{80,64},{96,80},{112,96},{128,112},... | collective-permute-start | bytes 3145736 | tf_op jit(solution)/shard_map/ppermute | solution.py:358
  78.6 1.7 %shard_map.175 = (f32[2,512,192]{2,1,0:T(8,128)S(1)}, f32[2,512,192]{2,1,0:T(8,128)S(1)}, f32[72,768]{1,0:T(8,128)S(1)}, f32[64,768]{1,0:T(8,128)S(1)}, f32[64,768]{1,0:T(8,128)S(1)}) custom-call(f32[72,768]{1,0:T(8,128)S(1)} %maximum_select_fusion.d0_ref, f32[72,768]{1,0:T(8,128)S(1)} %collective-permute-done.12.d1_ref, ...), custom_call_target="tpu_custom_call" | custom-call | tf_op jit(solution)/shard_map/pallas_call | solution.py:56
  80.4 2.0 %collective-permute-start.15 = (f32[64,768]{1,0:T(8,128)S(1)}, f32[64,768]{1,0:T(8,128)S(1)}, u32[]{:S(2)}, u32[]{:S(2)}) collective-permute-start(f32[64,768]{1,0:T(8,128)S(1)} %get-tuple-element.76), channel_id=1, source_target_pairs={{0,1},{1,0},{2,3},{3,2},{4,7},{5,6},{6,5},{7,4},{8,9},{9,8},{10,11... | collective-permute-start | bytes 589832 | tf_op jit(solution)/shard_map/ppermute | solution.py:318
  82.4 3.9 %collective-permute-done.13 = f32[72,768]{1,0:T(8,128)S(1)} collective-permute-done((f32[72,768]{1,0:T(8,128)S(1)}, f32[72,768]{1,0:T(8,128)S(1)}, u32[]{:S(2)}, u32[]{:S(2)}) %collective-permute-start.13) | collective-permute-done | bytes 221216 | tf_op jit(solution)/shard_map/ppermute | solution.py:318
  86.9 3.6 %collective-permute-done.15 = f32[64,768]{1,0:T(8,128)S(1)} collective-permute-done((f32[64,768]{1,0:T(8,128)S(1)}, f32[64,768]{1,0:T(8,128)S(1)}, u32[]{:S(2)}, u32[]{:S(2)}) %collective-permute-start.15) | collective-permute-done | bytes 196640 | tf_op jit(solution)/shard_map/ppermute | solution.py:318
  90.6 6.9 %collective-permute-done.16.b1 = f32[64,768]{1,0:T(8,128)S(1)} collective-permute-done((f32[64,768]{1,0:T(8,128)S(1)}, f32[64,768]{1,0:T(8,128)S(1)}, u32[]{:S(2)}, u32[]{:S(2)}) %collective-permute-start.16) | collective-permute-done | bytes 196640 | tf_op jit(solution)/shard_map/ppermute | solution.py:319
  97.5 1.2 %shard_map.176 = (f32[64,768]{1,0:T(8,128)S(1)}, f32[8,768]{1,0:T(8,128)S(1)}) custom-call(f32[72,768]{1,0:T(8,128)S(1)} %add.36.a0, f32[72,768]{1,0:T(8,128)S(1)} %collective-permute-done.14.a1, f32[64,768]{1,0:T(8,128)S(1)} %add.37.b0, f32[64,768]{1,0:T(8,128)S(1)} %collective-permute-done.16.b1, f32[64,768]{1,0:T(8,128)S(1)} %get-tuple-element.77.g_ref, ...), custom_call_target="tpu_custom_call" | custom-call | tf_op jit(solution)/shard_map/pallas_call | solution.py:56
  98.8 1.4 %collective-permute-done.17 = f32[64,768]{1,0:T(8,128)S(1)} collective-permute-done((f32[64,768]{1,0:T(8,128)S(1)}, f32[64,768]{1,0:T(8,128)S(1)}, u32[]{:S(2)}, u32[]{:S(2)}) %collective-permute-start.17) | collective-permute-done | bytes 196640 | tf_op jit(solution)/shard_map/ppermute | solution.py:362
  100.4 2.0 %shard_map.177 = (f32[512,256]{1,0:T(8,128)}, f32[512,256]{1,0:T(8,128)}) custom-call(f32[8,768]{1,0:T(8,128)S(1)} %get-tuple-element.79.row_ref, f32[2,512,192]{2,1,0:T(8,128)S(1)} %get-tuple-element.80.e_ref, f32[2,512,192]{2,1,0:T(8,128)S(1)} %get-tuple-element.81.dp_ref, f32[64,768]{1,0:T(8,128)S(1)} %get-tuple-element.82.dout_ref, ...), custom_call_target="tpu_custom_call" | custom-call | tf_op jit(solution)/shard_map/pallas_call | solution.py:56
  102.3 4.9 %collective-permute-done.18 = f32[64,768]{1,0:T(8,128)S(1)} collective-permute-done((f32[64,768]{1,0:T(8,128)S(1)}, f32[64,768]{1,0:T(8,128)S(1)}, u32[]{:S(2)}, u32[]{:S(2)}) %collective-permute-start.18) | collective-permute-done | bytes 196640 | tf_op jit(solution)/shard_map/ppermute | solution.py:364
  (57 shorter events, 5.3 us)
Async XLA Ops:
  1.9 19.9 %copy-start.2 = (f32[1,768,768]{2,1,0:T(8,128)S(1)}, f32[1,768,768]{2,1,0:T(8,128)}, u32[]{:S(2)}) copy-start(f32[1,768,768]{2,1,0:T(8,128)} %param.28) | copy-start | bytes 7077892
  8.6 10.0 %collective-permute-start = (f32[72,768]{1,0:T(8,128)}, f32[72,768]{1,0:T(8,128)S(1)}, u32[]{:S(2)}, u32[]{:S(2)}) collective-permute-start(f32[72,768]{1,0:T(8,128)} %get-tuple-element.45), channel_id=1, source_target_pairs={{0,1},{1,0},{2,3},{3,2},{4,7},{5,6},{6,5},{7,4},{8,9},{9,8},{10,11... | collective-permute-start | bytes 663560 | tf_op jit(solution)/shard_map/ppermute | solution.py:318
  10.2 47.0 %collective-permute-start.9 = (f32[1032,256]{1,0:T(8,128)}, f32[1032,256]{1,0:T(8,128)S(1)}, u32[]{:S(2)}, u32[]{:S(2)}) collective-permute-start(f32[1032,256]{1,0:T(8,128)} %get-tuple-element.63), channel_id=1, source_target_pairs={{16,0},{32,16},{48,32},{64,48},{80,64},{96,80},{112,96},{128,112},... | collective-permute-start | bytes 3170312 | tf_op jit(solution)/shard_map/ppermute | solution.py:341
  19.7 7.2 %collective-permute-start.1 = (f32[72,768]{1,0:T(8,128)S(1)}, f32[72,768]{1,0:T(8,128)S(1)}, u32[]{:S(2)}, u32[]{:S(2)}) collective-permute-start(f32[72,768]{1,0:T(8,128)S(1)} %maximum_select_fusion.1.refs_0_.d0_ref), channel_id=1, source_target_pairs={{0,3},{1,2},{2,1},{3,0},{4,5},{5,4},{6,7},{7,6},{8,11},{9,10},{10,... | collective-permute-start | bytes 663560 | tf_op jit(solution)/shard_map/ppermute | solution.py:319
  21.8 1.2 %copy-start.4 = (f32[1,512,256]{2,1,0:T(8,128)S(1)}, f32[1,512,256]{2,1,0:T(8,128)}, u32[]{:S(2)}) copy-start(f32[1,512,256]{2,1,0:T(8,128)} %v_hbm.1) | copy-start | bytes 1572868
  22.2 4.7 %copy-start.5 = (f32[2,512,192]{2,1,0:T(8,128)S(1)}, f32[2,512,192]{2,1,0:T(8,128)}, u32[]{:S(2)}) copy-start(f32[2,512,192]{2,1,0:T(8,128)} %get-tuple-element.46.s_ref) | copy-start | bytes 2359300
  26.9 14.4 %copy-start = (f32[1,768,768]{2,1,0:T(8,128)S(1)}, f32[1,768,768]{2,1,0:T(8,128)}, u32[]{:S(2)}) copy-start(f32[1,768,768]{2,1,0:T(8,128)} %w_hbm.1) | copy-start | bytes 7077892
  28.5 6.0 %collective-permute-start.2 = (f32[72,768]{1,0:T(8,128)S(1)}, f32[72,768]{1,0:T(8,128)S(1)}, u32[]{:S(2)}, u32[]{:S(2)}) collective-permute-start(f32[72,768]{1,0:T(8,128)S(1)} %get-tuple-element.52), channel_id=1, source_target_pairs={{0,1},{1,0},{2,3},{3,2},{4,7},{5,6},{6,5},{7,4},{8,9},{9,8},{10,11... | collective-permute-start | bytes 663560 | tf_op jit(solution)/shard_map/ppermute | solution.py:318
  28.6 8.8 %collective-permute-start.4 = (f32[64,768]{1,0:T(8,128)S(1)}, f32[64,768]{1,0:T(8,128)S(1)}, u32[]{:S(2)}, u32[]{:S(2)}) collective-permute-start(f32[64,768]{1,0:T(8,128)S(1)} %get-tuple-element.53), channel_id=1, source_target_pairs={{0,1},{1,0},{2,3},{3,2},{4,7},{5,6},{6,5},{7,4},{8,9},{9,8},{10,11... | collective-permute-start | bytes 589832 | tf_op jit(solution)/shard_map/ppermute | solution.py:318
  34.6 10.3 %collective-permute-start.3 = (f32[72,768]{1,0:T(8,128)S(1)}, f32[72,768]{1,0:T(8,128)S(1)}, u32[]{:S(2)}, u32[]{:S(2)}) collective-permute-start(f32[72,768]{1,0:T(8,128)S(1)} %add.31.refs_0_.a0), channel_id=1, source_target_pairs={{0,3},{1,2},{2,1},{3,0},{4,5},{5,4},{6,7},{7,6},{8,11},{9,10},{10,... | collective-permute-start | bytes 663560 | tf_op jit(solution)/shard_map/ppermute | solution.py:319
  37.5 7.4 %collective-permute-start.5 = (f32[64,768]{1,0:T(8,128)S(1)}, f32[64,768]{1,0:T(8,128)S(1)}, u32[]{:S(2)}, u32[]{:S(2)}) collective-permute-start(f32[64,768]{1,0:T(8,128)S(1)} %add.32.b0), channel_id=1, source_target_pairs={{0,3},{1,2},{2,1},{3,0},{4,5},{5,4},{6,7},{7,6},{8,11},{9,10},{10,... | collective-permute-start | bytes 589832 | tf_op jit(solution)/shard_map/ppermute | solution.py:319
  41.3 3.7 %copy-start.6 = (f32[1,64,768]{2,1,0:T(8,128)S(1)}, f32[1,64,768]{2,1,0:T(8,128)}, u32[]{:S(2)}) copy-start(f32[1,64,768]{2,1,0:T(8,128)} %g_hbm.1) | copy-start | bytes 589828
  44.9 2.7 %copy-start.1 = (f32[1,2,64,768]{3,2,1,0:T(8,128)S(1)}, f32[1,2,64,768]{3,2,1,0:T(8,128)}, u32[]{:S(2)}) copy-start(f32[1,2,64,768]{3,2,1,0:T(8,128)} %q_ref.5) | copy-start | bytes 1179652
  44.9 2.7 %copy-start.7 = (f32[1,512,256]{2,1,0:T(8,128)S(1)}, f32[1,512,256]{2,1,0:T(8,128)}, u32[]{:S(2)}) copy-start(f32[1,512,256]{2,1,0:T(8,128)} %refs_0_.1) | copy-start | bytes 1572868
  44.9 2.7 %copy-start.8 = (f32[1,512,256]{2,1,0:T(8,128)S(1)}, f32[1,512,256]{2,1,0:T(8,128)}, u32[]{:S(2)}) copy-start(f32[1,512,256]{2,1,0:T(8,128)} %refs_1_.1) | copy-start | bytes 1572868
  46.1 1.4 %collective-permute-start.6 = (f32[32,768]{1,0:T(8,128)S(1)}, f32[32,768]{1,0:T(8,128)S(1)}, u32[]{:S(2)}, u32[]{:S(2)}) collective-permute-start(f32[32,768]{1,0:T(8,128)S(1)} %get-tuple-element.57), channel_id=1, source_target_pairs={{0,4},{4,0},{8,12},{12,8},{1,5},{5,1},{9,13},{13,9},{2,6},{6,2},{1... | collective-permute-start | bytes 294920 | tf_op jit(solution)/shard_map/ppermute | solution.py:348
  47.6 4.9 %collective-permute-start.7 = (f32[32,768]{1,0:T(8,128)S(1)}, f32[32,768]{1,0:T(8,128)S(1)}, u32[]{:S(2)}, u32[]{:S(2)}) collective-permute-start(f32[32,768]{1,0:T(8,128)S(1)} %add.33.refs_2_), channel_id=1, source_target_pairs={{0,8},{4,12},{8,0},{12,4},{1,9},{5,13},{9,1},{13,5},{2,10},{6,14},... | collective-permute-start | bytes 294920 | tf_op jit(solution)/shard_map/ppermute | solution.py:350
  47.7 9.5 %copy-start.9 = (f32[512,256]{1,0:T(8,128)S(1)}, f32[512,256]{1,0:T(8,128)}, u32[]{:S(2)}) copy-start(f32[512,256]{1,0:T(8,128)} %k_ref.1) | copy-start | bytes 1572868
  47.7 9.5 %copy-start.10 = (f32[512,256]{1,0:T(8,128)S(1)}, f32[512,256]{1,0:T(8,128)}, u32[]{:S(2)}) copy-start(f32[512,256]{1,0:T(8,128)} %v_ref.1) | copy-start | bytes 1572868
  47.7 9.5 %copy-start.11 = (f32[64,768]{1,0:T(8,128)S(1)}, f32[64,768]{1,0:T(8,128)}, u32[]{:S(2)}) copy-start(f32[64,768]{1,0:T(8,128)} %grad_ref.1) | copy-start | bytes 589828
  47.7 9.5 %copy-start.12 = (f32[8,256]{1,0:T(8,128)S(1)}, f32[8,256]{1,0:T(8,128)}, u32[]{:S(2)}) copy-start(f32[8,256]{1,0:T(8,128)} %get-tuple-element.64.bounds_ref) | copy-start | bytes 24580
  52.5 6.7 %collective-permute-start.8 = (f32[32,768]{1,0:T(8,128)S(1)}, f32[32,768]{1,0:T(8,128)S(1)}, u32[]{:S(2)}, u32[]{:S(2)}) collective-permute-start(f32[32,768]{1,0:T(8,128)S(1)} %add.34.refs_0_), channel_id=1, source_target_pairs={{16,0},{32,16},{48,32},{64,48},{80,64},{96,80},{112,96},{128,112},... | collective-permute-start | bytes 294920 | tf_op jit(solution)/shard_map/ppermute | solution.py:351
  59.2 1.3 %collective-permute-start.10 = (f32[32,768]{1,0:T(8,128)S(1)}, f32[32,768]{1,0:T(8,128)S(1)}, u32[]{:S(2)}, u32[]{:S(2)}) collective-permute-start(f32[32,768]{1,0:T(8,128)S(1)} %collective-permute-done.8.mine_ref), channel_id=1, source_target_pairs={{0,4},{4,0},{8,12},{12,8},{1,5},{5,1},{9,13},{13,9},{2,6},{6,2},{1... | collective-permute-start | bytes 294920 | tf_op jit(solution)/shard_map/ppermute | solution.py:354
  61.7 6.0 %collective-permute-start.11 = (f32[72,768]{1,0:T(8,128)S(1)}, f32[72,768]{1,0:T(8,128)S(1)}, u32[]{:S(2)}, u32[]{:S(2)}) collective-permute-start(f32[72,768]{1,0:T(8,128)S(1)} %get-tuple-element.69), channel_id=1, source_target_pairs={{0,1},{1,0},{2,3},{3,2},{4,7},{5,6},{6,5},{7,4},{8,9},{9,8},{10,11... | collective-permute-start | bytes 663560 | tf_op jit(solution)/shard_map/ppermute | solution.py:318
  67.8 10.8 %collective-permute-start.12 = (f32[72,768]{1,0:T(8,128)S(1)}, f32[72,768]{1,0:T(8,128)S(1)}, u32[]{:S(2)}, u32[]{:S(2)}) collective-permute-start(f32[72,768]{1,0:T(8,128)S(1)} %maximum_select_fusion.d0_ref), channel_id=1, source_target_pairs={{0,3},{1,2},{2,1},{3,0},{4,5},{5,4},{6,7},{7,6},{8,11},{9,10},{10,... | collective-permute-start | bytes 663560 | tf_op jit(solution)/shard_map/ppermute | solution.py:319
  70.9 29.4 %collective-permute-start.19 = (f32[1024,256]{1,0:T(8,128)S(1)}, f32[1024,256]{1,0:T(8,128)S(1)}, u32[]{:S(2)}, u32[]{:S(2)}) collective-permute-start(f32[1024,256]{1,0:T(8,128)S(1)} %shard_map.172.refs_0_), channel_id=1, source_target_pairs={{16,0},{32,16},{48,32},{64,48},{80,64},{96,80},{112,96},{128,112},... | collective-permute-start | bytes 3145736 | tf_op jit(solution)/shard_map/ppermute | solution.py:358
  80.3 6.0 %collective-permute-start.13 = (f32[72,768]{1,0:T(8,128)S(1)}, f32[72,768]{1,0:T(8,128)S(1)}, u32[]{:S(2)}, u32[]{:S(2)}) collective-permute-start(f32[72,768]{1,0:T(8,128)S(1)} %get-tuple-element.75), channel_id=1, source_target_pairs={{0,1},{1,0},{2,3},{3,2},{4,7},{5,6},{6,5},{7,4},{8,9},{9,8},{10,11... | collective-permute-start | bytes 663560 | tf_op jit(solution)/shard_map/ppermute | solution.py:318
  80.4 10.1 %collective-permute-start.15 = (f32[64,768]{1,0:T(8,128)S(1)}, f32[64,768]{1,0:T(8,128)S(1)}, u32[]{:S(2)}, u32[]{:S(2)}) collective-permute-start(f32[64,768]{1,0:T(8,128)S(1)} %get-tuple-element.76), channel_id=1, source_target_pairs={{0,1},{1,0},{2,3},{3,2},{4,7},{5,6},{6,5},{7,4},{8,9},{9,8},{10,11... | collective-permute-start | bytes 589832 | tf_op jit(solution)/shard_map/ppermute | solution.py:318
  86.3 11.2 %collective-permute-start.14 = (f32[72,768]{1,0:T(8,128)S(1)}, f32[72,768]{1,0:T(8,128)S(1)}, u32[]{:S(2)}, u32[]{:S(2)}) collective-permute-start(f32[72,768]{1,0:T(8,128)S(1)} %add.36.a0), channel_id=1, source_target_pairs={{0,3},{1,2},{2,1},{3,0},{4,5},{5,4},{6,7},{7,6},{8,11},{9,10},{10,... | collective-permute-start | bytes 663560 | tf_op jit(solution)/shard_map/ppermute | solution.py:319
  90.5 7.0 %collective-permute-start.16 = (f32[64,768]{1,0:T(8,128)S(1)}, f32[64,768]{1,0:T(8,128)S(1)}, u32[]{:S(2)}, u32[]{:S(2)}) collective-permute-start(f32[64,768]{1,0:T(8,128)S(1)} %add.37.b0), channel_id=1, source_target_pairs={{0,3},{1,2},{2,1},{3,0},{4,5},{5,4},{6,7},{7,6},{8,11},{9,10},{10,... | collective-permute-start | bytes 589832 | tf_op jit(solution)/shard_map/ppermute | solution.py:319
  98.7 1.5 %collective-permute-start.17 = (f32[64,768]{1,0:T(8,128)S(1)}, f32[64,768]{1,0:T(8,128)S(1)}, u32[]{:S(2)}, u32[]{:S(2)}) collective-permute-start(f32[64,768]{1,0:T(8,128)S(1)} %get-tuple-element.78), channel_id=1, source_target_pairs={{0,4},{4,0},{8,12},{12,8},{1,5},{5,1},{9,13},{13,9},{2,6},{6,2},{1... | collective-permute-start | bytes 589832 | tf_op jit(solution)/shard_map/ppermute | solution.py:362
  100.3 7.0 %collective-permute-start.18 = (f32[64,768]{1,0:T(8,128)S(1)}, f32[64,768]{1,0:T(8,128)S(1)}, u32[]{:S(2)}, u32[]{:S(2)}) collective-permute-start(f32[64,768]{1,0:T(8,128)S(1)} %add.38.refs_1_), channel_id=1, source_target_pairs={{0,8},{4,12},{8,0},{12,4},{1,9},{5,13},{9,1},{13,5},{2,10},{6,14},... | collective-permute-start | bytes 589832 | tf_op jit(solution)/shard_map/ppermute | solution.py:364
  (1 other events, 1.0 us)

commit v3 on v2

--- a/solution.py
+++ b/solution.py
@@ -39,6 +39,19 @@
     return dot(a_high, b_high, dims) + (dot(a_low, b_high, dims) + dot(a_high, b_low, dims))
 
 
+def dot3_few(a, b, dims):
+    (a_high, a_low), (b_high, b_low) = a, b
+    rows = a_high.shape[0]
+    both = dot(jnp.concatenate([a_high, a_low], 0), b_high, dims)
+    return both[:rows] + (both[rows:] + dot(a_high, b_low, dims))
+
+
+def key_sum(kt, x):
+    high, low = split(x)
+    both = dot(kt, high, NN)
+    return both[:HD] + (both[HD:] + dot(kt[:HD], low, NN))
+
+
 def stacked(x, g):
     return jnp.concatenate([x[:, (g * GROUP + r) * HD : (g * GROUP + r + 1) * HD] for r in range(GROUP)], 0)
 
@@ -72,8 +85,8 @@
 STATS = ((TAIL, WIDE), F32)
 PACK = ((2 * KEYS + TAIL, KV * HD), F32)
 WEIGHT = ((WIDE, WIDE), BF16)
-KEYS_T = ((KV, HD, KEYS), BF16)
-CACHE_BF = ((KEYS, KV * HD), BF16)
+KEYS_T = ((KV, 2 * HD, KEYS), BF16)
+VALUES = ((KEYS, 2 * KV * HD), BF16)
 
 
 def limits(table_ref, offset_ref):
@@ -113,12 +126,12 @@
         pltpu.make_async_copy(k_hbm.at[0], pack_ref.at[pl.ds(0, KEYS)], sems.at[1]),
         pltpu.make_async_copy(g_hbm.at[0], g_ref, sems.at[2]),
     ]
-    for i in range(count):
-        part = pl.ds(i * tile, tile)
+    for i in range(2 * count):
+        part = pl.ds(i * tile // 2, tile // 2)
         copies.append(pltpu.make_async_copy(w_hbm.at[0, part], w_ref.at[part], sems.at[3 + i]))
     for copy in copies:
         copy.start()
-    load = pltpu.make_async_copy(v_hbm.at[0], pack_ref.at[pl.ds(KEYS, KEYS)], sems.at[3 + count])
+    load = pltpu.make_async_copy(v_hbm.at[0], pack_ref.at[pl.ds(KEYS, KEYS)], sems.at[3 + 2 * count])
     load.start()
     bounds = limits(table_ref, offset_ref)
     pack_ref[2 * KEYS :] = bounds
@@ -130,14 +143,15 @@
         best = masked_scores(g, q_ref[...], pack_ref[:KEYS, g * HD : (g + 1) * HD], bounds, s_ref)
         part_ref[Q + g : Q + g + 1, :ROWS] = best
     load.wait()
-    store = pltpu.make_async_copy(pack_ref, pack_hbm, sems.at[4 + count])
+    store = pltpu.make_async_copy(pack_ref, pack_hbm, sems.at[4 + 2 * count])
     store.start()
     copies[2].wait()
     grad = split(g_ref[...])
     for i in range(count):
-        copies[3 + i].wait()
+        copies[3 + 2 * i].wait()
+        copies[4 + 2 * i].wait()
         part = slice(i * tile, (i + 1) * tile)
-        part_ref[:Q, part] = dot3(grad, split(w_ref[part]), NT)
+        part_ref[:Q, part] = dot3_few(grad, split(w_ref[part]), NT)
     store.wait()
 
 
@@ -154,7 +168,7 @@
             pltpu.VMEM(PACK[0], F32),
             pltpu.VMEM((Q, WIDE), F32),
             pltpu.VMEM((WIDE, WIDE), F32),
-            pltpu.SemaphoreType.DMA((8,)),
+            pltpu.SemaphoreType.DMA((11,)),
         ],
         cost_estimate=pl.CostEstimate(flops=0, bytes_accessed=0, transcendentals=0),
         compiler_params=pltpu.CompilerParams(vmem_limit_bytes=FRONT_MB << 20),
@@ -171,7 +185,7 @@
     final = lax.axis_index("section") == lax.axis_size("section") - 1
     g = jnp.where(final, fresh_ref[...], joined(mine_ref[...], other_ref[...]))
     g_ref[...] = g
-    part_ref[:Q] = dot3(split(g), (high_ref[...], low_ref[...]), NT)
+    part_ref[:Q] = dot3_few(split(g), (high_ref[...], low_ref[...]), NT)
     part_ref[Q:] = stats_ref[...]
 
 
@@ -189,20 +203,28 @@
     return call(split_body, [WEIGHT, WEIGHT], w, *after, free=range(1, 1 + len(after)))
 
 
+def store_keys(kt_ref, g, k):
+    kt_ref[g, :HD], kt_ref[g, HD:] = split(jnp.transpose(k))
+
+
+def store_values(v_ref, g, v):
+    v_ref[:, 2 * g * HD : (2 * g + 1) * HD], v_ref[:, (2 * g + 1) * HD : (2 * g + 2) * HD] = split(v)
+
+
 def caches_body(k_ref, v_ref, *refs):
-    kt_high, kt_low, v_high, v_low = refs[-4:]
-    for g in range(KV):
-        kt_high[g], kt_low[g] = split(jnp.transpose(k_ref[:, g * HD : (g + 1) * HD]))
-    v_high[...], v_low[...] = split(v_ref[...])
+    kt_ref, v_out = refs[-2:]
+    for g in range(KV):
+        cols = slice(g * HD, (g + 1) * HD)
+        store_keys(kt_ref, g, k_ref[:, cols])
+        store_values(v_out, g, v_ref[:, cols])
 
 
 def caches(k, v, *after):
-    outs = [KEYS_T, KEYS_T, CACHE_BF, CACHE_BF]
-    return call(caches_body, outs, k, v, *after, free=range(2, 2 + len(after)))
+    return call(caches_body, [KEYS_T, VALUES], k, v, *after, free=range(2, 2 + len(after)))
 
 
 def second_body(q_ref, pack_ref, k_ref, v_ref, bounds_ref, grad_ref, *refs):
-    s_ref, top_ref, kt_high, kt_low, v_high, v_low, copy_ref = refs[-7:]
+    s_ref, top_ref, kt_ref, v_out, copy_ref = refs[-5:]
     final = lax.axis_index("section") == lax.axis_size("section") - 1
     bounds = jnp.where(final, bounds_ref[...], pack_ref[2 * KEYS :])
     top_ref[...] = jnp.full(top_ref.shape, -1e30, F32)
@@ -210,18 +232,18 @@
         cols = slice(g * HD, (g + 1) * HD)
         k = jnp.where(final, k_ref[:, cols], pack_ref[:KEYS, cols])
         top_ref[g : g + 1, :ROWS] = masked_scores(g, q_ref[0, 1], k, bounds, s_ref)
-        kt_high[g], kt_low[g] = split(jnp.transpose(k))
-    v_high[...], v_low[...] = split(jnp.where(final, v_ref[...], pack_ref[KEYS : 2 * KEYS]))
+        store_keys(kt_ref, g, k)
+        store_values(v_out, g, jnp.where(final, v_ref[:, cols], pack_ref[KEYS : 2 * KEYS, cols]))
     copy_ref[...] = grad_ref[...]
 
 
 def second(queries, pack, k_fresh, v_fresh, bounds, grad, *after):
-    outs = [SCORES, STATS, KEYS_T, KEYS_T, CACHE_BF, CACHE_BF, FULL]
+    outs = [SCORES, STATS, KEYS_T, VALUES, FULL]
     free = range(6, 6 + len(after))
     return call(second_body, outs, queries, pack, k_fresh, v_fresh, bounds, grad, *after, free=free)
 
 
-def products_body(d0_ref, d1_ref, s_ref, kt_high, kt_low, v_high, v_low, *refs):
+def products_body(d0_ref, d1_ref, s_ref, kt_ref, v_ref, *refs):
     e_ref, dp_ref, a_ref, b_ref, dout_ref = refs[-5:]
     d0, d1 = d0_ref[...], d1_ref[...]
     best = jnp.maximum(d0[Q:], d1[Q:])
@@ -230,17 +252,17 @@
     a_ref[Q:] = jnp.zeros((TAIL, WIDE), F32)
     a_groups, b_groups = [], []
     for g in range(KV):
-        cols = slice(g * HD, (g + 1) * HD)
-        kt = kt_high[g], kt_low[g]
         e = jnp.exp(s_ref[g] - best[g : g + 1, :ROWS])
         e_ref[g] = e
-        dp = dot3((v_high[:, cols], v_low[:, cols]), split(stacked(dout, g)), NT)
+        high, low = split(stacked(dout, g))
+        v = v_ref[:, 2 * g * HD : (2 * g + 2) * HD]
+        dp = dot(v, jnp.concatenate([high, high], 1), NT) + dot(v[:, :HD], low, NT)
         dp_ref[g] = dp
         total = jnp.sum(e, axis=0, keepdims=True)
         delta = jnp.sum(e * dp, axis=0, keepdims=True)
         mean = jnp.where(total > 0, delta / total, 0.0)
-        b = jnp.transpose(dot3(kt, split(e), NN))
-        centred = jnp.transpose(dot3(kt, split(e * (dp - mean)), NN))
+        b = jnp.transpose(key_sum(kt_ref[g], e))
+        centred = jnp.transpose(key_sum(kt_ref[g], e * (dp - mean)))
         a_groups.append(centred + as_columns(mean) * b)
         b_groups.append(b)
         a_ref[Q + g : Q + g + 1, :ROWS] = delta
@@ -249,10 +271,10 @@
     b_ref[...] = spread(b_groups)
 
 
-def products(dout, s, kt_high, kt_low, v_high, v_low, *after):
+def products(dout, s, kt, v, *after):
     outs = [SCORES, SCORES, WITH_ROWS, FULL, FULL]
-    free = range(7, 7 + len(after))
-    return call(products_body, outs, *dout, s, kt_high, kt_low, v_high, v_low, *after, free=free)
+    free = range(5, 5 + len(after))
+    return call(products_body, outs, *dout, s, kt, v, *after, free=free)
 
 
 def input_body(step, a0, a1, b0, b1, g_ref, high_ref, low_ref, *refs):
@@ -265,7 +287,7 @@
         delta = a_all[Q + g : Q + g + 1, :ROWS] / total
         a, b = stacked(a_all[:Q], g), stacked(b_all, g)
         groups.append((a - as_columns(delta) * b) * as_columns(SCALE / total))
-    part = dot3(split(spread(groups)), (high_ref[...], low_ref[...]), NT)
+    part = dot3_few(split(spread(groups)), (high_ref[...], low_ref[...]), NT)
     part = part + jnp.where(head == 0, g_ref[...], 0.0)
     if step == 1:
         refs[-2][...] = part

time: 108 us -> 106 us (0.981)
  Pallas kernels: 18.8 us -> 16.6 us
    pallas_call x11, Pallas kernels: 12.2 us -> 10.5 us  [call(): pl.pallas_call(body, out_shape=[jax.ShapeDtypeStruct(s, d) for s, d in ou...]
  transfers between devices with their start and end apart: 20 -> 20, of which waited for: 14 -> 14; matrix products, arithmetic and copies ran while one was open for 1% -> 1% of each run, Pallas kernels for 10% -> 9%
where the time goes in v3:
time: 106 us
  waiting for transfers between devices  44.9 us (42%)
  starting transfers between devices  39.1 us (37%)
  Pallas kernels  16.6 us (16%)
  between operations  2.26 us (2%)
  other arithmetic  2.01 us (2%)
    ppermute x6, waiting for transfers between devices, page_sum(): x = join(x, lax.ppermute(x, ('head', 'page'), neighbours(0)))  17.7 us
    ppermute x6, waiting for transfers between devices, page_sum(): return (x, lax.ppermute(x, ('head', 'page'), neighbours(1)))  13.7 us
    ppermute x6, starting transfers between devices, page_sum(): return (x, lax.ppermute(x, ('head', 'page'), neighbours(1)))  12.3 us
    pallas_call x11, Pallas kernels, call(): pl.pallas_call(body, out_shape=[jax.ShapeDtypeStruct(s, d) for s, d in ou...  10.5 us
    ppermute x1, starting transfers between devices, per_device(): pack2 = lax.ppermute(pack, 'section', back_section)  8.42 us
    ppermute x1, starting transfers between devices, per_device(): sums = lax.ppermute(tied(sums, part), 'section', back_section)  7.63 us
    pallas_call x1, Pallas kernels, front(): pl.pallas_call(front_body, out_shape=[jax.ShapeDtypeStruct(s, d) for s, d...  6.03 us
    ppermute x6, starting transfers between devices, page_sum(): x = join(x, lax.ppermute(x, ('head', 'page'), neighbours(0)))  5.88 us
  transfers between devices with their start and end apart: 20, of which 14 were waited for; matrix products, arithmetic and copies ran while one was open for 1% of the time, Pallas kernels for 9%

profile of v3, /device:TPU:24, one launch (start us, length us, event | category | flops | bytes accessed | tf_op | source)
XLA Modules:
  0.0 105.7 jit_solution(4399299705226080503)
XLA Ops:
  1.9 6.0 %shard_map.166 = (f32[2,512,192]{2,1,0:T(8,128)}, f32[72,768]{1,0:T(8,128)}, f32[1032,256]{1,0:T(8,128)}, f32[8,256]{1,0:T(8,128)}) custom-call(f32[1,2,64,768]{3,2,1,0:T(8,128)} %q_ref.5, f32[1,512,256]{2,1,0:T(8,128)} %k_hbm.1, f32[1,512,256]{2,1,0:T(8,128)} %v_hbm.1, f32[1,64,768]{2,1,0:T(8,128)} %g_hbm.1, f32[1,768,768]{2,1,0:T(8,128)} %w_hbm.1, ...), custom_call_target="tpu_custom_call" | custom-call | tf_op jit(solution)/shard_map/pallas_call | solution.py:161
  8.0 1.6 %collective-permute-start = (f32[72,768]{1,0:T(8,128)}, f32[72,768]{1,0:T(8,128)S(1)}, u32[]{:S(2)}, u32[]{:S(2)}) collective-permute-start(f32[72,768]{1,0:T(8,128)} %get-tuple-element.41), channel_id=1, source_target_pairs={{0,1},{1,0},{2,3},{3,2},{4,7},{5,6},{6,5},{7,4},{8,9},{9,8},{10,11... | collective-permute-start | bytes 663560 | tf_op jit(solution)/shard_map/ppermute | solution.py:340
  9.5 8.4 %collective-permute-start.9 = (f32[1032,256]{1,0:T(8,128)}, f32[1032,256]{1,0:T(8,128)S(1)}, u32[]{:S(2)}, u32[]{:S(2)}) collective-permute-start(f32[1032,256]{1,0:T(8,128)} %get-tuple-element.57), channel_id=1, source_target_pairs={{16,0},{32,16},{48,32},{64,48},{80,64},{96,80},{112,96},{128,112},... | collective-permute-start | bytes 3170312 | tf_op jit(solution)/shard_map/ppermute | solution.py:363
  18.0 1.0 maximum_select_fusion.1.refs_0_.d0_ref
  19.0 2.2 %collective-permute-start.1 = (f32[72,768]{1,0:T(8,128)S(1)}, f32[72,768]{1,0:T(8,128)S(1)}, u32[]{:S(2)}, u32[]{:S(2)}) collective-permute-start(f32[72,768]{1,0:T(8,128)S(1)} %maximum_select_fusion.1.refs_0_.d0_ref), channel_id=1, source_target_pairs={{0,3},{1,2},{2,1},{3,0},{4,5},{5,4},{6,7},{7,6},{8,11},{9,10},{10,... | collective-permute-start | bytes 663560 | tf_op jit(solution)/shard_map/ppermute | solution.py:341
  22.7 3.5 %collective-permute-done.1.d1_ref = f32[72,768]{1,0:T(8,128)S(1)} collective-permute-done((f32[72,768]{1,0:T(8,128)S(1)}, f32[72,768]{1,0:T(8,128)S(1)}, u32[]{:S(2)}, u32[]{:S(2)}) %collective-permute-start.1) | collective-permute-done | bytes 221216 | tf_op jit(solution)/shard_map/ppermute | solution.py:341
  26.3 1.3 %shard_map.169 = (f32[2,512,192]{2,1,0:T(8,128)S(1)}, f32[2,512,192]{2,1,0:T(8,128)S(1)}, f32[72,768]{1,0:T(8,128)S(1)}, f32[64,768]{1,0:T(8,128)S(1)}, f32[64,768]{1,0:T(8,128)S(1)}) custom-call(f32[72,768]{1,0:T(8,128)S(1)} %maximum_select_fusion.1.refs_0_.d0_ref, f32[72,768]{1,0:T(8,128)S(1)} %collective-permute-done.1.d1_ref, ...), custom_call_target="tpu_custom_call" | custom-call | tf_op jit(solution)/shard_map/pallas_call | solution.py:69
  27.7 2.0 %collective-permute-start.4 = (f32[64,768]{1,0:T(8,128)S(1)}, f32[64,768]{1,0:T(8,128)S(1)}, u32[]{:S(2)}, u32[]{:S(2)}) collective-permute-start(f32[64,768]{1,0:T(8,128)S(1)} %get-tuple-element.47), channel_id=1, source_target_pairs={{0,1},{1,0},{2,3},{3,2},{4,7},{5,6},{6,5},{7,4},{8,9},{9,8},{10,11... | collective-permute-start | bytes 589832 | tf_op jit(solution)/shard_map/ppermute | solution.py:340
  29.7 3.9 %collective-permute-done.2 = f32[72,768]{1,0:T(8,128)S(1)} collective-permute-done((f32[72,768]{1,0:T(8,128)S(1)}, f32[72,768]{1,0:T(8,128)S(1)}, u32[]{:S(2)}, u32[]{:S(2)}) %collective-permute-start.2) | collective-permute-done | bytes 221216 | tf_op jit(solution)/shard_map/ppermute | solution.py:340
  33.6 2.5 %collective-permute-start.3 = (f32[72,768]{1,0:T(8,128)S(1)}, f32[72,768]{1,0:T(8,128)S(1)}, u32[]{:S(2)}, u32[]{:S(2)}) collective-permute-start(f32[72,768]{1,0:T(8,128)S(1)} %add.31.refs_0_.a0), channel_id=1, source_target_pairs={{0,3},{1,2},{2,1},{3,0},{4,5},{5,4},{6,7},{7,6},{8,11},{9,10},{10,... | collective-permute-start | bytes 663560 | tf_op jit(solution)/shard_map/ppermute | solution.py:341
  36.5 3.8 %collective-permute-start.5 = (f32[64,768]{1,0:T(8,128)S(1)}, f32[64,768]{1,0:T(8,128)S(1)}, u32[]{:S(2)}, u32[]{:S(2)}) collective-permute-start(f32[64,768]{1,0:T(8,128)S(1)} %add.32.b0), channel_id=1, source_target_pairs={{0,3},{1,2},{2,1},{3,0},{4,5},{5,4},{6,7},{7,6},{8,11},{9,10},{10,... | collective-permute-start | bytes 589832 | tf_op jit(solution)/shard_map/ppermute | solution.py:341
  40.7 3.2 %collective-permute-done.5.b1 = f32[64,768]{1,0:T(8,128)S(1)} collective-permute-done((f32[64,768]{1,0:T(8,128)S(1)}, f32[64,768]{1,0:T(8,128)S(1)}, u32[]{:S(2)}, u32[]{:S(2)}) %collective-permute-start.5) | collective-permute-done | bytes 196640 | tf_op jit(solution)/shard_map/ppermute | solution.py:341
  44.0 0.9 shard_map.171
  45.0 1.3 %collective-permute-done.6 = f32[32,768]{1,0:T(8,128)S(1)} collective-permute-done((f32[32,768]{1,0:T(8,128)S(1)}, f32[32,768]{1,0:T(8,128)S(1)}, u32[]{:S(2)}, u32[]{:S(2)}) %collective-permute-start.6) | collective-permute-done | bytes 98336 | tf_op jit(solution)/shard_map/ppermute | solution.py:370
  46.5 1.0 shard_map.172.refs_0_
  47.5 3.7 %collective-permute-done.7 = f32[32,768]{1,0:T(8,128)S(1)} collective-permute-done((f32[32,768]{1,0:T(8,128)S(1)}, f32[32,768]{1,0:T(8,128)S(1)}, u32[]{:S(2)}, u32[]{:S(2)}) %collective-permute-start.7) | collective-permute-done | bytes 98336 | tf_op jit(solution)/shard_map/ppermute | solution.py:372
  51.3 4.5 %collective-permute-start.8 = (f32[32,768]{1,0:T(8,128)S(1)}, f32[32,768]{1,0:T(8,128)S(1)}, u32[]{:S(2)}, u32[]{:S(2)}) collective-permute-start(f32[32,768]{1,0:T(8,128)S(1)} %add.34.refs_0_), channel_id=1, source_target_pairs={{16,0},{32,16},{48,32},{64,48},{80,64},{96,80},{112,96},{128,112},... | collective-permute-start | bytes 294920 | tf_op jit(solution)/shard_map/ppermute | solution.py:373
  55.8 1.3 %shard_map.173 = (f32[2,512,192]{2,1,0:T(8,128)S(1)}, f32[8,768]{1,0:T(8,128)S(1)}, bf16[2,256,512]{2,1,0:T(8,128)(2,1)S(1)}, bf16[512,512]{1,0:T(8,128)(2,1)S(1)}, f32[64,768]{1,0:T(8,128)S(1)}) custom-call(f32[1,2,64,768]{3,2,1,0:T(8,128)S(1)} %copy-done.1, f32[1032,256]{1,0:T(8,128)S(1)} %collective-permute-done.9.pack_ref, f32[512,256]{1,0:T(8,128)S(1)} %copy-done.9, ...), custom_call_target="tpu_custom_call" | custom-call | tf_op jit(solution)/shard_map/pallas_call | solution.py:69
  57.1 0.9 collective-permute-done.8.mine_ref
  58.0 1.3 %collective-permute-done.10.other_ref = f32[32,768]{1,0:T(8,128)S(1)} collective-permute-done((f32[32,768]{1,0:T(8,128)S(1)}, f32[32,768]{1,0:T(8,128)S(1)}, u32[]{:S(2)}, u32[]{:S(2)}) %collective-permute-start.10) | collective-permute-done | bytes 98336 | tf_op jit(solution)/shard_map/ppermute | solution.py:376
  60.2 5.9 %collective-permute-done.11 = f32[72,768]{1,0:T(8,128)S(1)} collective-permute-done((f32[72,768]{1,0:T(8,128)S(1)}, f32[72,768]{1,0:T(8,128)S(1)}, u32[]{:S(2)}, u32[]{:S(2)}) %collective-permute-start.11) | collective-permute-done | bytes 221216 | tf_op jit(solution)/shard_map/ppermute | solution.py:340
  66.2 3.1 %collective-permute-start.12 = (f32[72,768]{1,0:T(8,128)S(1)}, f32[72,768]{1,0:T(8,128)S(1)}, u32[]{:S(2)}, u32[]{:S(2)}) collective-permute-start(f32[72,768]{1,0:T(8,128)S(1)} %maximum_select_fusion.d0_ref), channel_id=1, source_target_pairs={{0,3},{1,2},{2,1},{3,0},{4,5},{5,4},{6,7},{7,6},{8,11},{9,10},{10,... | collective-permute-start | bytes 663560 | tf_op jit(solution)/shard_map/ppermute | solution.py:341
  69.4 7.6 %collective-permute-start.19 = (f32[1024,256]{1,0:T(8,128)S(1)}, f32[1024,256]{1,0:T(8,128)S(1)}, u32[]{:S(2)}, u32[]{:S(2)}) collective-permute-start(f32[1024,256]{1,0:T(8,128)S(1)} %shard_map.172.refs_0_), channel_id=1, source_target_pairs={{16,0},{32,16},{48,32},{64,48},{80,64},{96,80},{112,96},{128,112},... | collective-permute-start | bytes 3145736 | tf_op jit(solution)/shard_map/ppermute | solution.py:380
  77.0 1.3 %shard_map.175 = (f32[2,512,192]{2,1,0:T(8,128)S(1)}, f32[2,512,192]{2,1,0:T(8,128)S(1)}, f32[72,768]{1,0:T(8,128)S(1)}, f32[64,768]{1,0:T(8,128)S(1)}, f32[64,768]{1,0:T(8,128)S(1)}) custom-call(f32[72,768]{1,0:T(8,128)S(1)} %maximum_select_fusion.d0_ref, f32[72,768]{1,0:T(8,128)S(1)} %collective-permute-done.12.d1_ref, ...), custom_call_target="tpu_custom_call" | custom-call | tf_op jit(solution)/shard_map/pallas_call | solution.py:69
  78.4 2.0 %collective-permute-start.15 = (f32[64,768]{1,0:T(8,128)S(1)}, f32[64,768]{1,0:T(8,128)S(1)}, u32[]{:S(2)}, u32[]{:S(2)}) collective-permute-start(f32[64,768]{1,0:T(8,128)S(1)} %get-tuple-element.68), channel_id=1, source_target_pairs={{0,1},{1,0},{2,3},{3,2},{4,7},{5,6},{6,5},{7,4},{8,9},{9,8},{10,11... | collective-permute-start | bytes 589832 | tf_op jit(solution)/shard_map/ppermute | solution.py:340
  80.4 3.9 %collective-permute-done.13 = f32[72,768]{1,0:T(8,128)S(1)} collective-permute-done((f32[72,768]{1,0:T(8,128)S(1)}, f32[72,768]{1,0:T(8,128)S(1)}, u32[]{:S(2)}, u32[]{:S(2)}) %collective-permute-start.13) | collective-permute-done | bytes 221216 | tf_op jit(solution)/shard_map/ppermute | solution.py:340
  84.9 3.6 %collective-permute-done.15 = f32[64,768]{1,0:T(8,128)S(1)} collective-permute-done((f32[64,768]{1,0:T(8,128)S(1)}, f32[64,768]{1,0:T(8,128)S(1)}, u32[]{:S(2)}, u32[]{:S(2)}) %collective-permute-start.15) | collective-permute-done | bytes 196640 | tf_op jit(solution)/shard_map/ppermute | solution.py:340
  88.7 6.9 %collective-permute-done.16.b1 = f32[64,768]{1,0:T(8,128)S(1)} collective-permute-done((f32[64,768]{1,0:T(8,128)S(1)}, f32[64,768]{1,0:T(8,128)S(1)}, u32[]{:S(2)}, u32[]{:S(2)}) %collective-permute-start.16) | collective-permute-done | bytes 196640 | tf_op jit(solution)/shard_map/ppermute | solution.py:341
  95.5 0.9 shard_map.176
  96.5 1.4 %collective-permute-done.17 = f32[64,768]{1,0:T(8,128)S(1)} collective-permute-done((f32[64,768]{1,0:T(8,128)S(1)}, f32[64,768]{1,0:T(8,128)S(1)}, u32[]{:S(2)}, u32[]{:S(2)}) %collective-permute-start.17) | collective-permute-done | bytes 196640 | tf_op jit(solution)/shard_map/ppermute | solution.py:384
  98.1 2.0 %shard_map.177 = (f32[512,256]{1,0:T(8,128)}, f32[512,256]{1,0:T(8,128)}) custom-call(f32[8,768]{1,0:T(8,128)S(1)} %get-tuple-element.71.row_ref, f32[2,512,192]{2,1,0:T(8,128)S(1)} %get-tuple-element.72.e_ref, f32[2,512,192]{2,1,0:T(8,128)S(1)} %get-tuple-element.73.dp_ref, f32[64,768]{1,0:T(8,128)S(1)} %get-tuple-element.74.dout_ref, ...), custom_call_target="tpu_custom_call" | custom-call | tf_op jit(solution)/shard_map/pallas_call | solution.py:69
  100.1 4.9 %collective-permute-done.18 = f32[64,768]{1,0:T(8,128)S(1)} collective-permute-done((f32[64,768]{1,0:T(8,128)S(1)}, f32[64,768]{1,0:T(8,128)S(1)}, u32[]{:S(2)}, u32[]{:S(2)}) %collective-permute-start.18) | collective-permute-done | bytes 196640 | tf_op jit(solution)/shard_map/ppermute | solution.py:386
  (57 shorter events, 5.4 us)
Async XLA Ops:
  1.9 19.3 %copy-start.2 = (f32[1,768,768]{2,1,0:T(8,128)S(1)}, f32[1,768,768]{2,1,0:T(8,128)}, u32[]{:S(2)}) copy-start(f32[1,768,768]{2,1,0:T(8,128)} %param.28) | copy-start | bytes 7077892
  8.0 10.0 %collective-permute-start = (f32[72,768]{1,0:T(8,128)}, f32[72,768]{1,0:T(8,128)S(1)}, u32[]{:S(2)}, u32[]{:S(2)}) collective-permute-start(f32[72,768]{1,0:T(8,128)} %get-tuple-element.41), channel_id=1, source_target_pairs={{0,1},{1,0},{2,3},{3,2},{4,7},{5,6},{6,5},{7,4},{8,9},{9,8},{10,11... | collective-permute-start | bytes 663560 | tf_op jit(solution)/shard_map/ppermute | solution.py:340
  9.5 46.2 %collective-permute-start.9 = (f32[1032,256]{1,0:T(8,128)}, f32[1032,256]{1,0:T(8,128)S(1)}, u32[]{:S(2)}, u32[]{:S(2)}) collective-permute-start(f32[1032,256]{1,0:T(8,128)} %get-tuple-element.57), channel_id=1, source_target_pairs={{16,0},{32,16},{48,32},{64,48},{80,64},{96,80},{112,96},{128,112},... | collective-permute-start | bytes 3170312 | tf_op jit(solution)/shard_map/ppermute | solution.py:363
  19.0 7.2 %collective-permute-start.1 = (f32[72,768]{1,0:T(8,128)S(1)}, f32[72,768]{1,0:T(8,128)S(1)}, u32[]{:S(2)}, u32[]{:S(2)}) collective-permute-start(f32[72,768]{1,0:T(8,128)S(1)} %maximum_select_fusion.1.refs_0_.d0_ref), channel_id=1, source_target_pairs={{0,3},{1,2},{2,1},{3,0},{4,5},{5,4},{6,7},{7,6},{8,11},{9,10},{10,... | collective-permute-start | bytes 663560 | tf_op jit(solution)/shard_map/ppermute | solution.py:341
  21.2 1.2 %copy-start.4 = (f32[1,512,256]{2,1,0:T(8,128)S(1)}, f32[1,512,256]{2,1,0:T(8,128)}, u32[]{:S(2)}) copy-start(f32[1,512,256]{2,1,0:T(8,128)} %v_hbm.1) | copy-start | bytes 1572868
  21.6 4.7 %copy-start.5 = (f32[2,512,192]{2,1,0:T(8,128)S(1)}, f32[2,512,192]{2,1,0:T(8,128)}, u32[]{:S(2)}) copy-start(f32[2,512,192]{2,1,0:T(8,128)} %get-tuple-element.42.s_ref) | copy-start | bytes 2359300
  26.3 14.1 %copy-start = (f32[1,768,768]{2,1,0:T(8,128)S(1)}, f32[1,768,768]{2,1,0:T(8,128)}, u32[]{:S(2)}) copy-start(f32[1,768,768]{2,1,0:T(8,128)} %w_hbm.1) | copy-start | bytes 7077892
  27.6 6.0 %collective-permute-start.2 = (f32[72,768]{1,0:T(8,128)S(1)}, f32[72,768]{1,0:T(8,128)S(1)}, u32[]{:S(2)}, u32[]{:S(2)}) collective-permute-start(f32[72,768]{1,0:T(8,128)S(1)} %get-tuple-element.46), channel_id=1, source_target_pairs={{0,1},{1,0},{2,3},{3,2},{4,7},{5,6},{6,5},{7,4},{8,9},{9,8},{10,11... | collective-permute-start | bytes 663560 | tf_op jit(solution)/shard_map/ppermute | solution.py:340
  27.7 8.8 %collective-permute-start.4 = (f32[64,768]{1,0:T(8,128)S(1)}, f32[64,768]{1,0:T(8,128)S(1)}, u32[]{:S(2)}, u32[]{:S(2)}) collective-permute-start(f32[64,768]{1,0:T(8,128)S(1)} %get-tuple-element.47), channel_id=1, source_target_pairs={{0,1},{1,0},{2,3},{3,2},{4,7},{5,6},{6,5},{7,4},{8,9},{9,8},{10,11... | collective-permute-start | bytes 589832 | tf_op jit(solution)/shard_map/ppermute | solution.py:340
  33.6 10.4 %collective-permute-start.3 = (f32[72,768]{1,0:T(8,128)S(1)}, f32[72,768]{1,0:T(8,128)S(1)}, u32[]{:S(2)}, u32[]{:S(2)}) collective-permute-start(f32[72,768]{1,0:T(8,128)S(1)} %add.31.refs_0_.a0), channel_id=1, source_target_pairs={{0,3},{1,2},{2,1},{3,0},{4,5},{5,4},{6,7},{7,6},{8,11},{9,10},{10,... | collective-permute-start | bytes 663560 | tf_op jit(solution)/shard_map/ppermute | solution.py:341
  36.5 7.5 %collective-permute-start.5 = (f32[64,768]{1,0:T(8,128)S(1)}, f32[64,768]{1,0:T(8,128)S(1)}, u32[]{:S(2)}, u32[]{:S(2)}) collective-permute-start(f32[64,768]{1,0:T(8,128)S(1)} %add.32.b0), channel_id=1, source_target_pairs={{0,3},{1,2},{2,1},{3,0},{4,5},{5,4},{6,7},{7,6},{8,11},{9,10},{10,... | collective-permute-start | bytes 589832 | tf_op jit(solution)/shard_map/ppermute | solution.py:341
  40.3 3.7 %copy-start.6 = (f32[1,64,768]{2,1,0:T(8,128)S(1)}, f32[1,64,768]{2,1,0:T(8,128)}, u32[]{:S(2)}) copy-start(f32[1,64,768]{2,1,0:T(8,128)} %g_hbm.1) | copy-start | bytes 589828
  44.0 2.4 %copy-start.1 = (f32[1,2,64,768]{3,2,1,0:T(8,128)S(1)}, f32[1,2,64,768]{3,2,1,0:T(8,128)}, u32[]{:S(2)}) copy-start(f32[1,2,64,768]{3,2,1,0:T(8,128)} %q_ref.5) | copy-start | bytes 1179652
  44.0 2.4 %copy-start.7 = (f32[1,512,256]{2,1,0:T(8,128)S(1)}, f32[1,512,256]{2,1,0:T(8,128)}, u32[]{:S(2)}) copy-start(f32[1,512,256]{2,1,0:T(8,128)} %refs_0_.1) | copy-start | bytes 1572868
  44.0 2.4 %copy-start.8 = (f32[1,512,256]{2,1,0:T(8,128)S(1)}, f32[1,512,256]{2,1,0:T(8,128)}, u32[]{:S(2)}) copy-start(f32[1,512,256]{2,1,0:T(8,128)} %refs_1_.1) | copy-start | bytes 1572868
  44.9 1.4 %collective-permute-start.6 = (f32[32,768]{1,0:T(8,128)S(1)}, f32[32,768]{1,0:T(8,128)S(1)}, u32[]{:S(2)}, u32[]{:S(2)}) collective-permute-start(f32[32,768]{1,0:T(8,128)S(1)} %get-tuple-element.51), channel_id=1, source_target_pairs={{0,4},{4,0},{8,12},{12,8},{1,5},{5,1},{9,13},{13,9},{2,6},{6,2},{1... | collective-permute-start | bytes 294920 | tf_op jit(solution)/shard_map/ppermute | solution.py:370
  46.3 4.9 %collective-permute-start.7 = (f32[32,768]{1,0:T(8,128)S(1)}, f32[32,768]{1,0:T(8,128)S(1)}, u32[]{:S(2)}, u32[]{:S(2)}) collective-permute-start(f32[32,768]{1,0:T(8,128)S(1)} %add.33.refs_2_), channel_id=1, source_target_pairs={{0,8},{4,12},{8,0},{12,4},{1,9},{5,13},{9,1},{13,5},{2,10},{6,14},... | collective-permute-start | bytes 294920 | tf_op jit(solution)/shard_map/ppermute | solution.py:372
  46.4 9.3 %copy-start.9 = (f32[512,256]{1,0:T(8,128)S(1)}, f32[512,256]{1,0:T(8,128)}, u32[]{:S(2)}) copy-start(f32[512,256]{1,0:T(8,128)} %k_ref.1) | copy-start | bytes 1572868
  46.4 9.3 %copy-start.10 = (f32[512,256]{1,0:T(8,128)S(1)}, f32[512,256]{1,0:T(8,128)}, u32[]{:S(2)}) copy-start(f32[512,256]{1,0:T(8,128)} %v_ref.1) | copy-start | bytes 1572868
  46.5 9.3 %copy-start.11 = (f32[64,768]{1,0:T(8,128)S(1)}, f32[64,768]{1,0:T(8,128)}, u32[]{:S(2)}) copy-start(f32[64,768]{1,0:T(8,128)} %grad_ref.1) | copy-start | bytes 589828
  46.5 9.3 %copy-start.12 = (f32[8,256]{1,0:T(8,128)S(1)}, f32[8,256]{1,0:T(8,128)}, u32[]{:S(2)}) copy-start(f32[8,256]{1,0:T(8,128)} %get-tuple-element.58.bounds_ref) | copy-start | bytes 24580
  51.3 6.7 %collective-permute-start.8 = (f32[32,768]{1,0:T(8,128)S(1)}, f32[32,768]{1,0:T(8,128)S(1)}, u32[]{:S(2)}, u32[]{:S(2)}) collective-permute-start(f32[32,768]{1,0:T(8,128)S(1)} %add.34.refs_0_), channel_id=1, source_target_pairs={{16,0},{32,16},{48,32},{64,48},{80,64},{96,80},{112,96},{128,112},... | collective-permute-start | bytes 294920 | tf_op jit(solution)/shard_map/ppermute | solution.py:373
  58.0 1.3 %collective-permute-start.10 = (f32[32,768]{1,0:T(8,128)S(1)}, f32[32,768]{1,0:T(8,128)S(1)}, u32[]{:S(2)}, u32[]{:S(2)}) collective-permute-start(f32[32,768]{1,0:T(8,128)S(1)} %collective-permute-done.8.mine_ref), channel_id=1, source_target_pairs={{0,4},{4,0},{8,12},{12,8},{1,5},{5,1},{9,13},{13,9},{2,6},{6,2},{1... | collective-permute-start | bytes 294920 | tf_op jit(solution)/shard_map/ppermute | solution.py:376
  60.1 6.0 %collective-permute-start.11 = (f32[72,768]{1,0:T(8,128)S(1)}, f32[72,768]{1,0:T(8,128)S(1)}, u32[]{:S(2)}, u32[]{:S(2)}) collective-permute-start(f32[72,768]{1,0:T(8,128)S(1)} %get-tuple-element.63), channel_id=1, source_target_pairs={{0,1},{1,0},{2,3},{3,2},{4,7},{5,6},{6,5},{7,4},{8,9},{9,8},{10,11... | collective-permute-start | bytes 663560 | tf_op jit(solution)/shard_map/ppermute | solution.py:340
  66.2 10.8 %collective-permute-start.12 = (f32[72,768]{1,0:T(8,128)S(1)}, f32[72,768]{1,0:T(8,128)S(1)}, u32[]{:S(2)}, u32[]{:S(2)}) collective-permute-start(f32[72,768]{1,0:T(8,128)S(1)} %maximum_select_fusion.d0_ref), channel_id=1, source_target_pairs={{0,3},{1,2},{2,1},{3,0},{4,5},{5,4},{6,7},{7,6},{8,11},{9,10},{10,... | collective-permute-start | bytes 663560 | tf_op jit(solution)/shard_map/ppermute | solution.py:341
  69.4 28.7 %collective-permute-start.19 = (f32[1024,256]{1,0:T(8,128)S(1)}, f32[1024,256]{1,0:T(8,128)S(1)}, u32[]{:S(2)}, u32[]{:S(2)}) collective-permute-start(f32[1024,256]{1,0:T(8,128)S(1)} %shard_map.172.refs_0_), channel_id=1, source_target_pairs={{16,0},{32,16},{48,32},{64,48},{80,64},{96,80},{112,96},{128,112},... | collective-permute-start | bytes 3145736 | tf_op jit(solution)/shard_map/ppermute | solution.py:380
  78.3 6.0 %collective-permute-start.13 = (f32[72,768]{1,0:T(8,128)S(1)}, f32[72,768]{1,0:T(8,128)S(1)}, u32[]{:S(2)}, u32[]{:S(2)}) collective-permute-start(f32[72,768]{1,0:T(8,128)S(1)} %get-tuple-element.67), channel_id=1, source_target_pairs={{0,1},{1,0},{2,3},{3,2},{4,7},{5,6},{6,5},{7,4},{8,9},{9,8},{10,11... | collective-permute-start | bytes 663560 | tf_op jit(solution)/shard_map/ppermute | solution.py:340
  78.4 10.1 %collective-permute-start.15 = (f32[64,768]{1,0:T(8,128)S(1)}, f32[64,768]{1,0:T(8,128)S(1)}, u32[]{:S(2)}, u32[]{:S(2)}) collective-permute-start(f32[64,768]{1,0:T(8,128)S(1)} %get-tuple-element.68), channel_id=1, source_target_pairs={{0,1},{1,0},{2,3},{3,2},{4,7},{5,6},{6,5},{7,4},{8,9},{9,8},{10,11... | collective-permute-start | bytes 589832 | tf_op jit(solution)/shard_map/ppermute | solution.py:340
  84.4 11.2 %collective-permute-start.14 = (f32[72,768]{1,0:T(8,128)S(1)}, f32[72,768]{1,0:T(8,128)S(1)}, u32[]{:S(2)}, u32[]{:S(2)}) collective-permute-start(f32[72,768]{1,0:T(8,128)S(1)} %add.36.a0), channel_id=1, source_target_pairs={{0,3},{1,2},{2,1},{3,0},{4,5},{5,4},{6,7},{7,6},{8,11},{9,10},{10,... | collective-permute-start | bytes 663560 | tf_op jit(solution)/shard_map/ppermute | solution.py:341
  88.6 7.0 %collective-permute-start.16 = (f32[64,768]{1,0:T(8,128)S(1)}, f32[64,768]{1,0:T(8,128)S(1)}, u32[]{:S(2)}, u32[]{:S(2)}) collective-permute-start(f32[64,768]{1,0:T(8,128)S(1)} %add.37.b0), channel_id=1, source_target_pairs={{0,3},{1,2},{2,1},{3,0},{4,5},{5,4},{6,7},{7,6},{8,11},{9,10},{10,... | collective-permute-start | bytes 589832 | tf_op jit(solution)/shard_map/ppermute | solution.py:341
  96.4 1.5 %collective-permute-start.17 = (f32[64,768]{1,0:T(8,128)S(1)}, f32[64,768]{1,0:T(8,128)S(1)}, u32[]{:S(2)}, u32[]{:S(2)}) collective-permute-start(f32[64,768]{1,0:T(8,128)S(1)} %get-tuple-element.70), channel_id=1, source_target_pairs={{0,4},{4,0},{8,12},{12,8},{1,5},{5,1},{9,13},{13,9},{2,6},{6,2},{1... | collective-permute-start | bytes 589832 | tf_op jit(solution)/shard_map/ppermute | solution.py:384
  98.0 7.0 %collective-permute-start.18 = (f32[64,768]{1,0:T(8,128)S(1)}, f32[64,768]{1,0:T(8,128)S(1)}, u32[]{:S(2)}, u32[]{:S(2)}) collective-permute-start(f32[64,768]{1,0:T(8,128)S(1)} %add.38.refs_1_), channel_id=1, source_target_pairs={{0,8},{4,12},{8,0},{12,4},{1,9},{5,13},{9,1},{13,5},{2,10},{6,14},... | collective-permute-start | bytes 589832 | tf_op jit(solution)/shard_map/ppermute | solution.py:386
  (1 other events, 1.0 us)

commit v4 on v3

--- a/solution.py
+++ b/solution.py
@@ -211,16 +211,16 @@
     v_ref[:, 2 * g * HD : (2 * g + 1) * HD], v_ref[:, (2 * g + 1) * HD : (2 * g + 2) * HD] = split(v)
 
 
-def caches_body(k_ref, v_ref, *refs):
-    kt_ref, v_out = refs[-2:]
+def caches_body(k_ref, v_ref, part_ref, kt_ref, v_out, part_out):
+    part_out[...] = part_ref[...]
     for g in range(KV):
         cols = slice(g * HD, (g + 1) * HD)
         store_keys(kt_ref, g, k_ref[:, cols])
         store_values(v_out, g, v_ref[:, cols])
 
 
-def caches(k, v, *after):
-    return call(caches_body, [KEYS_T, VALUES], k, v, *after, free=range(2, 2 + len(after)))
+def caches(k, v, part):
+    return call(caches_body, [KEYS_T, VALUES, WITH_ROWS], k, v, part)
 
 
 def second_body(q_ref, pack_ref, k_ref, v_ref, bounds_ref, grad_ref, *refs):
@@ -336,8 +336,8 @@
     return [(h * 4 + p, h * 4 + (p ^ (1 if (h + turn) % 2 == 0 else 3))) for h in range(4) for p in range(4)]
 
 
-def page_sum(x, join=jnp.add):
-    x = join(x, lax.ppermute(x, ("head", "page"), neighbours(0)))
+def page_sum(x, join=jnp.add, held=None):
+    x = join(x if held is None else held, lax.ppermute(x, ("head", "page"), neighbours(0)))
     return x, lax.ppermute(x, ("head", "page"), neighbours(1))
 
 
@@ -359,10 +359,10 @@
     s1, part, pack, fresh_bounds = front(
         queries, key_cache, value_cache, grad_in, w_out, page_table[0], offsets, page_fresh, offset_fresh
     )
-    dout1 = page_sum(part, sum_and_top)
+    *split1, near = caches(key_cache[0], value_cache[0], part)
+    dout1 = page_sum(part, sum_and_top, near)
+    wq_high, wq_low = split_weights(w_query[0], dout1[0])
     pack2 = lax.ppermute(pack, "section", back_section)
-    split1 = caches(key_cache[0], value_cache[0], dout1[0])
-    wq_high, wq_low = split_weights(w_query[0], dout1[0])
     e1, dp1, a, b, dout1 = products(dout1, s1, *split1, wq_high)
     a1, b1 = page_sum(a), page_sum(b)
     wo_high, wo_low = split_weights(w_out[0], a1[0])
@@ -377,9 +377,9 @@
 
     part, g2 = dout_second((mine, other), fresh, m2, wo_high, wo_low, sums)
     dout2 = page_sum(part, sum_and_top)
-    sums = lax.ppermute(tied(sums, part), "section", back_section)
+    sums = lax.ppermute(tied(sums, m2), "section", back_section)
     e2, dp2, a, b, dout2 = products(dout2, s2, *split2)
-    a2, b2 = page_sum(a), page_sum(b)
+    a2, b2 = page_sum(a), page_sum(b, lambda x, y: tied(x + y, sums))
     part, rows2 = input_gradient(1, a2, b2, g2, wq_high, wq_low)
     part = part + lax.ppermute(part, "head", swap(1))
     key_final, value_final = gradient_sums(1, rows2, e2, dp2, dout2, queries, (sums,), part)

time: 106 us -> 103 us (0.972)
  waiting for transfers between devices: 44.9 us -> 43 us
    ppermute x6, starting transfers between devices: 12.3 us -> 17.6 us  [page_sum(): return (x, lax.ppermute(x, ('head', 'page'), neighbours(1)))]
    ppermute x7, starting transfers between devices: 13.5 us -> 9.1 us  [the longest x6 5.88 us: page_sum(): lax.ppermute(x, ('head', 'page'), neighbours(0))]
    ppermute x7, waiting for transfers between devices: 17.7 us -> 14.3 us  [the longest x6 14.3 us: page_sum(): lax.ppermute(x, ('head', 'page'), neighbours(0))]
    ppermute x6, waiting for transfers between devices: 13.7 us -> 16.1 us  [page_sum(): return (x, lax.ppermute(x, ('head', 'page'), neighbours(1)))]
    ppermute x1, starting transfers between devices: 4.49 us -> 3.04 us  [per_device(): mine = lax.ppermute(tied(part, sums), 'section', back_section)]
  transfers between devices with their start and end apart: 20 -> 20, of which waited for: 14 -> 15; matrix products, arithmetic and copies ran while one was open for 1% -> 0% of each run, Pallas kernels for 9% -> 9%
where the time goes in v4:
time: 103 us
  waiting for transfers between devices  43 us (42%)
  starting transfers between devices  38.6 us (37%)
  Pallas kernels  16.8 us (16%)
  between operations  2.29 us (2%)
  other arithmetic  1.06 us (1%)
    ppermute x6, starting transfers between devices, page_sum(): return (x, lax.ppermute(x, ('head', 'page'), neighbours(1)))  17.6 us
    ppermute x6, waiting for transfers between devices, page_sum(): return (x, lax.ppermute(x, ('head', 'page'), neighbours(1)))  16.1 us
    ppermute x6, waiting for transfers between devices, page_sum(): lax.ppermute(x, ('head', 'page'), neighbours(0))  14.3 us
    pallas_call x11, Pallas kernels, call(): pl.pallas_call(body, out_shape=[jax.ShapeDtypeStruct(s, d) for s, d in ou...  10.6 us
    ppermute x1, starting transfers between devices, per_device(): pack2 = lax.ppermute(pack, 'section', back_section)  8.42 us
    pallas_call x1, Pallas kernels, front(): pl.pallas_call(front_body, out_shape=[jax.ShapeDtypeStruct(s, d) for s, d...  6.2 us
    ppermute x6, starting transfers between devices, page_sum(): lax.ppermute(x, ('head', 'page'), neighbours(0))  5.88 us
    ppermute x1, waiting for transfers between devices, per_device(): grad_done = part + tied(lax.ppermute(part, 'head', swap(2)), key_final)  4.96 us
  transfers between devices with their start and end apart: 20, of which 15 were waited for; matrix products, arithmetic and copies ran while one was open for 0% of the time, Pallas kernels for 9%

profile of v4, /device:TPU:24, one launch (start us, length us, event | category | flops | bytes accessed | tf_op | source)
XLA Modules:
  0.0 102.8 jit_solution(5954735913928715216)
XLA Ops:
  2.0 6.2 %shard_map.166 = (f32[2,512,192]{2,1,0:T(8,128)}, f32[72,768]{1,0:T(8,128)}, f32[1032,256]{1,0:T(8,128)}, f32[8,256]{1,0:T(8,128)}) custom-call(f32[1,2,64,768]{3,2,1,0:T(8,128)} %q_ref.5, f32[1,512,256]{2,1,0:T(8,128)} %k_hbm.1, f32[1,512,256]{2,1,0:T(8,128)} %v_hbm.1, f32[1,64,768]{2,1,0:T(8,128)} %g_hbm.1, f32[1,768,768]{2,1,0:T(8,128)} %w_hbm.1, ...), custom_call_target="tpu_custom_call" | custom-call | tf_op jit(solution)/shard_map/pallas_call | solution.py:161
  8.2 1.6 %collective-permute-start = (f32[72,768]{1,0:T(8,128)}, f32[72,768]{1,0:T(8,128)S(1)}, u32[]{:S(2)}, u32[]{:S(2)}) collective-permute-start(f32[72,768]{1,0:T(8,128)} %get-tuple-element.43.part_ref), channel_id=1, source_target_pairs={{0,1},{1,0},{2,3},{3,2},{4,7},{5,6},{6,5},{7,4},{8,9},{9,8},{10,11... | collective-permute-start | bytes 663560 | tf_op jit(solution)/shard_map/ppermute | solution.py:340
  9.7 8.4 %collective-permute-start.9 = (f32[1032,256]{1,0:T(8,128)}, f32[1032,256]{1,0:T(8,128)S(1)}, u32[]{:S(2)}, u32[]{:S(2)}) collective-permute-start(f32[1032,256]{1,0:T(8,128)} %get-tuple-element.60), channel_id=1, source_target_pairs={{16,0},{32,16},{48,32},{64,48},{80,64},{96,80},{112,96},{128,112},... | collective-permute-start | bytes 3170312 | tf_op jit(solution)/shard_map/ppermute | solution.py:365
  18.2 0.9 copy-done.11
  19.6 2.2 %collective-permute-start.1 = (f32[72,768]{1,0:T(8,128)S(1)}, f32[72,768]{1,0:T(8,128)S(1)}, u32[]{:S(2)}, u32[]{:S(2)}) collective-permute-start(f32[72,768]{1,0:T(8,128)S(1)} %maximum_select_fusion.1.refs_0_.d0_ref), channel_id=1, source_target_pairs={{0,3},{1,2},{2,1},{3,0},{4,5},{5,4},{6,7},{7,6},{8,11},{9,10},{10,... | collective-permute-start | bytes 663560 | tf_op jit(solution)/shard_map/ppermute | solution.py:341
  22.1 4.7 %collective-permute-done.1.d1_ref = f32[72,768]{1,0:T(8,128)S(1)} collective-permute-done((f32[72,768]{1,0:T(8,128)S(1)}, f32[72,768]{1,0:T(8,128)S(1)}, u32[]{:S(2)}, u32[]{:S(2)}) %collective-permute-start.1) | collective-permute-done | bytes 221216 | tf_op jit(solution)/shard_map/ppermute | solution.py:341
  26.8 1.3 %shard_map.169 = (f32[2,512,192]{2,1,0:T(8,128)S(1)}, f32[2,512,192]{2,1,0:T(8,128)S(1)}, f32[72,768]{1,0:T(8,128)S(1)}, f32[64,768]{1,0:T(8,128)S(1)}, f32[64,768]{1,0:T(8,128)S(1)}) custom-call(f32[72,768]{1,0:T(8,128)S(1)} %maximum_select_fusion.1.refs_0_.d0_ref, f32[72,768]{1,0:T(8,128)S(1)} %collective-permute-done.1.d1_ref, ...), custom_call_target="tpu_custom_call" | custom-call | tf_op jit(solution)/shard_map/pallas_call | solution.py:69
  28.2 2.0 %collective-permute-start.4 = (f32[64,768]{1,0:T(8,128)S(1)}, f32[64,768]{1,0:T(8,128)S(1)}, u32[]{:S(2)}, u32[]{:S(2)}) collective-permute-start(f32[64,768]{1,0:T(8,128)S(1)} %get-tuple-element.50), channel_id=1, source_target_pairs={{0,1},{1,0},{2,3},{3,2},{4,7},{5,6},{6,5},{7,4},{8,9},{9,8},{10,11... | collective-permute-start | bytes 589832 | tf_op jit(solution)/shard_map/ppermute | solution.py:340
  30.3 3.9 %collective-permute-done.2 = f32[72,768]{1,0:T(8,128)S(1)} collective-permute-done((f32[72,768]{1,0:T(8,128)S(1)}, f32[72,768]{1,0:T(8,128)S(1)}, u32[]{:S(2)}, u32[]{:S(2)}) %collective-permute-start.2) | collective-permute-done | bytes 221216 | tf_op jit(solution)/shard_map/ppermute | solution.py:340
  34.2 2.5 %collective-permute-start.3 = (f32[72,768]{1,0:T(8,128)S(1)}, f32[72,768]{1,0:T(8,128)S(1)}, u32[]{:S(2)}, u32[]{:S(2)}) collective-permute-start(f32[72,768]{1,0:T(8,128)S(1)} %add.31.refs_0_.a0), channel_id=1, source_target_pairs={{0,3},{1,2},{2,1},{3,0},{4,5},{5,4},{6,7},{7,6},{8,11},{9,10},{10,... | collective-permute-start | bytes 663560 | tf_op jit(solution)/shard_map/ppermute | solution.py:341
  37.1 3.8 %collective-permute-start.5 = (f32[64,768]{1,0:T(8,128)S(1)}, f32[64,768]{1,0:T(8,128)S(1)}, u32[]{:S(2)}, u32[]{:S(2)}) collective-permute-start(f32[64,768]{1,0:T(8,128)S(1)} %add.32.b0), channel_id=1, source_target_pairs={{0,3},{1,2},{2,1},{3,0},{4,5},{5,4},{6,7},{7,6},{8,11},{9,10},{10,... | collective-permute-start | bytes 589832 | tf_op jit(solution)/shard_map/ppermute | solution.py:341
  41.3 3.2 %collective-permute-done.5.b1 = f32[64,768]{1,0:T(8,128)S(1)} collective-permute-done((f32[64,768]{1,0:T(8,128)S(1)}, f32[64,768]{1,0:T(8,128)S(1)}, u32[]{:S(2)}, u32[]{:S(2)}) %collective-permute-start.5) | collective-permute-done | bytes 196640 | tf_op jit(solution)/shard_map/ppermute | solution.py:341
  45.6 1.3 %collective-permute-done.6 = f32[32,768]{1,0:T(8,128)S(1)} collective-permute-done((f32[32,768]{1,0:T(8,128)S(1)}, f32[32,768]{1,0:T(8,128)S(1)}, u32[]{:S(2)}, u32[]{:S(2)}) %collective-permute-start.6) | collective-permute-done | bytes 98336 | tf_op jit(solution)/shard_map/ppermute | solution.py:370
  47.0 1.0 shard_map.172.refs_0_
  48.1 3.7 %collective-permute-done.7 = f32[32,768]{1,0:T(8,128)S(1)} collective-permute-done((f32[32,768]{1,0:T(8,128)S(1)}, f32[32,768]{1,0:T(8,128)S(1)}, u32[]{:S(2)}, u32[]{:S(2)}) %collective-permute-start.7) | collective-permute-done | bytes 98336 | tf_op jit(solution)/shard_map/ppermute | solution.py:372
  51.8 3.0 %collective-permute-start.8 = (f32[32,768]{1,0:T(8,128)S(1)}, f32[32,768]{1,0:T(8,128)S(1)}, u32[]{:S(2)}, u32[]{:S(2)}) collective-permute-start(f32[32,768]{1,0:T(8,128)S(1)} %add.34.refs_0_), channel_id=1, source_target_pairs={{16,0},{32,16},{48,32},{64,48},{80,64},{96,80},{112,96},{128,112},... | collective-permute-start | bytes 294920 | tf_op jit(solution)/shard_map/ppermute | solution.py:373
  54.9 1.3 %shard_map.173 = (f32[2,512,192]{2,1,0:T(8,128)S(1)}, f32[8,768]{1,0:T(8,128)S(1)}, bf16[2,256,512]{2,1,0:T(8,128)(2,1)S(1)}, bf16[512,512]{1,0:T(8,128)(2,1)S(1)}, f32[64,768]{1,0:T(8,128)S(1)}) custom-call(f32[1,2,64,768]{3,2,1,0:T(8,128)S(1)} %copy-done.1, f32[1032,256]{1,0:T(8,128)S(1)} %collective-permute-done.9.pack_ref, f32[512,256]{1,0:T(8,128)S(1)} %copy-done.9, ...), custom_call_target="tpu_custom_call" | custom-call | tf_op jit(solution)/shard_map/pallas_call | solution.py:69
  56.2 3.2 %collective-permute-start.16 = (f32[1024,256]{1,0:T(8,128)S(1)}, f32[1024,256]{1,0:T(8,128)S(1)}, u32[]{:S(2)}, u32[]{:S(2)}) collective-permute-start(f32[1024,256]{1,0:T(8,128)S(1)} %shard_map.172.refs_0_), channel_id=1, source_target_pairs={{16,0},{32,16},{48,32},{64,48},{80,64},{96,80},{112,96},{128,112},... | collective-permute-start | bytes 3145736 | tf_op jit(solution)/shard_map/ppermute | solution.py:380
  59.5 1.3 %collective-permute-done.10.other_ref = f32[32,768]{1,0:T(8,128)S(1)} collective-permute-done((f32[32,768]{1,0:T(8,128)S(1)}, f32[32,768]{1,0:T(8,128)S(1)}, u32[]{:S(2)}, u32[]{:S(2)}) %collective-permute-start.10) | collective-permute-done | bytes 98336 | tf_op jit(solution)/shard_map/ppermute | solution.py:376
  61.8 5.9 %collective-permute-done.11 = f32[72,768]{1,0:T(8,128)S(1)} collective-permute-done((f32[72,768]{1,0:T(8,128)S(1)}, f32[72,768]{1,0:T(8,128)S(1)}, u32[]{:S(2)}, u32[]{:S(2)}) %collective-permute-start.11) | collective-permute-done | bytes 221216 | tf_op jit(solution)/shard_map/ppermute | solution.py:340
  67.8 3.0 %collective-permute-start.12 = (f32[72,768]{1,0:T(8,128)S(1)}, f32[72,768]{1,0:T(8,128)S(1)}, u32[]{:S(2)}, u32[]{:S(2)}) collective-permute-start(f32[72,768]{1,0:T(8,128)S(1)} %maximum_select_fusion.d0_ref), channel_id=1, source_target_pairs={{0,3},{1,2},{2,1},{3,0},{4,5},{5,4},{6,7},{7,6},{8,11},{9,10},{10,... | collective-permute-start | bytes 663560 | tf_op jit(solution)/shard_map/ppermute | solution.py:341
  70.8 4.2 %collective-permute-done.12.d1_ref = f32[72,768]{1,0:T(8,128)S(1)} collective-permute-done((f32[72,768]{1,0:T(8,128)S(1)}, f32[72,768]{1,0:T(8,128)S(1)}, u32[]{:S(2)}, u32[]{:S(2)}) %collective-permute-start.12) | collective-permute-done | bytes 221216 | tf_op jit(solution)/shard_map/ppermute | solution.py:341
  75.0 1.3 %shard_map.175 = (f32[2,512,192]{2,1,0:T(8,128)S(1)}, f32[2,512,192]{2,1,0:T(8,128)S(1)}, f32[72,768]{1,0:T(8,128)S(1)}, f32[64,768]{1,0:T(8,128)S(1)}, f32[64,768]{1,0:T(8,128)S(1)}) custom-call(f32[72,768]{1,0:T(8,128)S(1)} %maximum_select_fusion.d0_ref, f32[72,768]{1,0:T(8,128)S(1)} %collective-permute-done.12.d1_ref, ...), custom_call_target="tpu_custom_call" | custom-call | tf_op jit(solution)/shard_map/pallas_call | solution.py:69
  76.4 2.0 %collective-permute-start.15 = (f32[64,768]{1,0:T(8,128)S(1)}, f32[64,768]{1,0:T(8,128)S(1)}, u32[]{:S(2)}, u32[]{:S(2)}) collective-permute-start(f32[64,768]{1,0:T(8,128)S(1)} %get-tuple-element.71), channel_id=1, source_target_pairs={{0,1},{1,0},{2,3},{3,2},{4,7},{5,6},{6,5},{7,4},{8,9},{9,8},{10,11... | collective-permute-start | bytes 589832 | tf_op jit(solution)/shard_map/ppermute | solution.py:340
  78.4 3.9 %collective-permute-done.13 = f32[72,768]{1,0:T(8,128)S(1)} collective-permute-done((f32[72,768]{1,0:T(8,128)S(1)}, f32[72,768]{1,0:T(8,128)S(1)}, u32[]{:S(2)}, u32[]{:S(2)}) %collective-permute-start.13) | collective-permute-done | bytes 221216 | tf_op jit(solution)/shard_map/ppermute | solution.py:340
  82.4 3.0 %collective-permute-start.14 = (f32[72,768]{1,0:T(8,128)S(1)}, f32[72,768]{1,0:T(8,128)S(1)}, u32[]{:S(2)}, u32[]{:S(2)}) collective-permute-start(f32[72,768]{1,0:T(8,128)S(1)} %add.36.a0), channel_id=1, source_target_pairs={{0,3},{1,2},{2,1},{3,0},{4,5},{5,4},{6,7},{7,6},{8,11},{9,10},{10,... | collective-permute-start | bytes 663560 | tf_op jit(solution)/shard_map/ppermute | solution.py:341
  85.6 3.0 %collective-permute-start.17 = (f32[64,768]{1,0:T(8,128)S(1)}, f32[64,768]{1,0:T(8,128)S(1)}, u32[]{:S(2)}, u32[]{:S(2)}) collective-permute-start(f32[64,768]{1,0:T(8,128)S(1)} %add.37.b0), channel_id=1, source_target_pairs={{0,3},{1,2},{2,1},{3,0},{4,5},{5,4},{6,7},{7,6},{8,11},{9,10},{10,... | collective-permute-start | bytes 589832 | tf_op jit(solution)/shard_map/ppermute | solution.py:341
  88.6 1.0 collective-permute-done.14.a1
  89.6 3.0 %collective-permute-done.17.b1 = f32[64,768]{1,0:T(8,128)S(1)} collective-permute-done((f32[64,768]{1,0:T(8,128)S(1)}, f32[64,768]{1,0:T(8,128)S(1)}, u32[]{:S(2)}, u32[]{:S(2)}) %collective-permute-start.17) | collective-permute-done | bytes 196640 | tf_op jit(solution)/shard_map/ppermute | solution.py:341
  93.6 1.4 %collective-permute-done.18 = f32[64,768]{1,0:T(8,128)S(1)} collective-permute-done((f32[64,768]{1,0:T(8,128)S(1)}, f32[64,768]{1,0:T(8,128)S(1)}, u32[]{:S(2)}, u32[]{:S(2)}) %collective-permute-start.18) | collective-permute-done | bytes 196640 | tf_op jit(solution)/shard_map/ppermute | solution.py:384
  95.1 2.0 %shard_map.177 = (f32[512,256]{1,0:T(8,128)}, f32[512,256]{1,0:T(8,128)}) custom-call(f32[8,768]{1,0:T(8,128)S(1)} %get-tuple-element.76.row_ref, f32[2,512,192]{2,1,0:T(8,128)S(1)} %get-tuple-element.77.e_ref, f32[2,512,192]{2,1,0:T(8,128)S(1)} %get-tuple-element.78.dp_ref, f32[64,768]{1,0:T(8,128)S(1)} %get-tuple-element.79.dout_ref, ...), custom_call_target="tpu_custom_call" | custom-call | tf_op jit(solution)/shard_map/pallas_call | solution.py:69
  97.1 5.0 %collective-permute-done.19 = f32[64,768]{1,0:T(8,128)S(1)} collective-permute-done((f32[64,768]{1,0:T(8,128)S(1)}, f32[64,768]{1,0:T(8,128)S(1)}, u32[]{:S(2)}, u32[]{:S(2)}) %collective-permute-start.19) | collective-permute-done | bytes 196640 | tf_op jit(solution)/shard_map/ppermute | solution.py:386
  (59 shorter events, 6.1 us)
Async XLA Ops:
  1.9 16.2 %copy-start.3 = (f32[1,512,256]{2,1,0:T(8,128)S(1)}, f32[1,512,256]{2,1,0:T(8,128)}, u32[]{:S(2)}) copy-start(f32[1,512,256]{2,1,0:T(8,128)} %k_hbm.1) | copy-start | bytes 1572868
  1.9 16.2 %copy-start.4 = (f32[1,512,256]{2,1,0:T(8,128)S(1)}, f32[1,512,256]{2,1,0:T(8,128)}, u32[]{:S(2)}) copy-start(f32[1,512,256]{2,1,0:T(8,128)} %v_hbm.1) | copy-start | bytes 1572868
  1.9 19.8 %copy-start.2 = (f32[1,768,768]{2,1,0:T(8,128)S(1)}, f32[1,768,768]{2,1,0:T(8,128)}, u32[]{:S(2)}) copy-start(f32[1,768,768]{2,1,0:T(8,128)} %param.28) | copy-start | bytes 7077892
  8.2 11.3 %collective-permute-start = (f32[72,768]{1,0:T(8,128)}, f32[72,768]{1,0:T(8,128)S(1)}, u32[]{:S(2)}, u32[]{:S(2)}) collective-permute-start(f32[72,768]{1,0:T(8,128)} %get-tuple-element.43.part_ref), channel_id=1, source_target_pairs={{0,1},{1,0},{2,3},{3,2},{4,7},{5,6},{6,5},{7,4},{8,9},{9,8},{10,11... | collective-permute-start | bytes 663560 | tf_op jit(solution)/shard_map/ppermute | solution.py:340
  9.7 45.1 %collective-permute-start.9 = (f32[1032,256]{1,0:T(8,128)}, f32[1032,256]{1,0:T(8,128)S(1)}, u32[]{:S(2)}, u32[]{:S(2)}) collective-permute-start(f32[1032,256]{1,0:T(8,128)} %get-tuple-element.60), channel_id=1, source_target_pairs={{16,0},{32,16},{48,32},{64,48},{80,64},{96,80},{112,96},{128,112},... | collective-permute-start | bytes 3170312 | tf_op jit(solution)/shard_map/ppermute | solution.py:365
  19.6 7.2 %collective-permute-start.1 = (f32[72,768]{1,0:T(8,128)S(1)}, f32[72,768]{1,0:T(8,128)S(1)}, u32[]{:S(2)}, u32[]{:S(2)}) collective-permute-start(f32[72,768]{1,0:T(8,128)S(1)} %maximum_select_fusion.1.refs_0_.d0_ref), channel_id=1, source_target_pairs={{0,3},{1,2},{2,1},{3,0},{4,5},{5,4},{6,7},{7,6},{8,11},{9,10},{10,... | collective-permute-start | bytes 663560 | tf_op jit(solution)/shard_map/ppermute | solution.py:341
  21.7 5.0 %copy-start.5 = (f32[2,512,192]{2,1,0:T(8,128)S(1)}, f32[2,512,192]{2,1,0:T(8,128)}, u32[]{:S(2)}) copy-start(f32[2,512,192]{2,1,0:T(8,128)} %get-tuple-element.45.s_ref) | copy-start | bytes 2359300
  26.8 14.1 %copy-start = (f32[1,768,768]{2,1,0:T(8,128)S(1)}, f32[1,768,768]{2,1,0:T(8,128)}, u32[]{:S(2)}) copy-start(f32[1,768,768]{2,1,0:T(8,128)} %w_hbm.1) | copy-start | bytes 7077892
  28.1 6.0 %collective-permute-start.2 = (f32[72,768]{1,0:T(8,128)S(1)}, f32[72,768]{1,0:T(8,128)S(1)}, u32[]{:S(2)}, u32[]{:S(2)}) collective-permute-start(f32[72,768]{1,0:T(8,128)S(1)} %get-tuple-element.49), channel_id=1, source_target_pairs={{0,1},{1,0},{2,3},{3,2},{4,7},{5,6},{6,5},{7,4},{8,9},{9,8},{10,11... | collective-permute-start | bytes 663560 | tf_op jit(solution)/shard_map/ppermute | solution.py:340
  28.2 8.8 %collective-permute-start.4 = (f32[64,768]{1,0:T(8,128)S(1)}, f32[64,768]{1,0:T(8,128)S(1)}, u32[]{:S(2)}, u32[]{:S(2)}) collective-permute-start(f32[64,768]{1,0:T(8,128)S(1)} %get-tuple-element.50), channel_id=1, source_target_pairs={{0,1},{1,0},{2,3},{3,2},{4,7},{5,6},{6,5},{7,4},{8,9},{9,8},{10,11... | collective-permute-start | bytes 589832 | tf_op jit(solution)/shard_map/ppermute | solution.py:340
  34.2 10.3 %collective-permute-start.3 = (f32[72,768]{1,0:T(8,128)S(1)}, f32[72,768]{1,0:T(8,128)S(1)}, u32[]{:S(2)}, u32[]{:S(2)}) collective-permute-start(f32[72,768]{1,0:T(8,128)S(1)} %add.31.refs_0_.a0), channel_id=1, source_target_pairs={{0,3},{1,2},{2,1},{3,0},{4,5},{5,4},{6,7},{7,6},{8,11},{9,10},{10,... | collective-permute-start | bytes 663560 | tf_op jit(solution)/shard_map/ppermute | solution.py:341
  37.1 7.4 %collective-permute-start.5 = (f32[64,768]{1,0:T(8,128)S(1)}, f32[64,768]{1,0:T(8,128)S(1)}, u32[]{:S(2)}, u32[]{:S(2)}) collective-permute-start(f32[64,768]{1,0:T(8,128)S(1)} %add.32.b0), channel_id=1, source_target_pairs={{0,3},{1,2},{2,1},{3,0},{4,5},{5,4},{6,7},{7,6},{8,11},{9,10},{10,... | collective-permute-start | bytes 589832 | tf_op jit(solution)/shard_map/ppermute | solution.py:341
  40.9 3.7 %copy-start.6 = (f32[1,64,768]{2,1,0:T(8,128)S(1)}, f32[1,64,768]{2,1,0:T(8,128)}, u32[]{:S(2)}) copy-start(f32[1,64,768]{2,1,0:T(8,128)} %g_hbm.1) | copy-start | bytes 589828
  44.5 2.4 %copy-start.7 = (f32[1,512,256]{2,1,0:T(8,128)S(1)}, f32[1,512,256]{2,1,0:T(8,128)}, u32[]{:S(2)}) copy-start(f32[1,512,256]{2,1,0:T(8,128)} %refs_0_.1) | copy-start | bytes 1572868
  44.5 2.4 %copy-start.8 = (f32[1,512,256]{2,1,0:T(8,128)S(1)}, f32[1,512,256]{2,1,0:T(8,128)}, u32[]{:S(2)}) copy-start(f32[1,512,256]{2,1,0:T(8,128)} %refs_1_.1) | copy-start | bytes 1572868
  45.5 1.4 %collective-permute-start.6 = (f32[32,768]{1,0:T(8,128)S(1)}, f32[32,768]{1,0:T(8,128)S(1)}, u32[]{:S(2)}, u32[]{:S(2)}) collective-permute-start(f32[32,768]{1,0:T(8,128)S(1)} %get-tuple-element.54), channel_id=1, source_target_pairs={{0,4},{4,0},{8,12},{12,8},{1,5},{5,1},{9,13},{13,9},{2,6},{6,2},{1... | collective-permute-start | bytes 294920 | tf_op jit(solution)/shard_map/ppermute | solution.py:370
  46.9 4.9 %collective-permute-start.7 = (f32[32,768]{1,0:T(8,128)S(1)}, f32[32,768]{1,0:T(8,128)S(1)}, u32[]{:S(2)}, u32[]{:S(2)}) collective-permute-start(f32[32,768]{1,0:T(8,128)S(1)} %add.33.refs_2_), channel_id=1, source_target_pairs={{0,8},{4,12},{8,0},{12,4},{1,9},{5,13},{9,1},{13,5},{2,10},{6,14},... | collective-permute-start | bytes 294920 | tf_op jit(solution)/shard_map/ppermute | solution.py:372
  47.0 7.9 %copy-start.9 = (f32[512,256]{1,0:T(8,128)S(1)}, f32[512,256]{1,0:T(8,128)}, u32[]{:S(2)}) copy-start(f32[512,256]{1,0:T(8,128)} %k_ref.1) | copy-start | bytes 1572868
  47.0 7.9 %copy-start.10 = (f32[512,256]{1,0:T(8,128)S(1)}, f32[512,256]{1,0:T(8,128)}, u32[]{:S(2)}) copy-start(f32[512,256]{1,0:T(8,128)} %v_ref.1) | copy-start | bytes 1572868
  47.0 7.9 %copy-start.12 = (f32[64,768]{1,0:T(8,128)S(1)}, f32[64,768]{1,0:T(8,128)}, u32[]{:S(2)}) copy-start(f32[64,768]{1,0:T(8,128)} %grad_ref.1) | copy-start | bytes 589828
  47.0 7.9 %copy-start.13 = (f32[8,256]{1,0:T(8,128)S(1)}, f32[8,256]{1,0:T(8,128)}, u32[]{:S(2)}) copy-start(f32[8,256]{1,0:T(8,128)} %get-tuple-element.61.bounds_ref) | copy-start | bytes 24580
  51.8 7.6 %collective-permute-start.8 = (f32[32,768]{1,0:T(8,128)S(1)}, f32[32,768]{1,0:T(8,128)S(1)}, u32[]{:S(2)}, u32[]{:S(2)}) collective-permute-start(f32[32,768]{1,0:T(8,128)S(1)} %add.34.refs_0_), channel_id=1, source_target_pairs={{16,0},{32,16},{48,32},{64,48},{80,64},{96,80},{112,96},{128,112},... | collective-permute-start | bytes 294920 | tf_op jit(solution)/shard_map/ppermute | solution.py:373
  56.2 29.4 %collective-permute-start.16 = (f32[1024,256]{1,0:T(8,128)S(1)}, f32[1024,256]{1,0:T(8,128)S(1)}, u32[]{:S(2)}, u32[]{:S(2)}) collective-permute-start(f32[1024,256]{1,0:T(8,128)S(1)} %shard_map.172.refs_0_), channel_id=1, source_target_pairs={{16,0},{32,16},{48,32},{64,48},{80,64},{96,80},{112,96},{128,112},... | collective-permute-start | bytes 3145736 | tf_op jit(solution)/shard_map/ppermute | solution.py:380
  59.4 1.4 %collective-permute-start.10 = (f32[32,768]{1,0:T(8,128)S(1)}, f32[32,768]{1,0:T(8,128)S(1)}, u32[]{:S(2)}, u32[]{:S(2)}) collective-permute-start(f32[32,768]{1,0:T(8,128)S(1)} %collective-permute-done.8.mine_ref), channel_id=1, source_target_pairs={{0,4},{4,0},{8,12},{12,8},{1,5},{5,1},{9,13},{13,9},{2,6},{6,2},{1... | collective-permute-start | bytes 294920 | tf_op jit(solution)/shard_map/ppermute | solution.py:376
  61.7 6.0 %collective-permute-start.11 = (f32[72,768]{1,0:T(8,128)S(1)}, f32[72,768]{1,0:T(8,128)S(1)}, u32[]{:S(2)}, u32[]{:S(2)}) collective-permute-start(f32[72,768]{1,0:T(8,128)S(1)} %get-tuple-element.66), channel_id=1, source_target_pairs={{0,1},{1,0},{2,3},{3,2},{4,7},{5,6},{6,5},{7,4},{8,9},{9,8},{10,11... | collective-permute-start | bytes 663560 | tf_op jit(solution)/shard_map/ppermute | solution.py:340
  67.8 7.2 %collective-permute-start.12 = (f32[72,768]{1,0:T(8,128)S(1)}, f32[72,768]{1,0:T(8,128)S(1)}, u32[]{:S(2)}, u32[]{:S(2)}) collective-permute-start(f32[72,768]{1,0:T(8,128)S(1)} %maximum_select_fusion.d0_ref), channel_id=1, source_target_pairs={{0,3},{1,2},{2,1},{3,0},{4,5},{5,4},{6,7},{7,6},{8,11},{9,10},{10,... | collective-permute-start | bytes 663560 | tf_op jit(solution)/shard_map/ppermute | solution.py:341
  76.3 6.0 %collective-permute-start.13 = (f32[72,768]{1,0:T(8,128)S(1)}, f32[72,768]{1,0:T(8,128)S(1)}, u32[]{:S(2)}, u32[]{:S(2)}) collective-permute-start(f32[72,768]{1,0:T(8,128)S(1)} %get-tuple-element.70), channel_id=1, source_target_pairs={{0,1},{1,0},{2,3},{3,2},{4,7},{5,6},{6,5},{7,4},{8,9},{9,8},{10,11... | collective-permute-start | bytes 663560 | tf_op jit(solution)/shard_map/ppermute | solution.py:340
  76.4 9.1 %collective-permute-start.15 = (f32[64,768]{1,0:T(8,128)S(1)}, f32[64,768]{1,0:T(8,128)S(1)}, u32[]{:S(2)}, u32[]{:S(2)}) collective-permute-start(f32[64,768]{1,0:T(8,128)S(1)} %get-tuple-element.71), channel_id=1, source_target_pairs={{0,1},{1,0},{2,3},{3,2},{4,7},{5,6},{6,5},{7,4},{8,9},{9,8},{10,11... | collective-permute-start | bytes 589832 | tf_op jit(solution)/shard_map/ppermute | solution.py:340
  82.4 7.2 %collective-permute-start.14 = (f32[72,768]{1,0:T(8,128)S(1)}, f32[72,768]{1,0:T(8,128)S(1)}, u32[]{:S(2)}, u32[]{:S(2)}) collective-permute-start(f32[72,768]{1,0:T(8,128)S(1)} %add.36.a0), channel_id=1, source_target_pairs={{0,3},{1,2},{2,1},{3,0},{4,5},{5,4},{6,7},{7,6},{8,11},{9,10},{10,... | collective-permute-start | bytes 663560 | tf_op jit(solution)/shard_map/ppermute | solution.py:341
  85.6 7.0 %collective-permute-start.17 = (f32[64,768]{1,0:T(8,128)S(1)}, f32[64,768]{1,0:T(8,128)S(1)}, u32[]{:S(2)}, u32[]{:S(2)}) collective-permute-start(f32[64,768]{1,0:T(8,128)S(1)} %add.37.b0), channel_id=1, source_target_pairs={{0,3},{1,2},{2,1},{3,0},{4,5},{5,4},{6,7},{7,6},{8,11},{9,10},{10,... | collective-permute-start | bytes 589832 | tf_op jit(solution)/shard_map/ppermute | solution.py:341
  93.5 1.5 %collective-permute-start.18 = (f32[64,768]{1,0:T(8,128)S(1)}, f32[64,768]{1,0:T(8,128)S(1)}, u32[]{:S(2)}, u32[]{:S(2)}) collective-permute-start(f32[64,768]{1,0:T(8,128)S(1)} %get-tuple-element.75), channel_id=1, source_target_pairs={{0,4},{4,0},{8,12},{12,8},{1,5},{5,1},{9,13},{13,9},{2,6},{6,2},{1... | collective-permute-start | bytes 589832 | tf_op jit(solution)/shard_map/ppermute | solution.py:384
  95.0 7.0 %collective-permute-start.19 = (f32[64,768]{1,0:T(8,128)S(1)}, f32[64,768]{1,0:T(8,128)S(1)}, u32[]{:S(2)}, u32[]{:S(2)}) collective-permute-start(f32[64,768]{1,0:T(8,128)S(1)} %add.38.refs_1_), channel_id=1, source_target_pairs={{0,8},{4,12},{8,0},{12,4},{1,9},{5,13},{9,1},{13,5},{2,10},{6,14},... | collective-permute-start | bytes 589832 | tf_op jit(solution)/shard_map/ppermute | solution.py:386
  (2 other events, 3.4 us)

commit v5 on v4

--- a/solution.py
+++ b/solution.py
@@ -336,9 +336,9 @@
     return [(h * 4 + p, h * 4 + (p ^ (1 if (h + turn) % 2 == 0 else 3))) for h in range(4) for p in range(4)]
 
 
-def page_sum(x, join=jnp.add, held=None):
-    x = join(x if held is None else held, lax.ppermute(x, ("head", "page"), neighbours(0)))
-    return x, lax.ppermute(x, ("head", "page"), neighbours(1))
+def page_sum(x, join=jnp.add, held=None, turn=0):
+    x = join(x if held is None else held, lax.ppermute(x, ("head", "page"), neighbours(turn)))
+    return x, lax.ppermute(x, ("head", "page"), neighbours(turn + 1))
 
 
 def sum_and_top(a, b):
@@ -364,7 +364,7 @@
     wq_high, wq_low = split_weights(w_query[0], dout1[0])
     pack2 = lax.ppermute(pack, "section", back_section)
     e1, dp1, a, b, dout1 = products(dout1, s1, *split1, wq_high)
-    a1, b1 = page_sum(a), page_sum(b)
+    a1, b1 = page_sum(a), page_sum(b, turn=1)
     wo_high, wo_low = split_weights(w_out[0], a1[0])
     keep, send, rows1 = input_gradient(0, a1, b1, grad_in[0], wq_high, wq_low, wo_high)
     part = keep + lax.ppermute(send, "head", swap(1))
@@ -379,7 +379,7 @@
     dout2 = page_sum(part, sum_and_top)
     sums = lax.ppermute(tied(sums, m2), "section", back_section)
     e2, dp2, a, b, dout2 = products(dout2, s2, *split2)
-    a2, b2 = page_sum(a), page_sum(b, lambda x, y: tied(x + y, sums))
+    a2, b2 = page_sum(a), page_sum(b, lambda x, y: tied(x + y, sums), turn=1)
     part, rows2 = input_gradient(1, a2, b2, g2, wq_high, wq_low)
     part = part + lax.ppermute(part, "head", swap(1))
     key_final, value_final = gradient_sums(1, rows2, e2, dp2, dout2, queries, (sums,), part)

time: 103 us -> 99.8 us (0.969)
  starting transfers between devices: 38.6 us -> 30.4 us
  waiting for transfers between devices: 43 us -> 48.1 us
    ppermute x12, starting transfers between devices: 23.5 us -> 15.2 us  [the longest x6 9.21 us: page_sum(): return (x, lax.ppermute(x, ('head', 'page'), neighbours(turn + 1)))]
    ppermute x12, waiting for transfers between devices: 30.3 us -> 35.3 us  [the longest x6 20.8 us: page_sum(): return (x, lax.ppermute(x, ('head', 'page'), neighbours(turn + 1)))]
  transfers between devices with their start and end apart: 20 -> 20, of which waited for: 15 -> 12; matrix products, arithmetic and copies ran while one was open for 0% -> 0% of each run, Pallas kernels for 9% -> 10%
where the time goes in v5:
time: 99.8 us; the launch traced here: 99.6 us
  waiting for transfers between devices  48.1 us (48%)
  starting transfers between devices  30.4 us (30%)
  Pallas kernels  16.8 us (17%)
  between operations  2.32 us (2%)
  other arithmetic  1.06 us (1%)
  local copies, waits for them, and re-layouts  1 us (1%)
    ppermute x6, waiting for transfers between devices, page_sum(): return (x, lax.ppermute(x, ('head', 'page'), neighbours(turn + 1)))  20.8 us
    ppermute x6, waiting for transfers between devices, page_sum(): lax.ppermute(x, ('head', 'page'), neighbours(turn))  14.5 us
    pallas_call x11, Pallas kernels, call(): pl.pallas_call(body, out_shape=[jax.ShapeDtypeStruct(s, d) for s, d in ou...  10.6 us
    ppermute x6, starting transfers between devices, page_sum(): return (x, lax.ppermute(x, ('head', 'page'), neighbours(turn + 1)))  9.21 us
    ppermute x1, starting transfers between devices, per_device(): pack2 = lax.ppermute(pack, 'section', back_section)  8.42 us
    pallas_call x1, Pallas kernels, front(): pl.pallas_call(front_body, out_shape=[jax.ShapeDtypeStruct(s, d) for s, d...  6.2 us
    ppermute x6, starting transfers between devices, page_sum(): lax.ppermute(x, ('head', 'page'), neighbours(turn))  6.02 us
    ppermute x1, waiting for transfers between devices, per_device(): grad_done = part + tied(lax.ppermute(part, 'head', swap(2)), key_final)  4.96 us
  transfers between devices with their start and end apart: 20, of which 12 were waited for; matrix products, arithmetic and copies ran while one was open for 0% of the time, Pallas kernels for 10%

profile of v5, /device:TPU:24, one launch (start us, length us, event | category | flops | bytes accessed | tf_op | source)
XLA Modules:
  0.0 99.6 jit_solution(17756225397579397984)
XLA Ops:
  2.0 6.2 %shard_map.166 = (f32[2,512,192]{2,1,0:T(8,128)}, f32[72,768]{1,0:T(8,128)}, f32[1032,256]{1,0:T(8,128)}, f32[8,256]{1,0:T(8,128)}) custom-call(f32[1,2,64,768]{3,2,1,0:T(8,128)} %q_ref.5, f32[1,512,256]{2,1,0:T(8,128)} %k_hbm.1, f32[1,512,256]{2,1,0:T(8,128)} %v_hbm.1, f32[1,64,768]{2,1,0:T(8,128)} %g_hbm.1, f32[1,768,768]{2,1,0:T(8,128)} %w_hbm.1, ...), custom_call_target="tpu_custom_call" | custom-call | tf_op jit(solution)/shard_map/pallas_call | solution.py:161
  8.2 1.6 %collective-permute-start = (f32[72,768]{1,0:T(8,128)}, f32[72,768]{1,0:T(8,128)S(1)}, u32[]{:S(2)}, u32[]{:S(2)}) collective-permute-start(f32[72,768]{1,0:T(8,128)} %get-tuple-element.43.part_ref), channel_id=1, source_target_pairs={{0,1},{1,0},{2,3},{3,2},{4,7},{5,6},{6,5},{7,4},{8,9},{9,8},{10,11... | collective-permute-start | bytes 663560 | tf_op jit(solution)/shard_map/ppermute | solution.py:340
  9.7 8.4 %collective-permute-start.9 = (f32[1032,256]{1,0:T(8,128)}, f32[1032,256]{1,0:T(8,128)S(1)}, u32[]{:S(2)}, u32[]{:S(2)}) collective-permute-start(f32[1032,256]{1,0:T(8,128)} %get-tuple-element.60), channel_id=1, source_target_pairs={{16,0},{32,16},{48,32},{64,48},{80,64},{96,80},{112,96},{128,112},... | collective-permute-start | bytes 3170312 | tf_op jit(solution)/shard_map/ppermute | solution.py:365
  18.2 0.9 copy-done.11
  19.6 2.2 %collective-permute-start.1 = (f32[72,768]{1,0:T(8,128)S(1)}, f32[72,768]{1,0:T(8,128)S(1)}, u32[]{:S(2)}, u32[]{:S(2)}) collective-permute-start(f32[72,768]{1,0:T(8,128)S(1)} %maximum_select_fusion.1.refs_0_.d0_ref), channel_id=1, source_target_pairs={{0,3},{1,2},{2,1},{3,0},{4,5},{5,4},{6,7},{7,6},{8,11},{9,10},{10,... | collective-permute-start | bytes 663560 | tf_op jit(solution)/shard_map/ppermute | solution.py:341
  22.1 4.7 %collective-permute-done.1.d1_ref = f32[72,768]{1,0:T(8,128)S(1)} collective-permute-done((f32[72,768]{1,0:T(8,128)S(1)}, f32[72,768]{1,0:T(8,128)S(1)}, u32[]{:S(2)}, u32[]{:S(2)}) %collective-permute-start.1) | collective-permute-done | bytes 221216 | tf_op jit(solution)/shard_map/ppermute | solution.py:341
  26.8 1.3 %shard_map.169 = (f32[2,512,192]{2,1,0:T(8,128)S(1)}, f32[2,512,192]{2,1,0:T(8,128)S(1)}, f32[72,768]{1,0:T(8,128)S(1)}, f32[64,768]{1,0:T(8,128)S(1)}, f32[64,768]{1,0:T(8,128)S(1)}) custom-call(f32[72,768]{1,0:T(8,128)S(1)} %maximum_select_fusion.1.refs_0_.d0_ref, f32[72,768]{1,0:T(8,128)S(1)} %collective-permute-done.1.d1_ref, ...), custom_call_target="tpu_custom_call" | custom-call | tf_op jit(solution)/shard_map/pallas_call | solution.py:69
  28.2 2.2 %collective-permute-start.4 = (f32[64,768]{1,0:T(8,128)S(1)}, f32[64,768]{1,0:T(8,128)S(1)}, u32[]{:S(2)}, u32[]{:S(2)}) collective-permute-start(f32[64,768]{1,0:T(8,128)S(1)} %get-tuple-element.50), channel_id=1, source_target_pairs={{0,3},{1,2},{2,1},{3,0},{4,5},{5,4},{6,7},{7,6},{8,11},{9,10},{10,... | collective-permute-start | bytes 589832 | tf_op jit(solution)/shard_map/ppermute | solution.py:340
  30.4 3.7 %collective-permute-done.2 = f32[72,768]{1,0:T(8,128)S(1)} collective-permute-done((f32[72,768]{1,0:T(8,128)S(1)}, f32[72,768]{1,0:T(8,128)S(1)}, u32[]{:S(2)}, u32[]{:S(2)}) %collective-permute-start.2) | collective-permute-done | bytes 221216 | tf_op jit(solution)/shard_map/ppermute | solution.py:340
  34.2 3.4 %collective-permute-start.3 = (f32[72,768]{1,0:T(8,128)S(1)}, f32[72,768]{1,0:T(8,128)S(1)}, u32[]{:S(2)}, u32[]{:S(2)}) collective-permute-start(f32[72,768]{1,0:T(8,128)S(1)} %add.31.refs_0_.a0), channel_id=1, source_target_pairs={{0,3},{1,2},{2,1},{3,0},{4,5},{5,4},{6,7},{7,6},{8,11},{9,10},{10,... | collective-permute-start | bytes 663560 | tf_op jit(solution)/shard_map/ppermute | solution.py:341
  38.2 5.2 %collective-permute-done.5.b1 = f32[64,768]{1,0:T(8,128)S(1)} collective-permute-done((f32[64,768]{1,0:T(8,128)S(1)}, f32[64,768]{1,0:T(8,128)S(1)}, u32[]{:S(2)}, u32[]{:S(2)}) %collective-permute-start.5) | collective-permute-done | bytes 196640 | tf_op jit(solution)/shard_map/ppermute | solution.py:341
  43.4 0.9 shard_map.171
  44.4 1.3 %collective-permute-done.6 = f32[32,768]{1,0:T(8,128)S(1)} collective-permute-done((f32[32,768]{1,0:T(8,128)S(1)}, f32[32,768]{1,0:T(8,128)S(1)}, u32[]{:S(2)}, u32[]{:S(2)}) %collective-permute-start.6) | collective-permute-done | bytes 98336 | tf_op jit(solution)/shard_map/ppermute | solution.py:370
  45.9 1.0 %shard_map.172.refs_0_ = f32[1024,256]{1,0:T(8,128)S(1)} custom-call(f32[8,768]{1,0:T(8,128)S(1)} %get-tuple-element.55.row_ref, f32[2,512,192]{2,1,0:T(8,128)S(1)} %get-tuple-element.56.e_ref, f32[2,512,192]{2,1,0:T(8,128)S(1)} %get-tuple-element.57.dp_ref, f32[64,768]{1,0:T(8,128)S(1)} %get-tuple-element.58.dout_ref, f32[1,2,64,768]{3,2,1,0:T(8,128)S(1)} %copy-done.1, ...), custom_call_target="tpu_custom_call" | custom-call | tf_op jit(solution)/shard_map/pallas_call | solution.py:69
  46.9 3.7 %collective-permute-done.7 = f32[32,768]{1,0:T(8,128)S(1)} collective-permute-done((f32[32,768]{1,0:T(8,128)S(1)}, f32[32,768]{1,0:T(8,128)S(1)}, u32[]{:S(2)}, u32[]{:S(2)}) %collective-permute-start.7) | collective-permute-done | bytes 98336 | tf_op jit(solution)/shard_map/ppermute | solution.py:372
  50.7 3.2 %collective-permute-start.8 = (f32[32,768]{1,0:T(8,128)S(1)}, f32[32,768]{1,0:T(8,128)S(1)}, u32[]{:S(2)}, u32[]{:S(2)}) collective-permute-start(f32[32,768]{1,0:T(8,128)S(1)} %add.34.refs_0_), channel_id=1, source_target_pairs={{16,0},{32,16},{48,32},{64,48},{80,64},{96,80},{112,96},{128,112},... | collective-permute-start | bytes 294920 | tf_op jit(solution)/shard_map/ppermute | solution.py:373
  53.9 1.3 %shard_map.173 = (f32[2,512,192]{2,1,0:T(8,128)S(1)}, f32[8,768]{1,0:T(8,128)S(1)}, bf16[2,256,512]{2,1,0:T(8,128)(2,1)S(1)}, bf16[512,512]{1,0:T(8,128)(2,1)S(1)}, f32[64,768]{1,0:T(8,128)S(1)}) custom-call(f32[1,2,64,768]{3,2,1,0:T(8,128)S(1)} %copy-done.1, f32[1032,256]{1,0:T(8,128)S(1)} %collective-permute-done.9.pack_ref, f32[512,256]{1,0:T(8,128)S(1)} %copy-done.9, ...), custom_call_target="tpu_custom_call" | custom-call | tf_op jit(solution)/shard_map/pallas_call | solution.py:69
  55.2 3.1 %collective-permute-start.16 = (f32[1024,256]{1,0:T(8,128)S(1)}, f32[1024,256]{1,0:T(8,128)S(1)}, u32[]{:S(2)}, u32[]{:S(2)}) collective-permute-start(f32[1024,256]{1,0:T(8,128)S(1)} %shard_map.172.refs_0_), channel_id=1, source_target_pairs={{16,0},{32,16},{48,32},{64,48},{80,64},{96,80},{112,96},{128,112},... | collective-permute-start | bytes 3145736 | tf_op jit(solution)/shard_map/ppermute | solution.py:380
  58.5 1.3 %collective-permute-done.10.other_ref = f32[32,768]{1,0:T(8,128)S(1)} collective-permute-done((f32[32,768]{1,0:T(8,128)S(1)}, f32[32,768]{1,0:T(8,128)S(1)}, u32[]{:S(2)}, u32[]{:S(2)}) %collective-permute-start.10) | collective-permute-done | bytes 98336 | tf_op jit(solution)/shard_map/ppermute | solution.py:376
  59.7 0.8 shard_map.174
  60.7 5.9 %collective-permute-done.11 = f32[72,768]{1,0:T(8,128)S(1)} collective-permute-done((f32[72,768]{1,0:T(8,128)S(1)}, f32[72,768]{1,0:T(8,128)S(1)}, u32[]{:S(2)}, u32[]{:S(2)}) %collective-permute-start.11) | collective-permute-done | bytes 221216 | tf_op jit(solution)/shard_map/ppermute | solution.py:340
  66.7 2.0 %collective-permute-start.12 = (f32[72,768]{1,0:T(8,128)S(1)}, f32[72,768]{1,0:T(8,128)S(1)}, u32[]{:S(2)}, u32[]{:S(2)}) collective-permute-start(f32[72,768]{1,0:T(8,128)S(1)} %maximum_select_fusion.d0_ref), channel_id=1, source_target_pairs={{0,3},{1,2},{2,1},{3,0},{4,5},{5,4},{6,7},{7,6},{8,11},{9,10},{10,... | collective-permute-start | bytes 663560 | tf_op jit(solution)/shard_map/ppermute | solution.py:341
  68.7 5.2 %collective-permute-done.12.d1_ref = f32[72,768]{1,0:T(8,128)S(1)} collective-permute-done((f32[72,768]{1,0:T(8,128)S(1)}, f32[72,768]{1,0:T(8,128)S(1)}, u32[]{:S(2)}, u32[]{:S(2)}) %collective-permute-start.12) | collective-permute-done | bytes 221216 | tf_op jit(solution)/shard_map/ppermute | solution.py:341
  73.9 1.3 %shard_map.175 = (f32[2,512,192]{2,1,0:T(8,128)S(1)}, f32[2,512,192]{2,1,0:T(8,128)S(1)}, f32[72,768]{1,0:T(8,128)S(1)}, f32[64,768]{1,0:T(8,128)S(1)}, f32[64,768]{1,0:T(8,128)S(1)}) custom-call(f32[72,768]{1,0:T(8,128)S(1)} %maximum_select_fusion.d0_ref, f32[72,768]{1,0:T(8,128)S(1)} %collective-permute-done.12.d1_ref, ...), custom_call_target="tpu_custom_call" | custom-call | tf_op jit(solution)/shard_map/pallas_call | solution.py:69
  75.4 2.0 %collective-permute-start.15 = (f32[64,768]{1,0:T(8,128)S(1)}, f32[64,768]{1,0:T(8,128)S(1)}, u32[]{:S(2)}, u32[]{:S(2)}) collective-permute-start(f32[64,768]{1,0:T(8,128)S(1)} %get-tuple-element.71), channel_id=1, source_target_pairs={{0,3},{1,2},{2,1},{3,0},{4,5},{5,4},{6,7},{7,6},{8,11},{9,10},{10,... | collective-permute-start | bytes 589832 | tf_op jit(solution)/shard_map/ppermute | solution.py:340
  77.3 4.8 %collective-permute-done.13 = f32[72,768]{1,0:T(8,128)S(1)} collective-permute-done((f32[72,768]{1,0:T(8,128)S(1)}, f32[72,768]{1,0:T(8,128)S(1)}, u32[]{:S(2)}, u32[]{:S(2)}) %collective-permute-start.13) | collective-permute-done | bytes 221216 | tf_op jit(solution)/shard_map/ppermute | solution.py:340
  82.2 1.4 %collective-permute-start.14 = (f32[72,768]{1,0:T(8,128)S(1)}, f32[72,768]{1,0:T(8,128)S(1)}, u32[]{:S(2)}, u32[]{:S(2)}) collective-permute-start(f32[72,768]{1,0:T(8,128)S(1)} %add.36.a0), channel_id=1, source_target_pairs={{0,3},{1,2},{2,1},{3,0},{4,5},{5,4},{6,7},{7,6},{8,11},{9,10},{10,... | collective-permute-start | bytes 663560 | tf_op jit(solution)/shard_map/ppermute | solution.py:341
  83.8 5.7 %collective-permute-done.14.a1 = f32[72,768]{1,0:T(8,128)S(1)} collective-permute-done((f32[72,768]{1,0:T(8,128)S(1)}, f32[72,768]{1,0:T(8,128)S(1)}, u32[]{:S(2)}, u32[]{:S(2)}) %collective-permute-start.14) | collective-permute-done | bytes 221216 | tf_op jit(solution)/shard_map/ppermute | solution.py:341
  89.4 0.9 shard_map.176
  90.4 1.4 %collective-permute-done.18 = f32[64,768]{1,0:T(8,128)S(1)} collective-permute-done((f32[64,768]{1,0:T(8,128)S(1)}, f32[64,768]{1,0:T(8,128)S(1)}, u32[]{:S(2)}, u32[]{:S(2)}) %collective-permute-start.18) | collective-permute-done | bytes 196640 | tf_op jit(solution)/shard_map/ppermute | solution.py:384
  92.0 2.0 %shard_map.177 = (f32[512,256]{1,0:T(8,128)}, f32[512,256]{1,0:T(8,128)}) custom-call(f32[8,768]{1,0:T(8,128)S(1)} %get-tuple-element.76.row_ref, f32[2,512,192]{2,1,0:T(8,128)S(1)} %get-tuple-element.77.e_ref, f32[2,512,192]{2,1,0:T(8,128)S(1)} %get-tuple-element.78.dp_ref, f32[64,768]{1,0:T(8,128)S(1)} %get-tuple-element.79.dout_ref, ...), custom_call_target="tpu_custom_call" | custom-call | tf_op jit(solution)/shard_map/pallas_call | solution.py:69
  94.0 5.0 %collective-permute-done.19 = f32[64,768]{1,0:T(8,128)S(1)} collective-permute-done((f32[64,768]{1,0:T(8,128)S(1)}, f32[64,768]{1,0:T(8,128)S(1)}, u32[]{:S(2)}, u32[]{:S(2)}) %collective-permute-start.19) | collective-permute-done | bytes 196640 | tf_op jit(solution)/shard_map/ppermute | solution.py:386
  (59 shorter events, 3.1 us)
Async XLA Ops:
  1.9 16.2 %copy-start.3 = (f32[1,512,256]{2,1,0:T(8,128)S(1)}, f32[1,512,256]{2,1,0:T(8,128)}, u32[]{:S(2)}) copy-start(f32[1,512,256]{2,1,0:T(8,128)} %k_hbm.1) | copy-start | bytes 1572868
  1.9 16.2 %copy-start.4 = (f32[1,512,256]{2,1,0:T(8,128)S(1)}, f32[1,512,256]{2,1,0:T(8,128)}, u32[]{:S(2)}) copy-start(f32[1,512,256]{2,1,0:T(8,128)} %v_hbm.1) | copy-start | bytes 1572868
  1.9 19.8 %copy-start.2 = (f32[1,768,768]{2,1,0:T(8,128)S(1)}, f32[1,768,768]{2,1,0:T(8,128)}, u32[]{:S(2)}) copy-start(f32[1,768,768]{2,1,0:T(8,128)} %param.28) | copy-start | bytes 7077892
  8.2 11.3 %collective-permute-start = (f32[72,768]{1,0:T(8,128)}, f32[72,768]{1,0:T(8,128)S(1)}, u32[]{:S(2)}, u32[]{:S(2)}) collective-permute-start(f32[72,768]{1,0:T(8,128)} %get-tuple-element.43.part_ref), channel_id=1, source_target_pairs={{0,1},{1,0},{2,3},{3,2},{4,7},{5,6},{6,5},{7,4},{8,9},{9,8},{10,11... | collective-permute-start | bytes 663560 | tf_op jit(solution)/shard_map/ppermute | solution.py:340
  9.7 44.2 %collective-permute-start.9 = (f32[1032,256]{1,0:T(8,128)}, f32[1032,256]{1,0:T(8,128)S(1)}, u32[]{:S(2)}, u32[]{:S(2)}) collective-permute-start(f32[1032,256]{1,0:T(8,128)} %get-tuple-element.60), channel_id=1, source_target_pairs={{16,0},{32,16},{48,32},{64,48},{80,64},{96,80},{112,96},{128,112},... | collective-permute-start | bytes 3170312 | tf_op jit(solution)/shard_map/ppermute | solution.py:365
  19.6 7.2 %collective-permute-start.1 = (f32[72,768]{1,0:T(8,128)S(1)}, f32[72,768]{1,0:T(8,128)S(1)}, u32[]{:S(2)}, u32[]{:S(2)}) collective-permute-start(f32[72,768]{1,0:T(8,128)S(1)} %maximum_select_fusion.1.refs_0_.d0_ref), channel_id=1, source_target_pairs={{0,3},{1,2},{2,1},{3,0},{4,5},{5,4},{6,7},{7,6},{8,11},{9,10},{10,... | collective-permute-start | bytes 663560 | tf_op jit(solution)/shard_map/ppermute | solution.py:341
  21.7 5.0 %copy-start.5 = (f32[2,512,192]{2,1,0:T(8,128)S(1)}, f32[2,512,192]{2,1,0:T(8,128)}, u32[]{:S(2)}) copy-start(f32[2,512,192]{2,1,0:T(8,128)} %get-tuple-element.45.s_ref) | copy-start | bytes 2359300
  26.8 11.0 %copy-start = (f32[1,768,768]{2,1,0:T(8,128)S(1)}, f32[1,768,768]{2,1,0:T(8,128)}, u32[]{:S(2)}) copy-start(f32[1,768,768]{2,1,0:T(8,128)} %w_hbm.1) | copy-start | bytes 7077892
  28.1 6.0 %collective-permute-start.2 = (f32[72,768]{1,0:T(8,128)S(1)}, f32[72,768]{1,0:T(8,128)S(1)}, u32[]{:S(2)}, u32[]{:S(2)}) collective-permute-start(f32[72,768]{1,0:T(8,128)S(1)} %get-tuple-element.49), channel_id=1, source_target_pairs={{0,1},{1,0},{2,3},{3,2},{4,7},{5,6},{6,5},{7,4},{8,9},{9,8},{10,11... | collective-permute-start | bytes 663560 | tf_op jit(solution)/shard_map/ppermute | solution.py:340
  28.2 9.4 %collective-permute-start.4 = (f32[64,768]{1,0:T(8,128)S(1)}, f32[64,768]{1,0:T(8,128)S(1)}, u32[]{:S(2)}, u32[]{:S(2)}) collective-permute-start(f32[64,768]{1,0:T(8,128)S(1)} %get-tuple-element.50), channel_id=1, source_target_pairs={{0,3},{1,2},{2,1},{3,0},{4,5},{5,4},{6,7},{7,6},{8,11},{9,10},{10,... | collective-permute-start | bytes 589832 | tf_op jit(solution)/shard_map/ppermute | solution.py:340
  34.2 9.2 %collective-permute-start.3 = (f32[72,768]{1,0:T(8,128)S(1)}, f32[72,768]{1,0:T(8,128)S(1)}, u32[]{:S(2)}, u32[]{:S(2)}) collective-permute-start(f32[72,768]{1,0:T(8,128)S(1)} %add.31.refs_0_.a0), channel_id=1, source_target_pairs={{0,3},{1,2},{2,1},{3,0},{4,5},{5,4},{6,7},{7,6},{8,11},{9,10},{10,... | collective-permute-start | bytes 663560 | tf_op jit(solution)/shard_map/ppermute | solution.py:341
  37.6 5.8 %collective-permute-start.5 = (f32[64,768]{1,0:T(8,128)S(1)}, f32[64,768]{1,0:T(8,128)S(1)}, u32[]{:S(2)}, u32[]{:S(2)}) collective-permute-start(f32[64,768]{1,0:T(8,128)S(1)} %add.32.b0), channel_id=1, source_target_pairs={{0,1},{1,0},{2,3},{3,2},{4,7},{5,6},{6,5},{7,4},{8,9},{9,8},{10,11... | collective-permute-start | bytes 589832 | tf_op jit(solution)/shard_map/ppermute | solution.py:341
  37.8 5.7 %copy-start.6 = (f32[1,64,768]{2,1,0:T(8,128)S(1)}, f32[1,64,768]{2,1,0:T(8,128)}, u32[]{:S(2)}) copy-start(f32[1,64,768]{2,1,0:T(8,128)} %g_hbm.1) | copy-start | bytes 589828
  43.4 2.4 %copy-start.7 = (f32[1,512,256]{2,1,0:T(8,128)S(1)}, f32[1,512,256]{2,1,0:T(8,128)}, u32[]{:S(2)}) copy-start(f32[1,512,256]{2,1,0:T(8,128)} %refs_0_.1) | copy-start | bytes 1572868
  43.4 2.4 %copy-start.8 = (f32[1,512,256]{2,1,0:T(8,128)S(1)}, f32[1,512,256]{2,1,0:T(8,128)}, u32[]{:S(2)}) copy-start(f32[1,512,256]{2,1,0:T(8,128)} %refs_1_.1) | copy-start | bytes 1572868
  44.3 1.4 %collective-permute-start.6 = (f32[32,768]{1,0:T(8,128)S(1)}, f32[32,768]{1,0:T(8,128)S(1)}, u32[]{:S(2)}, u32[]{:S(2)}) collective-permute-start(f32[32,768]{1,0:T(8,128)S(1)} %get-tuple-element.54), channel_id=1, source_target_pairs={{0,4},{4,0},{8,12},{12,8},{1,5},{5,1},{9,13},{13,9},{2,6},{6,2},{1... | collective-permute-start | bytes 294920 | tf_op jit(solution)/shard_map/ppermute | solution.py:370
  45.8 4.9 %collective-permute-start.7 = (f32[32,768]{1,0:T(8,128)S(1)}, f32[32,768]{1,0:T(8,128)S(1)}, u32[]{:S(2)}, u32[]{:S(2)}) collective-permute-start(f32[32,768]{1,0:T(8,128)S(1)} %add.33.refs_2_), channel_id=1, source_target_pairs={{0,8},{4,12},{8,0},{12,4},{1,9},{5,13},{9,1},{13,5},{2,10},{6,14},... | collective-permute-start | bytes 294920 | tf_op jit(solution)/shard_map/ppermute | solution.py:372
  45.9 8.0 %copy-start.9 = (f32[512,256]{1,0:T(8,128)S(1)}, f32[512,256]{1,0:T(8,128)}, u32[]{:S(2)}) copy-start(f32[512,256]{1,0:T(8,128)} %k_ref.1) | copy-start | bytes 1572868
  45.9 8.0 %copy-start.10 = (f32[512,256]{1,0:T(8,128)S(1)}, f32[512,256]{1,0:T(8,128)}, u32[]{:S(2)}) copy-start(f32[512,256]{1,0:T(8,128)} %v_ref.1) | copy-start | bytes 1572868
  45.9 8.0 %copy-start.12 = (f32[64,768]{1,0:T(8,128)S(1)}, f32[64,768]{1,0:T(8,128)}, u32[]{:S(2)}) copy-start(f32[64,768]{1,0:T(8,128)} %grad_ref.1) | copy-start | bytes 589828
  45.9 8.0 %copy-start.13 = (f32[8,256]{1,0:T(8,128)S(1)}, f32[8,256]{1,0:T(8,128)}, u32[]{:S(2)}) copy-start(f32[8,256]{1,0:T(8,128)} %get-tuple-element.61.bounds_ref) | copy-start | bytes 24580
  50.7 7.6 %collective-permute-start.8 = (f32[32,768]{1,0:T(8,128)S(1)}, f32[32,768]{1,0:T(8,128)S(1)}, u32[]{:S(2)}, u32[]{:S(2)}) collective-permute-start(f32[32,768]{1,0:T(8,128)S(1)} %add.34.refs_0_), channel_id=1, source_target_pairs={{16,0},{32,16},{48,32},{64,48},{80,64},{96,80},{112,96},{128,112},... | collective-permute-start | bytes 294920 | tf_op jit(solution)/shard_map/ppermute | solution.py:373
  55.2 28.5 %collective-permute-start.16 = (f32[1024,256]{1,0:T(8,128)S(1)}, f32[1024,256]{1,0:T(8,128)S(1)}, u32[]{:S(2)}, u32[]{:S(2)}) collective-permute-start(f32[1024,256]{1,0:T(8,128)S(1)} %shard_map.172.refs_0_), channel_id=1, source_target_pairs={{16,0},{32,16},{48,32},{64,48},{80,64},{96,80},{112,96},{128,112},... | collective-permute-start | bytes 3145736 | tf_op jit(solution)/shard_map/ppermute | solution.py:380
  58.4 1.4 %collective-permute-start.10 = (f32[32,768]{1,0:T(8,128)S(1)}, f32[32,768]{1,0:T(8,128)S(1)}, u32[]{:S(2)}, u32[]{:S(2)}) collective-permute-start(f32[32,768]{1,0:T(8,128)S(1)} %collective-permute-done.8.mine_ref), channel_id=1, source_target_pairs={{0,4},{4,0},{8,12},{12,8},{1,5},{5,1},{9,13},{13,9},{2,6},{6,2},{1... | collective-permute-start | bytes 294920 | tf_op jit(solution)/shard_map/ppermute | solution.py:376
  60.6 6.0 %collective-permute-start.11 = (f32[72,768]{1,0:T(8,128)S(1)}, f32[72,768]{1,0:T(8,128)S(1)}, u32[]{:S(2)}, u32[]{:S(2)}) collective-permute-start(f32[72,768]{1,0:T(8,128)S(1)} %get-tuple-element.66), channel_id=1, source_target_pairs={{0,1},{1,0},{2,3},{3,2},{4,7},{5,6},{6,5},{7,4},{8,9},{9,8},{10,11... | collective-permute-start | bytes 663560 | tf_op jit(solution)/shard_map/ppermute | solution.py:340
  66.7 7.2 %collective-permute-start.12 = (f32[72,768]{1,0:T(8,128)S(1)}, f32[72,768]{1,0:T(8,128)S(1)}, u32[]{:S(2)}, u32[]{:S(2)}) collective-permute-start(f32[72,768]{1,0:T(8,128)S(1)} %maximum_select_fusion.d0_ref), channel_id=1, source_target_pairs={{0,3},{1,2},{2,1},{3,0},{4,5},{5,4},{6,7},{7,6},{8,11},{9,10},{10,... | collective-permute-start | bytes 663560 | tf_op jit(solution)/shard_map/ppermute | solution.py:341
  75.3 6.9 %collective-permute-start.13 = (f32[72,768]{1,0:T(8,128)S(1)}, f32[72,768]{1,0:T(8,128)S(1)}, u32[]{:S(2)}, u32[]{:S(2)}) collective-permute-start(f32[72,768]{1,0:T(8,128)S(1)} %get-tuple-element.70), channel_id=1, source_target_pairs={{0,1},{1,0},{2,3},{3,2},{4,7},{5,6},{6,5},{7,4},{8,9},{9,8},{10,11... | collective-permute-start | bytes 663560 | tf_op jit(solution)/shard_map/ppermute | solution.py:340
  75.4 8.3 %collective-permute-start.15 = (f32[64,768]{1,0:T(8,128)S(1)}, f32[64,768]{1,0:T(8,128)S(1)}, u32[]{:S(2)}, u32[]{:S(2)}) collective-permute-start(f32[64,768]{1,0:T(8,128)S(1)} %get-tuple-element.71), channel_id=1, source_target_pairs={{0,3},{1,2},{2,1},{3,0},{4,5},{5,4},{6,7},{7,6},{8,11},{9,10},{10,... | collective-permute-start | bytes 589832 | tf_op jit(solution)/shard_map/ppermute | solution.py:340
  82.2 7.2 %collective-permute-start.14 = (f32[72,768]{1,0:T(8,128)S(1)}, f32[72,768]{1,0:T(8,128)S(1)}, u32[]{:S(2)}, u32[]{:S(2)}) collective-permute-start(f32[72,768]{1,0:T(8,128)S(1)} %add.36.a0), channel_id=1, source_target_pairs={{0,3},{1,2},{2,1},{3,0},{4,5},{5,4},{6,7},{7,6},{8,11},{9,10},{10,... | collective-permute-start | bytes 663560 | tf_op jit(solution)/shard_map/ppermute | solution.py:341
  83.7 5.8 %collective-permute-start.17 = (f32[64,768]{1,0:T(8,128)S(1)}, f32[64,768]{1,0:T(8,128)S(1)}, u32[]{:S(2)}, u32[]{:S(2)}) collective-permute-start(f32[64,768]{1,0:T(8,128)S(1)} %add.37.b0), channel_id=1, source_target_pairs={{0,1},{1,0},{2,3},{3,2},{4,7},{5,6},{6,5},{7,4},{8,9},{9,8},{10,11... | collective-permute-start | bytes 589832 | tf_op jit(solution)/shard_map/ppermute | solution.py:341
  90.3 1.5 %collective-permute-start.18 = (f32[64,768]{1,0:T(8,128)S(1)}, f32[64,768]{1,0:T(8,128)S(1)}, u32[]{:S(2)}, u32[]{:S(2)}) collective-permute-start(f32[64,768]{1,0:T(8,128)S(1)} %get-tuple-element.75), channel_id=1, source_target_pairs={{0,4},{4,0},{8,12},{12,8},{1,5},{5,1},{9,13},{13,9},{2,6},{6,2},{1... | collective-permute-start | bytes 589832 | tf_op jit(solution)/shard_map/ppermute | solution.py:384
  91.9 7.0 %collective-permute-start.19 = (f32[64,768]{1,0:T(8,128)S(1)}, f32[64,768]{1,0:T(8,128)S(1)}, u32[]{:S(2)}, u32[]{:S(2)}) collective-permute-start(f32[64,768]{1,0:T(8,128)S(1)} %add.38.refs_1_), channel_id=1, source_target_pairs={{0,8},{4,12},{8,0},{12,4},{1,9},{5,13},{9,1},{13,5},{2,10},{6,14},... | collective-permute-start | bytes 589832 | tf_op jit(solution)/shard_map/ppermute | solution.py:386
  (2 other events, 3.4 us)

commit v6 on v5

--- a/solution.py
+++ b/solution.py
@@ -341,6 +341,15 @@
     return x, lax.ppermute(x, ("head", "page"), neighbours(turn + 1))
 
 
+def page_sum_halves(x, join, held=None):
+    half = WIDE // 2
+    parts = []
+    for turn in (0, 1):
+        cols = slice(turn * half, (turn + 1) * half)
+        parts.append(page_sum(x[:, cols], join, None if held is None else held[:, cols], turn))
+    return [jnp.concatenate([left, right], 1) for left, right in zip(*parts)]
+
+
 def sum_and_top(a, b):
     rows = lax.broadcasted_iota(jnp.int32, a.shape, 0)
     return jnp.where(rows < Q, a + b, jnp.maximum(a, b))
@@ -360,7 +369,7 @@
         queries, key_cache, value_cache, grad_in, w_out, page_table[0], offsets, page_fresh, offset_fresh
     )
     *split1, near = caches(key_cache[0], value_cache[0], part)
-    dout1 = page_sum(part, sum_and_top, near)
+    dout1 = page_sum_halves(part, sum_and_top, near)
     wq_high, wq_low = split_weights(w_query[0], dout1[0])
     pack2 = lax.ppermute(pack, "section", back_section)
     e1, dp1, a, b, dout1 = products(dout1, s1, *split1, wq_high)
@@ -376,7 +385,7 @@
     other = lax.ppermute(mine, "head", swap(1))
 
     part, g2 = dout_second((mine, other), fresh, m2, wo_high, wo_low, sums)
-    dout2 = page_sum(part, sum_and_top)
+    dout2 = page_sum_halves(part, sum_and_top)
     sums = lax.ppermute(tied(sums, m2), "section", back_section)
     e2, dp2, a, b, dout2 = products(dout2, s2, *split2)
     a2, b2 = page_sum(a), page_sum(b, lambda x, y: tied(x + y, sums), turn=1)

time: 99.8 us -> 108 us (1.082)
  starting transfers between devices: 30.4 us -> 36.8 us
    ppermute x6 -> x8, starting transfers between devices: 6.02 us -> 9.35 us  [page_sum(): lax.ppermute(x, ('head', 'page'), neighbours(turn))]
    ppermute x1, starting transfers between devices: 3.12 us -> 6.21 us  [per_device(): sums = lax.ppermute(tied(sums, m2), 'section', back_section)]
    ppermute x1, waiting for transfers between devices: 0.01 us -> 2.39 us  [per_device(): mine = lax.ppermute(tied(part, sums), 'section', back_section)]
    ppermute x1, waiting for transfers between devices: 1.29 us -> 0.01 us  [per_device(): other = lax.ppermute(mine, 'head', swap(1))]
    ppermute x6 -> x8, waiting for transfers between devices: 14.5 us -> 13.8 us  [page_sum(): lax.ppermute(x, ('head', 'page'), neighbours(turn))]
    ppermute x6 -> x8, starting transfers between devices: 9.21 us -> 9.61 us  [page_sum(): return (x, lax.ppermute(x, ('head', 'page'), neighbours(turn + 1)))]
    ppermute x6 -> x8, waiting for transfers between devices: 20.8 us -> 20.8 us  [page_sum(): return (x, lax.ppermute(x, ('head', 'page'), neighbours(turn + 1)))]
  transfers between devices with their start and end apart: 20 -> 24, of which waited for: 12 -> 14; matrix products, arithmetic and copies ran while one was open for 0% -> 0% of each run, Pallas kernels for 10% -> 9%
where the time goes in v6:
time: 108 us; the launch traced here: 107 us
  waiting for transfers between devices  48.4 us (45%)
  starting transfers between devices  36.8 us (34%)
  Pallas kernels  16.7 us (15%)
  between operations  2.36 us (2%)
  local copies, waits for them, and re-layouts  1.99 us (2%)
  other arithmetic  1.13 us (1%)
    ppermute x8, waiting for transfers between devices, page_sum(): return (x, lax.ppermute(x, ('head', 'page'), neighbours(turn + 1)))  20.8 us
    ppermute x8, waiting for transfers between devices, page_sum(): lax.ppermute(x, ('head', 'page'), neighbours(turn))  13.8 us
    pallas_call x11, Pallas kernels, call(): pl.pallas_call(body, out_shape=[jax.ShapeDtypeStruct(s, d) for s, d in ou...  10.6 us
    ppermute x8, starting transfers between devices, page_sum(): return (x, lax.ppermute(x, ('head', 'page'), neighbours(turn + 1)))  9.61 us
    ppermute x8, starting transfers between devices, page_sum(): lax.ppermute(x, ('head', 'page'), neighbours(turn))  9.35 us
    ppermute x1, starting transfers between devices, per_device(): pack2 = lax.ppermute(pack, 'section', back_section)  8.42 us
    ppermute x1, starting transfers between devices, per_device(): sums = lax.ppermute(tied(sums, m2), 'section', back_section)  6.21 us
    pallas_call x1, Pallas kernels, front(): pl.pallas_call(front_body, out_shape=[jax.ShapeDtypeStruct(s, d) for s, d...  6.02 us
  transfers between devices with their start and end apart: 24, of which 14 were waited for; matrix products, arithmetic and copies ran while one was open for 0% of the time, Pallas kernels for 9%

profile of v6, /device:TPU:24, one launch (start us, length us, event | category | flops | bytes accessed | tf_op | source)
XLA Modules:
  0.0 107.3 jit_solution(4383590480040597874)
XLA Ops:
  1.9 6.0 %shard_map.166 = (f32[2,512,192]{2,1,0:T(8,128)}, f32[72,768]{1,0:T(8,128)}, f32[1032,256]{1,0:T(8,128)}, f32[8,256]{1,0:T(8,128)}) custom-call(f32[1,2,64,768]{3,2,1,0:T(8,128)} %q_ref.5, f32[1,512,256]{2,1,0:T(8,128)} %k_hbm.1, f32[1,512,256]{2,1,0:T(8,128)} %v_hbm.1, f32[1,64,768]{2,1,0:T(8,128)} %g_hbm.1, f32[1,768,768]{2,1,0:T(8,128)} %w_hbm.1, ...), custom_call_target="tpu_custom_call" | custom-call | tf_op jit(solution)/shard_map/pallas_call | solution.py:161
  8.0 1.0 fusion.1
  8.9 1.6 %collective-permute-start = (f32[72,384]{1,0:T(8,128)S(1)}, f32[72,384]{1,0:T(8,128)S(1)}, u32[]{:S(2)}, u32[]{:S(2)}) collective-permute-start(f32[72,384]{1,0:T(8,128)S(1)} %get-tuple-element.89), channel_id=1, source_target_pairs={{0,1},{1,0},{2,3},{3,2},{4,7},{5,6},{6,5},{7,4},{8,9},{9,8},{10,11... | collective-permute-start | bytes 331784 | tf_op jit(solution)/shard_map/ppermute | solution.py:340
  10.5 2.1 %collective-permute-start.1 = (f32[72,384]{1,0:T(8,128)S(1)}, f32[72,384]{1,0:T(8,128)S(1)}, u32[]{:S(2)}, u32[]{:S(2)}) collective-permute-start(f32[72,384]{1,0:T(8,128)S(1)} %get-tuple-element.90), channel_id=1, source_target_pairs={{0,3},{1,2},{2,1},{3,0},{4,5},{5,4},{6,7},{7,6},{8,11},{9,10},{10,... | collective-permute-start | bytes 331784 | tf_op jit(solution)/shard_map/ppermute | solution.py:340
  12.6 8.4 %collective-permute-start.11 = (f32[1032,256]{1,0:T(8,128)}, f32[1032,256]{1,0:T(8,128)S(1)}, u32[]{:S(2)}, u32[]{:S(2)}) collective-permute-start(f32[1032,256]{1,0:T(8,128)} %get-tuple-element.60), channel_id=1, source_target_pairs={{16,0},{32,16},{48,32},{64,48},{80,64},{96,80},{112,96},{128,112},... | collective-permute-start | bytes 3170312 | tf_op jit(solution)/shard_map/ppermute | solution.py:374
  22.5 1.2 %collective-permute-start.2 = (f32[72,384]{1,0:T(8,128)S(1)}, f32[72,384]{1,0:T(8,128)S(1)}, u32[]{:S(2)}, u32[]{:S(2)}) collective-permute-start(f32[72,384]{1,0:T(8,128)S(1)} %get-tuple-element.85), channel_id=1, source_target_pairs={{0,3},{1,2},{2,1},{3,0},{4,5},{5,4},{6,7},{7,6},{8,11},{9,10},{10,... | collective-permute-start | bytes 331784 | tf_op jit(solution)/shard_map/ppermute | solution.py:341
  24.1 4.5 %collective-permute-done.2 = f32[72,384]{1,0:T(8,128)S(1)} collective-permute-done((f32[72,384]{1,0:T(8,128)S(1)}, f32[72,384]{1,0:T(8,128)S(1)}, u32[]{:S(2)}, u32[]{:S(2)}) %collective-permute-start.2) | collective-permute-done | bytes 110624 | tf_op jit(solution)/shard_map/ppermute | solution.py:341
  28.7 1.3 %shard_map.169 = (f32[2,512,192]{2,1,0:T(8,128)S(1)}, f32[2,512,192]{2,1,0:T(8,128)S(1)}, f32[72,768]{1,0:T(8,128)S(1)}, f32[64,768]{1,0:T(8,128)S(1)}, f32[64,768]{1,0:T(8,128)S(1)}) custom-call(f32[72,768]{1,0:T(8,128)S(1)} %pad_maximum_fusion.refs_0_.d0_ref, f32[72,768]{1,0:T(8,128)S(1)} %pad_maximum_fusion.1.d1_ref, f32[2,512,192]{2,1,0:T(8,128)S(1)} %copy-done.5, ...), custom_call_target="tpu_custom_call" | custom-call | tf_op jit(solution)/shard_map/pallas_call | solution.py:69
  30.1 2.0 %collective-permute-start.6 = (f32[64,768]{1,0:T(8,128)S(1)}, f32[64,768]{1,0:T(8,128)S(1)}, u32[]{:S(2)}, u32[]{:S(2)}) collective-permute-start(f32[64,768]{1,0:T(8,128)S(1)} %get-tuple-element.50), channel_id=1, source_target_pairs={{0,3},{1,2},{2,1},{3,0},{4,5},{5,4},{6,7},{7,6},{8,11},{9,10},{10,... | collective-permute-start | bytes 589832 | tf_op jit(solution)/shard_map/ppermute | solution.py:340
  32.1 4.2 %collective-permute-done.4 = f32[72,768]{1,0:T(8,128)S(1)} collective-permute-done((f32[72,768]{1,0:T(8,128)S(1)}, f32[72,768]{1,0:T(8,128)S(1)}, u32[]{:S(2)}, u32[]{:S(2)}) %collective-permute-start.4) | collective-permute-done | bytes 221216 | tf_op jit(solution)/shard_map/ppermute | solution.py:340
  36.4 3.9 %collective-permute-start.5 = (f32[72,768]{1,0:T(8,128)S(1)}, f32[72,768]{1,0:T(8,128)S(1)}, u32[]{:S(2)}, u32[]{:S(2)}) collective-permute-start(f32[72,768]{1,0:T(8,128)S(1)} %add.38.refs_0_.a0), channel_id=1, source_target_pairs={{0,3},{1,2},{2,1},{3,0},{4,5},{5,4},{6,7},{7,6},{8,11},{9,10},{10,... | collective-permute-start | bytes 663560 | tf_op jit(solution)/shard_map/ppermute | solution.py:341
  40.8 5.2 %collective-permute-done.7.b1 = f32[64,768]{1,0:T(8,128)S(1)} collective-permute-done((f32[64,768]{1,0:T(8,128)S(1)}, f32[64,768]{1,0:T(8,128)S(1)}, u32[]{:S(2)}, u32[]{:S(2)}) %collective-permute-start.7) | collective-permute-done | bytes 196640 | tf_op jit(solution)/shard_map/ppermute | solution.py:341
  47.1 1.3 %collective-permute-done.8 = f32[32,768]{1,0:T(8,128)S(1)} collective-permute-done((f32[32,768]{1,0:T(8,128)S(1)}, f32[32,768]{1,0:T(8,128)S(1)}, u32[]{:S(2)}, u32[]{:S(2)}) %collective-permute-start.8) | collective-permute-done | bytes 98336 | tf_op jit(solution)/shard_map/ppermute | solution.py:379
  48.6 1.0 shard_map.172.refs_0_
  49.6 3.7 %collective-permute-done.9 = f32[32,768]{1,0:T(8,128)S(1)} collective-permute-done((f32[32,768]{1,0:T(8,128)S(1)}, f32[32,768]{1,0:T(8,128)S(1)}, u32[]{:S(2)}, u32[]{:S(2)}) %collective-permute-start.9) | collective-permute-done | bytes 98336 | tf_op jit(solution)/shard_map/ppermute | solution.py:381
  53.3 2.8 %collective-permute-start.10 = (f32[32,768]{1,0:T(8,128)S(1)}, f32[32,768]{1,0:T(8,128)S(1)}, u32[]{:S(2)}, u32[]{:S(2)}) collective-permute-start(f32[32,768]{1,0:T(8,128)S(1)} %add.41.refs_0_), channel_id=1, source_target_pairs={{16,0},{32,16},{48,32},{64,48},{80,64},{96,80},{112,96},{128,112},... | collective-permute-start | bytes 294920 | tf_op jit(solution)/shard_map/ppermute | solution.py:382
  56.2 1.3 %shard_map.173 = (f32[2,512,192]{2,1,0:T(8,128)S(1)}, f32[8,768]{1,0:T(8,128)S(1)}, bf16[2,256,512]{2,1,0:T(8,128)(2,1)S(1)}, bf16[512,512]{1,0:T(8,128)(2,1)S(1)}, f32[64,768]{1,0:T(8,128)S(1)}) custom-call(f32[1,2,64,768]{3,2,1,0:T(8,128)S(1)} %copy-done.1, f32[1032,256]{1,0:T(8,128)S(1)} %collective-permute-done.11.pack_ref, f32[512,256]{1,0:T(8,128)S(1)} %copy-done.10, ...), custom_call_target="tpu_custom_call" | custom-call | tf_op jit(solution)/shard_map/pallas_call | solution.py:69
  57.5 2.4 %collective-permute-done.10.mine_ref = f32[32,768]{1,0:T(8,128)S(1)} collective-permute-done((f32[32,768]{1,0:T(8,128)S(1)}, f32[32,768]{1,0:T(8,128)S(1)}, u32[]{:S(2)}, u32[]{:S(2)}) %collective-permute-start.10) | collective-permute-done | bytes 98336 | tf_op jit(solution)/shard_map/ppermute | solution.py:382
  59.9 6.2 %collective-permute-start.20 = (f32[1024,256]{1,0:T(8,128)S(1)}, f32[1024,256]{1,0:T(8,128)S(1)}, u32[]{:S(2)}, u32[]{:S(2)}) collective-permute-start(f32[1024,256]{1,0:T(8,128)S(1)} %shard_map.172.refs_0_), channel_id=1, source_target_pairs={{16,0},{32,16},{48,32},{64,48},{80,64},{96,80},{112,96},{128,112},... | collective-permute-start | bytes 3145736 | tf_op jit(solution)/shard_map/ppermute | solution.py:389
  67.1 1.4 %collective-permute-start.14 = (f32[72,384]{1,0:T(8,128)S(1)}, f32[72,384]{1,0:T(8,128)S(1)}, u32[]{:S(2)}, u32[]{:S(2)}) collective-permute-start(f32[72,384]{1,0:T(8,128)S(1)} %get-tuple-element.88), channel_id=1, source_target_pairs={{0,3},{1,2},{2,1},{3,0},{4,5},{5,4},{6,7},{7,6},{8,11},{9,10},{10,... | collective-permute-start | bytes 331784 | tf_op jit(solution)/shard_map/ppermute | solution.py:340
  68.5 4.2 %collective-permute-done.13 = f32[72,384]{1,0:T(8,128)S(1)} collective-permute-done((f32[72,384]{1,0:T(8,128)S(1)}, f32[72,384]{1,0:T(8,128)S(1)}, u32[]{:S(2)}, u32[]{:S(2)}) %collective-permute-start.13) | collective-permute-done | bytes 110624 | tf_op jit(solution)/shard_map/ppermute | solution.py:340
  73.5 1.4 %collective-permute-start.15 = (f32[72,384]{1,0:T(8,128)S(1)}, f32[72,384]{1,0:T(8,128)S(1)}, u32[]{:S(2)}, u32[]{:S(2)}) collective-permute-start(f32[72,384]{1,0:T(8,128)S(1)} %get-tuple-element.83), channel_id=1, source_target_pairs={{0,3},{1,2},{2,1},{3,0},{4,5},{5,4},{6,7},{7,6},{8,11},{9,10},{10,... | collective-permute-start | bytes 331784 | tf_op jit(solution)/shard_map/ppermute | solution.py:341
  75.0 4.6 %collective-permute-done.15 = f32[72,384]{1,0:T(8,128)S(1)} collective-permute-done((f32[72,384]{1,0:T(8,128)S(1)}, f32[72,384]{1,0:T(8,128)S(1)}, u32[]{:S(2)}, u32[]{:S(2)}) %collective-permute-start.15) | collective-permute-done | bytes 110624 | tf_op jit(solution)/shard_map/ppermute | solution.py:341
  79.7 1.3 %shard_map.175 = (f32[2,512,192]{2,1,0:T(8,128)S(1)}, f32[2,512,192]{2,1,0:T(8,128)S(1)}, f32[72,768]{1,0:T(8,128)S(1)}, f32[64,768]{1,0:T(8,128)S(1)}, f32[64,768]{1,0:T(8,128)S(1)}) custom-call(f32[72,768]{1,0:T(8,128)S(1)} %pad_maximum_fusion.2.d0_ref, f32[72,768]{1,0:T(8,128)S(1)} %pad_maximum_fusion.3.d1_ref, ...), custom_call_target="tpu_custom_call" | custom-call | tf_op jit(solution)/shard_map/pallas_call | solution.py:69
  81.3 1.8 %collective-permute-start.19 = (f32[64,768]{1,0:T(8,128)S(1)}, f32[64,768]{1,0:T(8,128)S(1)}, u32[]{:S(2)}, u32[]{:S(2)}) collective-permute-start(f32[64,768]{1,0:T(8,128)S(1)} %get-tuple-element.71), channel_id=1, source_target_pairs={{0,3},{1,2},{2,1},{3,0},{4,5},{5,4},{6,7},{7,6},{8,11},{9,10},{10,... | collective-permute-start | bytes 589832 | tf_op jit(solution)/shard_map/ppermute | solution.py:340
  83.2 4.6 %collective-permute-done.17 = f32[72,768]{1,0:T(8,128)S(1)} collective-permute-done((f32[72,768]{1,0:T(8,128)S(1)}, f32[72,768]{1,0:T(8,128)S(1)}, u32[]{:S(2)}, u32[]{:S(2)}) %collective-permute-start.17) | collective-permute-done | bytes 221216 | tf_op jit(solution)/shard_map/ppermute | solution.py:340
  87.8 2.0 %collective-permute-start.18 = (f32[72,768]{1,0:T(8,128)S(1)}, f32[72,768]{1,0:T(8,128)S(1)}, u32[]{:S(2)}, u32[]{:S(2)}) collective-permute-start(f32[72,768]{1,0:T(8,128)S(1)} %add.44.a0), channel_id=1, source_target_pairs={{0,3},{1,2},{2,1},{3,0},{4,5},{5,4},{6,7},{7,6},{8,11},{9,10},{10,... | collective-permute-start | bytes 663560 | tf_op jit(solution)/shard_map/ppermute | solution.py:341
  89.8 1.0 collective-permute-start.21
  90.8 6.3 %collective-permute-done.18.a1 = f32[72,768]{1,0:T(8,128)S(1)} collective-permute-done((f32[72,768]{1,0:T(8,128)S(1)}, f32[72,768]{1,0:T(8,128)S(1)}, u32[]{:S(2)}, u32[]{:S(2)}) %collective-permute-start.18) | collective-permute-done | bytes 221216 | tf_op jit(solution)/shard_map/ppermute | solution.py:341
  98.1 1.4 %collective-permute-done.22 = f32[64,768]{1,0:T(8,128)S(1)} collective-permute-done((f32[64,768]{1,0:T(8,128)S(1)}, f32[64,768]{1,0:T(8,128)S(1)}, u32[]{:S(2)}, u32[]{:S(2)}) %collective-permute-start.22) | collective-permute-done | bytes 196640 | tf_op jit(solution)/shard_map/ppermute | solution.py:393
  99.7 2.0 %shard_map.177 = (f32[512,256]{1,0:T(8,128)}, f32[512,256]{1,0:T(8,128)}) custom-call(f32[8,768]{1,0:T(8,128)S(1)} %get-tuple-element.76.row_ref, f32[2,512,192]{2,1,0:T(8,128)S(1)} %get-tuple-element.77.e_ref, f32[2,512,192]{2,1,0:T(8,128)S(1)} %get-tuple-element.78.dp_ref, f32[64,768]{1,0:T(8,128)S(1)} %get-tuple-element.79.dout_ref, ...), custom_call_target="tpu_custom_call" | custom-call | tf_op jit(solution)/shard_map/pallas_call | solution.py:69
  101.7 5.0 %collective-permute-done.23 = f32[64,768]{1,0:T(8,128)S(1)} collective-permute-done((f32[64,768]{1,0:T(8,128)S(1)}, f32[64,768]{1,0:T(8,128)S(1)}, u32[]{:S(2)}, u32[]{:S(2)}) %collective-permute-start.23) | collective-permute-done | bytes 196640 | tf_op jit(solution)/shard_map/ppermute | solution.py:395
  (73 shorter events, 7.7 us)
Async XLA Ops:
  1.9 19.1 %copy-start.3 = (f32[1,512,256]{2,1,0:T(8,128)S(1)}, f32[1,512,256]{2,1,0:T(8,128)}, u32[]{:S(2)}) copy-start(f32[1,512,256]{2,1,0:T(8,128)} %k_hbm.1) | copy-start | bytes 1572868
  1.9 19.1 %copy-start.4 = (f32[1,512,256]{2,1,0:T(8,128)S(1)}, f32[1,512,256]{2,1,0:T(8,128)}, u32[]{:S(2)}) copy-start(f32[1,512,256]{2,1,0:T(8,128)} %v_hbm.1) | copy-start | bytes 1572868
  8.9 13.4 %collective-permute-start = (f32[72,384]{1,0:T(8,128)S(1)}, f32[72,384]{1,0:T(8,128)S(1)}, u32[]{:S(2)}, u32[]{:S(2)}) collective-permute-start(f32[72,384]{1,0:T(8,128)S(1)} %get-tuple-element.89), channel_id=1, source_target_pairs={{0,1},{1,0},{2,3},{3,2},{4,7},{5,6},{6,5},{7,4},{8,9},{9,8},{10,11... | collective-permute-start | bytes 331784 | tf_op jit(solution)/shard_map/ppermute | solution.py:340
  10.5 11.8 %collective-permute-start.1 = (f32[72,384]{1,0:T(8,128)S(1)}, f32[72,384]{1,0:T(8,128)S(1)}, u32[]{:S(2)}, u32[]{:S(2)}) collective-permute-start(f32[72,384]{1,0:T(8,128)S(1)} %get-tuple-element.90), channel_id=1, source_target_pairs={{0,3},{1,2},{2,1},{3,0},{4,5},{5,4},{6,7},{7,6},{8,11},{9,10},{10,... | collective-permute-start | bytes 331784 | tf_op jit(solution)/shard_map/ppermute | solution.py:340
  12.6 43.5 %collective-permute-start.11 = (f32[1032,256]{1,0:T(8,128)}, f32[1032,256]{1,0:T(8,128)S(1)}, u32[]{:S(2)}, u32[]{:S(2)}) collective-permute-start(f32[1032,256]{1,0:T(8,128)} %get-tuple-element.60), channel_id=1, source_target_pairs={{16,0},{32,16},{48,32},{64,48},{80,64},{96,80},{112,96},{128,112},... | collective-permute-start | bytes 3170312 | tf_op jit(solution)/shard_map/ppermute | solution.py:374
  22.5 6.2 %collective-permute-start.2 = (f32[72,384]{1,0:T(8,128)S(1)}, f32[72,384]{1,0:T(8,128)S(1)}, u32[]{:S(2)}, u32[]{:S(2)}) collective-permute-start(f32[72,384]{1,0:T(8,128)S(1)} %get-tuple-element.85), channel_id=1, source_target_pairs={{0,3},{1,2},{2,1},{3,0},{4,5},{5,4},{6,7},{7,6},{8,11},{9,10},{10,... | collective-permute-start | bytes 331784 | tf_op jit(solution)/shard_map/ppermute | solution.py:341
  23.7 4.9 %collective-permute-start.3 = (f32[72,384]{1,0:T(8,128)S(1)}, f32[72,384]{1,0:T(8,128)S(1)}, u32[]{:S(2)}, u32[]{:S(2)}) collective-permute-start(f32[72,384]{1,0:T(8,128)S(1)} %get-tuple-element.86), channel_id=1, source_target_pairs={{0,1},{1,0},{2,3},{3,2},{4,7},{5,6},{6,5},{7,4},{8,9},{9,8},{10,11... | collective-permute-start | bytes 331784 | tf_op jit(solution)/shard_map/ppermute | solution.py:341
  28.7 11.7 %copy-start = (f32[1,768,768]{2,1,0:T(8,128)S(1)}, f32[1,768,768]{2,1,0:T(8,128)}, u32[]{:S(2)}) copy-start(f32[1,768,768]{2,1,0:T(8,128)} %w_hbm.1) | copy-start | bytes 7077892
  30.0 6.3 %collective-permute-start.4 = (f32[72,768]{1,0:T(8,128)S(1)}, f32[72,768]{1,0:T(8,128)S(1)}, u32[]{:S(2)}, u32[]{:S(2)}) collective-permute-start(f32[72,768]{1,0:T(8,128)S(1)} %get-tuple-element.49), channel_id=1, source_target_pairs={{0,1},{1,0},{2,3},{3,2},{4,7},{5,6},{6,5},{7,4},{8,9},{9,8},{10,11... | collective-permute-start | bytes 663560 | tf_op jit(solution)/shard_map/ppermute | solution.py:340
  30.1 10.1 %collective-permute-start.6 = (f32[64,768]{1,0:T(8,128)S(1)}, f32[64,768]{1,0:T(8,128)S(1)}, u32[]{:S(2)}, u32[]{:S(2)}) collective-permute-start(f32[64,768]{1,0:T(8,128)S(1)} %get-tuple-element.50), channel_id=1, source_target_pairs={{0,3},{1,2},{2,1},{3,0},{4,5},{5,4},{6,7},{7,6},{8,11},{9,10},{10,... | collective-permute-start | bytes 589832 | tf_op jit(solution)/shard_map/ppermute | solution.py:340
  36.4 9.7 %collective-permute-start.5 = (f32[72,768]{1,0:T(8,128)S(1)}, f32[72,768]{1,0:T(8,128)S(1)}, u32[]{:S(2)}, u32[]{:S(2)}) collective-permute-start(f32[72,768]{1,0:T(8,128)S(1)} %add.38.refs_0_.a0), channel_id=1, source_target_pairs={{0,3},{1,2},{2,1},{3,0},{4,5},{5,4},{6,7},{7,6},{8,11},{9,10},{10,... | collective-permute-start | bytes 663560 | tf_op jit(solution)/shard_map/ppermute | solution.py:341
  40.3 5.8 %collective-permute-start.7 = (f32[64,768]{1,0:T(8,128)S(1)}, f32[64,768]{1,0:T(8,128)S(1)}, u32[]{:S(2)}, u32[]{:S(2)}) collective-permute-start(f32[64,768]{1,0:T(8,128)S(1)} %add.39.b0), channel_id=1, source_target_pairs={{0,1},{1,0},{2,3},{3,2},{4,7},{5,6},{6,5},{7,4},{8,9},{9,8},{10,11... | collective-permute-start | bytes 589832 | tf_op jit(solution)/shard_map/ppermute | solution.py:341
  40.4 5.7 %copy-start.7 = (f32[1,64,768]{2,1,0:T(8,128)S(1)}, f32[1,64,768]{2,1,0:T(8,128)}, u32[]{:S(2)}) copy-start(f32[1,64,768]{2,1,0:T(8,128)} %g_hbm.1) | copy-start | bytes 589828
  47.0 1.4 %collective-permute-start.8 = (f32[32,768]{1,0:T(8,128)S(1)}, f32[32,768]{1,0:T(8,128)S(1)}, u32[]{:S(2)}, u32[]{:S(2)}) collective-permute-start(f32[32,768]{1,0:T(8,128)S(1)} %get-tuple-element.54), channel_id=1, source_target_pairs={{0,4},{4,0},{8,12},{12,8},{1,5},{5,1},{9,13},{13,9},{2,6},{6,2},{1... | collective-permute-start | bytes 294920 | tf_op jit(solution)/shard_map/ppermute | solution.py:379
  48.4 4.9 %collective-permute-start.9 = (f32[32,768]{1,0:T(8,128)S(1)}, f32[32,768]{1,0:T(8,128)S(1)}, u32[]{:S(2)}, u32[]{:S(2)}) collective-permute-start(f32[32,768]{1,0:T(8,128)S(1)} %add.40.refs_2_), channel_id=1, source_target_pairs={{0,8},{4,12},{8,0},{12,4},{1,9},{5,13},{9,1},{13,5},{2,10},{6,14},... | collective-permute-start | bytes 294920 | tf_op jit(solution)/shard_map/ppermute | solution.py:381
  48.5 7.6 %copy-start.10 = (f32[512,256]{1,0:T(8,128)S(1)}, f32[512,256]{1,0:T(8,128)}, u32[]{:S(2)}) copy-start(f32[512,256]{1,0:T(8,128)} %k_ref.1) | copy-start | bytes 1572868
  48.5 7.6 %copy-start.11 = (f32[512,256]{1,0:T(8,128)S(1)}, f32[512,256]{1,0:T(8,128)}, u32[]{:S(2)}) copy-start(f32[512,256]{1,0:T(8,128)} %v_ref.1) | copy-start | bytes 1572868
  48.5 7.6 %copy-start.12 = (f32[64,768]{1,0:T(8,128)S(1)}, f32[64,768]{1,0:T(8,128)}, u32[]{:S(2)}) copy-start(f32[64,768]{1,0:T(8,128)} %grad_ref.1) | copy-start | bytes 589828
  48.6 7.6 %copy-start.13 = (f32[8,256]{1,0:T(8,128)S(1)}, f32[8,256]{1,0:T(8,128)}, u32[]{:S(2)}) copy-start(f32[8,256]{1,0:T(8,128)} %get-tuple-element.61.bounds_ref) | copy-start | bytes 24580
  53.3 6.5 %collective-permute-start.10 = (f32[32,768]{1,0:T(8,128)S(1)}, f32[32,768]{1,0:T(8,128)S(1)}, u32[]{:S(2)}, u32[]{:S(2)}) collective-permute-start(f32[32,768]{1,0:T(8,128)S(1)} %add.41.refs_0_), channel_id=1, source_target_pairs={{16,0},{32,16},{48,32},{64,48},{80,64},{96,80},{112,96},{128,112},... | collective-permute-start | bytes 294920 | tf_op jit(solution)/shard_map/ppermute | solution.py:382
  59.9 6.2 %collective-permute-start.12 = (f32[32,768]{1,0:T(8,128)S(1)}, f32[32,768]{1,0:T(8,128)S(1)}, u32[]{:S(2)}, u32[]{:S(2)}) collective-permute-start(f32[32,768]{1,0:T(8,128)S(1)} %collective-permute-done.10.mine_ref), channel_id=1, source_target_pairs={{0,4},{4,0},{8,12},{12,8},{1,5},{5,1},{9,13},{13,9},{2,6},{6,2},{1... | collective-permute-start | bytes 294920 | tf_op jit(solution)/shard_map/ppermute | solution.py:385
  59.9 30.0 %collective-permute-start.20 = (f32[1024,256]{1,0:T(8,128)S(1)}, f32[1024,256]{1,0:T(8,128)S(1)}, u32[]{:S(2)}, u32[]{:S(2)}) collective-permute-start(f32[1024,256]{1,0:T(8,128)S(1)} %shard_map.172.refs_0_), channel_id=1, source_target_pairs={{16,0},{32,16},{48,32},{64,48},{80,64},{96,80},{112,96},{128,112},... | collective-permute-start | bytes 3145736 | tf_op jit(solution)/shard_map/ppermute | solution.py:389
  67.0 5.7 %collective-permute-start.13 = (f32[72,384]{1,0:T(8,128)S(1)}, f32[72,384]{1,0:T(8,128)S(1)}, u32[]{:S(2)}, u32[]{:S(2)}) collective-permute-start(f32[72,384]{1,0:T(8,128)S(1)} %get-tuple-element.87), channel_id=1, source_target_pairs={{0,1},{1,0},{2,3},{3,2},{4,7},{5,6},{6,5},{7,4},{8,9},{9,8},{10,11... | collective-permute-start | bytes 331784 | tf_op jit(solution)/shard_map/ppermute | solution.py:340
  67.1 6.4 %collective-permute-start.14 = (f32[72,384]{1,0:T(8,128)S(1)}, f32[72,384]{1,0:T(8,128)S(1)}, u32[]{:S(2)}, u32[]{:S(2)}) collective-permute-start(f32[72,384]{1,0:T(8,128)S(1)} %get-tuple-element.88), channel_id=1, source_target_pairs={{0,3},{1,2},{2,1},{3,0},{4,5},{5,4},{6,7},{7,6},{8,11},{9,10},{10,... | collective-permute-start | bytes 331784 | tf_op jit(solution)/shard_map/ppermute | solution.py:340
  73.5 6.0 %collective-permute-start.15 = (f32[72,384]{1,0:T(8,128)S(1)}, f32[72,384]{1,0:T(8,128)S(1)}, u32[]{:S(2)}, u32[]{:S(2)}) collective-permute-start(f32[72,384]{1,0:T(8,128)S(1)} %get-tuple-element.83), channel_id=1, source_target_pairs={{0,3},{1,2},{2,1},{3,0},{4,5},{5,4},{6,7},{7,6},{8,11},{9,10},{10,... | collective-permute-start | bytes 331784 | tf_op jit(solution)/shard_map/ppermute | solution.py:341
  75.0 4.7 %collective-permute-start.16 = (f32[72,384]{1,0:T(8,128)S(1)}, f32[72,384]{1,0:T(8,128)S(1)}, u32[]{:S(2)}, u32[]{:S(2)}) collective-permute-start(f32[72,384]{1,0:T(8,128)S(1)} %get-tuple-element.84), channel_id=1, source_target_pairs={{0,1},{1,0},{2,3},{3,2},{4,7},{5,6},{6,5},{7,4},{8,9},{9,8},{10,11... | collective-permute-start | bytes 331784 | tf_op jit(solution)/shard_map/ppermute | solution.py:341
  81.1 6.7 %collective-permute-start.17 = (f32[72,768]{1,0:T(8,128)S(1)}, f32[72,768]{1,0:T(8,128)S(1)}, u32[]{:S(2)}, u32[]{:S(2)}) collective-permute-start(f32[72,768]{1,0:T(8,128)S(1)} %get-tuple-element.70), channel_id=1, source_target_pairs={{0,1},{1,0},{2,3},{3,2},{4,7},{5,6},{6,5},{7,4},{8,9},{9,8},{10,11... | collective-permute-start | bytes 663560 | tf_op jit(solution)/shard_map/ppermute | solution.py:340
  81.3 8.5 %collective-permute-start.19 = (f32[64,768]{1,0:T(8,128)S(1)}, f32[64,768]{1,0:T(8,128)S(1)}, u32[]{:S(2)}, u32[]{:S(2)}) collective-permute-start(f32[64,768]{1,0:T(8,128)S(1)} %get-tuple-element.71), channel_id=1, source_target_pairs={{0,3},{1,2},{2,1},{3,0},{4,5},{5,4},{6,7},{7,6},{8,11},{9,10},{10,... | collective-permute-start | bytes 589832 | tf_op jit(solution)/shard_map/ppermute | solution.py:340
  87.8 9.3 %collective-permute-start.18 = (f32[72,768]{1,0:T(8,128)S(1)}, f32[72,768]{1,0:T(8,128)S(1)}, u32[]{:S(2)}, u32[]{:S(2)}) collective-permute-start(f32[72,768]{1,0:T(8,128)S(1)} %add.44.a0), channel_id=1, source_target_pairs={{0,3},{1,2},{2,1},{3,0},{4,5},{5,4},{6,7},{7,6},{8,11},{9,10},{10,... | collective-permute-start | bytes 663560 | tf_op jit(solution)/shard_map/ppermute | solution.py:341
  89.8 7.3 %collective-permute-start.21 = (f32[64,768]{1,0:T(8,128)S(1)}, f32[64,768]{1,0:T(8,128)S(1)}, u32[]{:S(2)}, u32[]{:S(2)}) collective-permute-start(f32[64,768]{1,0:T(8,128)S(1)} %add.45.b0), channel_id=1, source_target_pairs={{0,1},{1,0},{2,3},{3,2},{4,7},{5,6},{6,5},{7,4},{8,9},{9,8},{10,11... | collective-permute-start | bytes 589832 | tf_op jit(solution)/shard_map/ppermute | solution.py:341
  98.0 1.5 %collective-permute-start.22 = (f32[64,768]{1,0:T(8,128)S(1)}, f32[64,768]{1,0:T(8,128)S(1)}, u32[]{:S(2)}, u32[]{:S(2)}) collective-permute-start(f32[64,768]{1,0:T(8,128)S(1)} %get-tuple-element.75), channel_id=1, source_target_pairs={{0,4},{4,0},{8,12},{12,8},{1,5},{5,1},{9,13},{13,9},{2,6},{6,2},{1... | collective-permute-start | bytes 589832 | tf_op jit(solution)/shard_map/ppermute | solution.py:393
  99.6 7.0 %collective-permute-start.23 = (f32[64,768]{1,0:T(8,128)S(1)}, f32[64,768]{1,0:T(8,128)S(1)}, u32[]{:S(2)}, u32[]{:S(2)}) collective-permute-start(f32[64,768]{1,0:T(8,128)S(1)} %add.46.refs_1_), channel_id=1, source_target_pairs={{0,8},{4,12},{8,0},{12,4},{1,9},{5,13},{9,1},{13,5},{2,10},{6,14},... | collective-permute-start | bytes 589832 | tf_op jit(solution)/shard_map/ppermute | solution.py:395
  (6 other events, 14.9 us)
